TPU v7x, 32 devices: a whole 2x2x4 slice. The times are simulated.
32 devices in a mesh: dp: 4 (over x, core), tensor: 8 (over z, y).
Axes of the slice: x: 2, y: 2, z: 4, core: 2. Of those that a mesh axis runs over, the one named last changes fastest.
Arguments:
- inputs: bfloat16 [8192, 1024], P(('dp', 'tensor')), may hold values from -6 to 6
- segments: int32 [8, 1024], P('dp'), may hold values from 0 to 7, never falling along the last dimension, each value on 1 to 512 neighbouring positions
- query_weight: bfloat16 [2, 1024, 1024], P(None, None, 'tensor'), may hold values from -0.1875 to 0.1875
- query_bias: float32 [2, 1024], P(None, 'tensor'), may hold values from -1.2 to 1.2
- key_weight: bfloat16 [2, 1024, 1024], P(None, None, 'tensor'), may hold values from -0.1875 to 0.1875
- value_weight: bfloat16 [2, 1024, 1024], P(None, None, 'tensor'), may hold values from -0.1875 to 0.1875
- value_bias: float32 [2, 1024], P(None, 'tensor'), may hold values from -1.2 to 1.2
- out_weight: bfloat16 [2, 1024, 1024], P(None, 'tensor'), may hold values from -0.75 to 0.75
- out_bias: float32 [2, 1024], replicated, may hold values from -1.2 to 1.2
- first_gain: float32 [2, 1024], replicated, may hold values from 0.5 to 1.5
- first_shift: float32 [2, 1024], replicated, may hold values from -1.2 to 1.2
- inner_weight: bfloat16 [2, 1024, 4096], P(None, None, 'tensor'), may hold values from -0.1875 to 0.1875
- inner_bias: float32 [2, 4096], P(None, 'tensor'), may hold values from -1.2 to 1.2
- outer_weight: bfloat16 [2, 4096, 1024], P(None, 'tensor'), may hold values from -0.125 to 0.125
- outer_bias: float32 [2, 1024], replicated, may hold values from -1.2 to 1.2
- second_gain: float32 [2, 1024], replicated, may hold values from 0.5 to 1.5
- second_shift: float32 [2, 1024], replicated, may hold values from -1.2 to 1.2
- cotangent: bfloat16 [8192, 1024], P(('dp', 'tensor')), may hold values from -6 to 6
Outputs:
- result: float32 [8192, 1024], P(('dp', 'tensor'))
- input_grad: float32 [8192, 1024], P(('dp', 'tensor'))
- grad_query_weight: float32 [2, 1024, 1024], P(None, None, 'tensor')
- grad_query_bias: float32 [2, 1024], P(None, 'tensor')
- grad_key_weight: float32 [2, 1024, 1024], P(None, None, 'tensor')
- grad_value_weight: float32 [2, 1024, 1024], P(None, None, 'tensor')
- grad_value_bias: float32 [2, 1024], P(None, 'tensor')
- grad_out_weight: float32 [2, 1024, 1024], P(None, 'tensor')
- grad_out_bias: float32 [2, 1024], replicated
- grad_first_gain: float32 [2, 1024], replicated
- grad_first_shift: float32 [2, 1024], replicated
- grad_inner_weight: float32 [2, 1024, 4096], P(None, None, 'tensor')
- grad_inner_bias: float32 [2, 4096], P(None, 'tensor')
- grad_outer_weight: float32 [2, 4096, 1024], P(None, 'tensor')
- grad_outer_bias: float32 [2, 1024], replicated
- grad_second_gain: float32 [2, 1024], replicated
- grad_second_shift: float32 [2, 1024], replicated
Inputs may be any that keep to these rules, and one draw needn't show every extreme that they name: `segments`: within each sequence segment numbers never fall; a document holds 1 to 512 tokens, and some document holds exactly 512.
All inputs are finite; a program needn't handle non-finite values.
Results may differ from a plain program's by a relative error of at most 0.04.
Values may be sent and summed in bfloat16 or wider, within the bound.
No kernel may reach another device: no remote copies, remote signals or barrier semaphores. Data moves between devices by JAX's collectives and lax.ppermute only.
A program may use at most 192 MiB of HBM per device.

v0:
```python
from functools import partial

import jax
import jax.numpy as jnp
from jax import lax
from jax.sharding import PartitionSpec as P

HD = 64
WINDOW = 256


EPS = 1e-05
NEGATIVE = -1e30


def matmul(left, right):
    return jnp.dot(left, right, preferred_element_type=jnp.float32)


def layer_norm(values, norm_gain, norm_shift):
    center = values - jnp.mean(values, axis=-1, keepdims=True)
    spread = jnp.mean(center * center, axis=-1, keepdims=True)
    return center * lax.rsqrt(spread + EPS) * norm_gain + norm_shift


def key_mask(seg_row, windowed):
    allowed = seg_row[:, None] == seg_row[None, :]
    if windowed:
        places = jnp.arange(seg_row.shape[0], dtype=jnp.int32)
        in_window = jnp.abs(places[:, None] - places[None, :]) <= WINDOW // 2
        allowed = jnp.logical_and(allowed, in_window)
    return allowed


def masked_scores(query_rows, key_rows, seg_row, windowed):
    score_scale = query_rows.shape[-1] ** (-0.5)
    scores = (
        jnp.einsum("qhd,khd->hqk", query_rows, key_rows, preferred_element_type=jnp.float32)
        * score_scale
    )
    return jnp.where(key_mask(seg_row, windowed)[None], scores, NEGATIVE)


def shaped_heads(array, segments):
    seq_count, length = segments.shape
    return array.reshape(seq_count, length, array.shape[1] // HD, HD)


def attend_forward(query_all, key_all, value_all, segments, windowed):

    def one_sequence(blocks):
        query_rows, key_rows, value_rows, seg_row = blocks
        scores = masked_scores(query_rows, key_rows, seg_row, windowed)
        row_max = jnp.max(scores, axis=-1, keepdims=True)
        raised = jnp.exp(scores - row_max)
        row_total = jnp.sum(raised, axis=-1, keepdims=True)
        attn_probs = (raised / row_total).astype(jnp.bfloat16)
        context = jnp.einsum(
            "hqk,khd->qhd", attn_probs, value_rows, preferred_element_type=jnp.float32
        )
        return (context.astype(jnp.bfloat16), row_max[..., 0] + jnp.log(row_total[..., 0]))

    context, log_total = lax.map(
        one_sequence,
        (
            shaped_heads(query_all, segments),
            shaped_heads(key_all, segments),
            shaped_heads(value_all, segments),
            segments,
        ),
    )
    return (context.reshape(query_all.shape), log_total)


def attend_backward(query_all, key_all, value_all, segments, log_total, grad_context, windowed):

    def one_sequence(blocks):
        query_rows, key_rows, value_rows, seg_row, row_log, grad_rows = blocks
        score_scale = query_rows.shape[-1] ** (-0.5)
        scores = masked_scores(query_rows, key_rows, seg_row, windowed)
        attn_probs = jnp.exp(scores - row_log[..., None])
        grad_probs = jnp.einsum(
            "qhd,khd->hqk", grad_rows, value_rows, preferred_element_type=jnp.float32
        )
        row_delta = jnp.sum(attn_probs * grad_probs, axis=-1, keepdims=True)
        grad_scores = (attn_probs * (grad_probs - row_delta)).astype(jnp.bfloat16)
        grad_query = (
            jnp.einsum("hqk,khd->qhd", grad_scores, key_rows, preferred_element_type=jnp.float32)
            * score_scale
        )
        grad_key = (
            jnp.einsum("hqk,qhd->khd", grad_scores, query_rows, preferred_element_type=jnp.float32)
            * score_scale
        )
        grad_value = jnp.einsum(
            "hqk,qhd->khd",
            attn_probs.astype(jnp.bfloat16),
            grad_rows,
            preferred_element_type=jnp.float32,
        )
        return (
            grad_query.astype(jnp.bfloat16),
            grad_key.astype(jnp.bfloat16),
            grad_value.astype(jnp.bfloat16),
        )

    grad_query, grad_key, grad_value = lax.map(
        one_sequence,
        (
            shaped_heads(query_all, segments),
            shaped_heads(key_all, segments),
            shaped_heads(value_all, segments),
            segments,
            log_total,
            shaped_heads(grad_context, segments),
        ),
    )
    return (
        grad_query.reshape(query_all.shape),
        grad_key.reshape(key_all.shape),
        grad_value.reshape(value_all.shape),
    )


def row_product(left, right):
    return matmul(left, right)


def row_product_back(left, right):
    return jnp.einsum("tf,df->td", left, right, preferred_element_type=jnp.float32)


def input_back_rows(grad_parts, weight_parts):
    summed = None
    for grad_part, weight_part in zip(grad_parts, weight_parts):
        term = jnp.einsum("te,de->td", grad_part, weight_part, preferred_element_type=jnp.float32)
        summed = term if summed is None else summed + term
    return summed


def shards(
    inputs,
    segments,
    query_weight,
    query_bias,
    key_weight,
    value_weight,
    value_bias,
    out_weight,
    out_bias,
    first_gain,
    first_shift,
    inner_weight,
    inner_bias,
    outer_weight,
    outer_bias,
    second_gain,
    second_shift,
    cotangent,
):
    layer_count = query_weight.shape[0]
    saved_layers = []
    hidden_in = inputs.astype(jnp.float32)
    for layer_index in range(layer_count):
        windowed = layer_index % 2 == 1
        rows_low = lax.all_gather(hidden_in.astype(jnp.bfloat16), "tensor", axis=0, tiled=True)
        query_all = (matmul(rows_low, query_weight[layer_index]) + query_bias[layer_index]).astype(
            jnp.bfloat16
        )
        key_all = matmul(rows_low, key_weight[layer_index]).astype(jnp.bfloat16)
        value_all = (matmul(rows_low, value_weight[layer_index]) + value_bias[layer_index]).astype(
            jnp.bfloat16
        )
        context, log_total = attend_forward(query_all, key_all, value_all, segments, windowed)
        attn_out = lax.psum_scatter(
            row_product(context, out_weight[layer_index]).astype(jnp.bfloat16),
            "tensor",
            scatter_dimension=0,
            tiled=True,
        ).astype(jnp.float32)
        attended = hidden_in + attn_out + out_bias[layer_index]
        normed = layer_norm(attended, first_gain[layer_index], first_shift[layer_index])
        normed_low = lax.all_gather(normed.astype(jnp.bfloat16), "tensor", axis=0, tiled=True)
        inner = matmul(normed_low, inner_weight[layer_index]) + inner_bias[layer_index]
        activated = jax.nn.gelu(inner, approximate=False).astype(jnp.bfloat16)
        ffn_out = lax.psum_scatter(
            row_product(activated, outer_weight[layer_index]).astype(jnp.bfloat16),
            "tensor",
            scatter_dimension=0,
            tiled=True,
        ).astype(jnp.float32)
        mixed = normed + ffn_out + outer_bias[layer_index]
        saved_layers.append(
            (
                rows_low,
                query_all,
                key_all,
                value_all,
                context,
                log_total,
                attended,
                normed_low,
                inner,
                activated,
                mixed,
            )
        )
        hidden_in = layer_norm(mixed, second_gain[layer_index], second_shift[layer_index])
    grad_rows = cotangent.astype(jnp.float32)
    sharded_list = [None] * layer_count
    shared_list = [None] * layer_count
    for layer_index in reversed(range(layer_count)):
        windowed = layer_index % 2 == 1
        (
            rows_low,
            query_all,
            key_all,
            value_all,
            context,
            log_total,
            attended,
            normed_low,
            inner,
            activated,
            mixed,
        ) = saved_layers[layer_index]
        unused, second_back = jax.vjp(
            layer_norm, mixed, second_gain[layer_index], second_shift[layer_index]
        )
        grad_mixed, grad_second_gain, grad_second_shift = second_back(grad_rows)
        grad_outer_bias = jnp.sum(grad_mixed, axis=0)
        grad_branch = lax.all_gather(grad_mixed.astype(jnp.bfloat16), "tensor", axis=0, tiled=True)
        grad_outer = jnp.einsum(
            "tf,td->fd", activated, grad_branch, preferred_element_type=jnp.float32
        )
        grad_act = jnp.einsum(
            "td,fd->tf", grad_branch, outer_weight[layer_index], preferred_element_type=jnp.float32
        )
        unused, gelu_back = jax.vjp(partial(jax.nn.gelu, approximate=False), inner)
        grad_inner_low = gelu_back(grad_act)[0].astype(jnp.bfloat16)
        grad_inner_bias = jnp.sum(grad_inner_low, axis=0, dtype=jnp.float32)
        grad_inner = jnp.einsum(
            "td,tf->df", normed_low, grad_inner_low, preferred_element_type=jnp.float32
        )
        grad_normed = grad_mixed + lax.psum_scatter(
            row_product_back(grad_inner_low, inner_weight[layer_index]).astype(jnp.bfloat16),
            "tensor",
            scatter_dimension=0,
            tiled=True,
        ).astype(jnp.float32)
        unused, first_back = jax.vjp(
            layer_norm, attended, first_gain[layer_index], first_shift[layer_index]
        )
        grad_attended, grad_first_gain, grad_first_shift = first_back(grad_normed)
        grad_out_bias = jnp.sum(grad_attended, axis=0)
        grad_attn = lax.all_gather(grad_attended.astype(jnp.bfloat16), "tensor", axis=0, tiled=True)
        grad_out = jnp.einsum("te,td->ed", context, grad_attn, preferred_element_type=jnp.float32)
        grad_context = jnp.einsum(
            "td,ed->te", grad_attn, out_weight[layer_index], preferred_element_type=jnp.float32
        ).astype(jnp.bfloat16)
        grad_query_low, grad_key_low, grad_value_low = attend_backward(
            query_all, key_all, value_all, segments, log_total, grad_context, windowed
        )
        grad_query = jnp.einsum(
            "td,te->de", rows_low, grad_query_low, preferred_element_type=jnp.float32
        )
        grad_query_bias = jnp.sum(grad_query_low, axis=0, dtype=jnp.float32)
        grad_key = jnp.einsum(
            "td,te->de", rows_low, grad_key_low, preferred_element_type=jnp.float32
        )
        grad_value = jnp.einsum(
            "td,te->de", rows_low, grad_value_low, preferred_element_type=jnp.float32
        )
        grad_value_bias = jnp.sum(grad_value_low, axis=0, dtype=jnp.float32)
        input_part = lax.psum_scatter(
            input_back_rows(
                (grad_query_low, grad_key_low, grad_value_low),
                (query_weight[layer_index], key_weight[layer_index], value_weight[layer_index]),
            ).astype(jnp.bfloat16),
            "tensor",
            scatter_dimension=0,
            tiled=True,
        ).astype(jnp.float32)
        grad_rows = grad_attended + input_part
        sharded = (
            grad_query,
            grad_query_bias,
            grad_key,
            grad_value,
            grad_value_bias,
            grad_out,
            grad_inner,
            grad_inner_bias,
            grad_outer,
        )
        shared = (
            grad_out_bias,
            grad_first_gain,
            grad_first_shift,
            grad_outer_bias,
            grad_second_gain,
            grad_second_shift,
        )
        sharded_list[layer_index] = sharded
        shared_list[layer_index] = shared
    stacked_sharded = tuple(
        (
            jnp.stack([sharded_list[layer_index][slot_index] for layer_index in range(layer_count)])
            for slot_index in range(9)
        )
    )
    stacked_shared = tuple(
        (
            jnp.stack([shared_list[layer_index][slot_index] for layer_index in range(layer_count)])
            for slot_index in range(6)
        )
    )
    stacked_sharded = (
        lax.psum(stacked_sharded[0].astype(jnp.bfloat16), "dp").astype(jnp.float32),
        lax.psum(stacked_sharded[1].astype(jnp.bfloat16), "dp").astype(jnp.float32),
        lax.psum(stacked_sharded[2].astype(jnp.bfloat16), "dp").astype(jnp.float32),
        lax.psum(stacked_sharded[3].astype(jnp.bfloat16), "dp").astype(jnp.float32),
        lax.psum(stacked_sharded[4].astype(jnp.bfloat16), "dp").astype(jnp.float32),
        lax.psum(stacked_sharded[5].astype(jnp.bfloat16), "dp").astype(jnp.float32),
        lax.psum(stacked_sharded[6].astype(jnp.bfloat16), "dp").astype(jnp.float32),
        lax.psum(stacked_sharded[7].astype(jnp.bfloat16), "dp").astype(jnp.float32),
        lax.psum(stacked_sharded[8].astype(jnp.bfloat16), "dp").astype(jnp.float32),
    )
    stacked_shared = lax.psum(
        (
            stacked_shared[0],
            stacked_shared[1],
            stacked_shared[2],
            stacked_shared[3],
            stacked_shared[4],
            stacked_shared[5],
        ),
        ("dp", "tensor"),
    )
    return (
        hidden_in,
        grad_rows,
        stacked_sharded[0],
        stacked_sharded[1],
        stacked_sharded[2],
        stacked_sharded[3],
        stacked_sharded[4],
        stacked_sharded[5],
        stacked_shared[0],
        stacked_shared[1],
        stacked_shared[2],
        stacked_sharded[6],
        stacked_sharded[7],
        stacked_sharded[8],
        stacked_shared[3],
        stacked_shared[4],
        stacked_shared[5],
    )


def solution(mesh):
    in_specs = (
        P(("dp", "tensor"), None),
        P("dp", None),
        P(None, None, "tensor"),
        P(None, "tensor"),
        P(None, None, "tensor"),
        P(None, None, "tensor"),
        P(None, "tensor"),
        P(None, "tensor", None),
        P(),
        P(),
        P(),
        P(None, None, "tensor"),
        P(None, "tensor"),
        P(None, "tensor", None),
        P(),
        P(),
        P(),
        P(("dp", "tensor"), None),
    )
    out_specs = (
        P(("dp", "tensor"), None),
        P(("dp", "tensor"), None),
        P(None, None, "tensor"),
        P(None, "tensor"),
        P(None, None, "tensor"),
        P(None, None, "tensor"),
        P(None, "tensor"),
        P(None, "tensor", None),
        P(),
        P(),
        P(),
        P(None, None, "tensor"),
        P(None, "tensor"),
        P(None, "tensor", None),
        P(),
        P(),
        P(),
    )
    return jax.shard_map(shards, mesh=mesh, in_specs=in_specs, out_specs=out_specs, check_vma=False)
```

profile of v0, /device:TPU:0, one launch (start us, length us, event | category | flops | bytes accessed | tf_op | source)
XLA Modules:
  0.0 1688.2 jit_solution(14604146737322304409)
XLA Ops:
  9.5 76.8 %all-gather.9.cloned.1.call-done = bf16[2048,1024]{1,0:T(8,128)(2,1)} async-done(((bf16[256,1024]{1,0:T(8,128)(2,1)}), bf16[2048,1024]{1,0:T(8,128)(2,1)}) %all-gather.9.cloned.1.call-update) | async-done | bytes 4194320 | tf_op jit(solution)/shard_map/all_gather | solution.py:166
  100.4 14.9 while.52
  120.9 85.8 %reduce-scatter.9.cloned.1.call-done = bf16[256,1024]{1,0:T(8,128)(2,1)} async-done(((bf16[2048,1024]{1,0:T(8,128)(2,1)}), bf16[256,1024]{1,0:T(8,128)(2,1)}) %reduce-scatter.9.cloned.1.call-update) | async-done | bytes 524304 | tf_op jit(solution)/shard_map/reduce_scatter | solution.py:175
  211.6 73.2 %all-gather.11.cloned.1.call-done = bf16[2048,1024]{1,0:T(8,128)(2,1)} async-done(((bf16[256,1024]{1,0:T(8,128)(2,1)}), bf16[2048,1024]{1,0:T(8,128)(2,1)}) %all-gather.11.cloned.1.call-update) | async-done | bytes 4194320 | tf_op jit(solution)/shard_map/all_gather | solution.py:183
  284.9 14.6 multiply_convert_fusion.3
  300.8 4.4 convolution_convert_fusion.3
  306.0 85.6 %reduce-scatter.11.cloned.1.call-done = bf16[256,1024]{1,0:T(8,128)(2,1)} async-done(((bf16[2048,1024]{1,0:T(8,128)(2,1)}), bf16[256,1024]{1,0:T(8,128)(2,1)}) %reduce-scatter.11.cloned.1.call-update) | async-done | bytes 524304 | tf_op jit(solution)/shard_map/reduce_scatter | solution.py:186
  395.1 72.9 %all-gather.13.cloned.1.call-done = bf16[2048,1024]{1,0:T(8,128)(2,1)} async-done(((bf16[256,1024]{1,0:T(8,128)(2,1)}), bf16[2048,1024]{1,0:T(8,128)(2,1)}) %all-gather.13.cloned.1.call-update) | async-done | bytes 4194320 | tf_op jit(solution)/shard_map/all_gather | solution.py:166
  487.1 14.8 while.53
  502.9 4.3 convolution_convert_fusion.4
  507.5 86.1 %reduce-scatter.13.cloned.1.call-done = bf16[256,1024]{1,0:T(8,128)(2,1)} async-done(((bf16[2048,1024]{1,0:T(8,128)(2,1)}), bf16[256,1024]{1,0:T(8,128)(2,1)}) %reduce-scatter.13.cloned.1.call-update) | async-done | bytes 524304 | tf_op jit(solution)/shard_map/reduce_scatter | solution.py:175
  596.5 73.3 %all-gather.15.cloned.1.call-done = bf16[2048,1024]{1,0:T(8,128)(2,1)} async-done(((bf16[256,1024]{1,0:T(8,128)(2,1)}), bf16[2048,1024]{1,0:T(8,128)(2,1)}) %all-gather.15.cloned.1.call-update) | async-done | bytes 4194320 | tf_op jit(solution)/shard_map/all_gather | solution.py:183
  669.8 14.7 multiply_convert_fusion.2
  690.2 86.3 %reduce-scatter.15.cloned.1.call-done = bf16[256,1024]{1,0:T(8,128)(2,1)} async-done(((bf16[2048,1024]{1,0:T(8,128)(2,1)}), bf16[256,1024]{1,0:T(8,128)(2,1)}) %reduce-scatter.15.cloned.1.call-update) | async-done | bytes 524304 | tf_op jit(solution)/shard_map/reduce_scatter | solution.py:186
  783.0 73.1 %all-gather.17.cloned.1.call-done = bf16[2048,1024]{1,0:T(8,128)(2,1)} async-done(((bf16[256,1024]{1,0:T(8,128)(2,1)}), bf16[2048,1024]{1,0:T(8,128)(2,1)}) %all-gather.17.cloned.1.call-update) | async-done | bytes 4194320 | tf_op jit(solution)/shard_map/all_gather | solution.py:232
  856.0 9.7 fusion.240
  867.1 4.4 convolution_convert_fusion.1
  871.5 86.3 %reduce-scatter.17.cloned.1.call-done = bf16[256,1024]{1,0:T(8,128)(2,1)} async-done(((bf16[2048,1024]{1,0:T(8,128)(2,1)}), bf16[256,1024]{1,0:T(8,128)(2,1)}) %reduce-scatter.17.cloned.1.call-update) | async-done | bytes 524304 | tf_op jit(solution)/shard_map/reduce_scatter | solution.py:245
  963.9 73.0 %all-gather.19.cloned.1.call-done = bf16[2048,1024]{1,0:T(8,128)(2,1)} async-done(((bf16[256,1024]{1,0:T(8,128)(2,1)}), bf16[2048,1024]{1,0:T(8,128)(2,1)}) %all-gather.19.cloned.1.call-update) | async-done | bytes 4194320 | tf_op jit(solution)/shard_map/all_gather | solution.py:256
  1042.5 25.4 %while.54 = (s32[]{:T(128)}, bf16[2,1024,2,64]{1,3,2,0:T(8,128)(2,1)S(1)}, bf16[2,1024,2,64]{1,3,2,0:T(8,128)(2,1)}, bf16[2,1024,2,64]{1,3,2,0:T(8,128)(2,1)S(1)...) while((s32[]{:T(128)}, ...), condition=%wide.region_27.28_spmd, body=%wide.region_25.27_spmd.sunk | while | flops 1379530752 | bytes 73999536 | solution.py:107
  1077.6 86.3 %reduce-scatter.19.cloned.1.call-done = bf16[256,1024]{1,0:T(8,128)(2,1)} async-done(((bf16[2048,1024]{1,0:T(8,128)(2,1)}), bf16[256,1024]{1,0:T(8,128)(2,1)}) %reduce-scatter.19.cloned.1.call-update) | async-done | bytes 524304 | tf_op jit(solution)/shard_map/reduce_scatter | solution.py:275
  1168.8 73.1 %all-gather.21.cloned.1.call-done = bf16[2048,1024]{1,0:T(8,128)(2,1)} async-done(((bf16[256,1024]{1,0:T(8,128)(2,1)}), bf16[2048,1024]{1,0:T(8,128)(2,1)}) %all-gather.21.cloned.1.call-update) | async-done | bytes 4194320 | tf_op jit(solution)/shard_map/all_gather | solution.py:232
  1241.9 9.7 fusion.241
  1253.0 4.4 convolution_convert_fusion
  1257.5 86.3 %reduce-scatter.21.cloned.1.call-done = bf16[256,1024]{1,0:T(8,128)(2,1)} async-done(((bf16[2048,1024]{1,0:T(8,128)(2,1)}), bf16[256,1024]{1,0:T(8,128)(2,1)}) %reduce-scatter.21.cloned.1.call-update) | async-done | bytes 524304 | tf_op jit(solution)/shard_map/reduce_scatter | solution.py:245
  1350.6 5.3 fusion.139
  1373.2 50.4 %all-gather.23.cloned.1.call-done = bf16[2048,1024]{1,0:T(8,128)(2,1)} async-done(((bf16[256,1024]{1,0:T(8,128)(2,1)}), bf16[2048,1024]{1,0:T(8,128)(2,1)}) %all-gather.23.cloned.1.call-update) | async-done | bytes 4194320 | tf_op jit(solution)/shard_map/all_gather | solution.py:256
  1432.5 25.2 %while.55 = (s32[]{:T(128)}, bf16[2,1024,2,64]{1,3,2,0:T(8,128)(2,1)S(1)}, bf16[2,1024,2,64]{1,3,2,0:T(8,128)(2,1)}, bf16[2,1024,2,64]{1,3,2,0:T(8,128)(2,1)S(1)...) while((s32[]{:T(128)}, ...), condition=%wide.region_36.37_spmd, body=%wide.region_34.36_spmd.sunk | while | flops 1375336448 | bytes 73999536 | solution.py:107
  1474.6 41.4 %all-reduce = (f32[2,1024]{1,0:T(2,128)}, f32[2,1024]{1,0:T(2,128)}, f32[2,1024]{1,0:T(2,128)}, f32[2,1024]{1,0:T(2,128)}, f32[2,1024]{1,0:T(2,128)}, /*index=5*/f32[2,1024]{1,0:T(2,128)}) all-reduce(f32[2,1024]{1,0:T(2,128)S(1)} %get-tuple-element.468, ...), channel_id=1, replica_groups=mesh['dp'=4,'tensor'=8] {'dp','tensor'}, use_global_device_ids=true, to_apply=%region_50.51 | all-reduce | flops 12288 | bytes 98304 | tf_op jit(solution)/shard_map/psum | solution.py:329
  1516.4 7.5 all-reduce.1
  1525.6 61.7 %all-reduce.5.cloned.1.call-done = (bf16[2,1024,128]{1,2,0:T(8,128)(2,1)}, bf16[2,1024,128]{1,2,0:T(8,128)(2,1)}, bf16[2,1024,128]{1,2,0:T(8,128)(2,1)}, bf16[2,...) async-done(((bf16[2,1024,128]{1,2,0:T(8,128)(2,1)}, bf16[2,1024,128]{1,2,0:T(8,128)(2,1)}, bf16[2,1024,128]{1,2,0:T(8,128)(2,1)}, ...) | async-done | bytes 6291472 | tf_op jit(solution)/shard_map/psum | solution.py:319
  1600.3 79.0 %reduce-scatter.23.cloned.1.call-done = bf16[256,1024]{1,0:T(8,128)(2,1)} async-done(((bf16[2048,1024]{1,0:T(8,128)(2,1)}), bf16[256,1024]{1,0:T(8,128)(2,1)}) %reduce-scatter.23.cloned.1.call-update) | async-done | bytes 524304 | tf_op jit(solution)/shard_map/reduce_scatter | solution.py:275
  (485 shorter events, 241.9 us)
Async XLA Ops:
  7.2 79.1 %all-gather.9.cloned.1.call-start = ((), (), s32[]{:S(2)}) async-start(), calls=%async_computation.8 | async-start | bytes 4718592 | tf_op jit(solution)/shard_map/all_gather | solution.py:166
  7.9 198.8 %reduce-scatter.9.cloned.1.call-start = ((), (), s32[]{:S(2)}) async-start(), calls=%async_computation.9 | async-start | bytes 4718592 | tf_op jit(solution)/shard_map/reduce_scatter | solution.py:175
  120.2 91.5 %copy-start.99 = (f32[2,512]{1,0:T(2,128)S(1)}, f32[2,512]{1,0:T(2,128)}, u32[]{:S(2)}) copy-start(f32[2,512]{1,0:T(2,128)} %param.38) | copy-start | bytes 12292
  120.2 164.7 %all-gather.11.cloned.1.call-start = ((), (), s32[]{:S(2)}) async-start(), calls=%async_computation.10 | async-start | bytes 4718592 | tf_op jit(solution)/shard_map/all_gather | solution.py:183
  120.8 270.8 %copy-start.59 = (f32[1,1024]{1,0:T(1,128)}, f32[1,1024]{1,0:T(1,128)S(1)}, u32[]{:S(2)}) copy-start(f32[1,1024]{1,0:T(1,128)S(1)} %get-tuple-element.448) | copy-start | bytes 12292
  120.9 270.7 %copy-start.63 = (f32[1,1024]{1,0:T(1,128)}, f32[1,1024]{1,0:T(1,128)S(1)}, u32[]{:S(2)}) copy-start(f32[1,1024]{1,0:T(1,128)S(1)} %get-tuple-element.445) | copy-start | bytes 12292
  208.0 183.6 %copy-start.67 = (f32[256]{0:T(256)}, f32[256]{0:T(256)S(1)}, u32[]{:S(2)}) copy-start(f32[256]{0:T(256)S(1)} %broadcast_multiply_fusion.3) | copy-start | bytes 3076
  209.4 90.2 %copy-start.89 = (f32[256]{0:T(256)}, f32[256]{0:T(256)S(1)}, u32[]{:S(2)}) copy-start(f32[256]{0:T(256)S(1)} %multiply_reduce_fusion.11) | copy-start | bytes 3076
  209.4 182.2 %copy-start.71 = (f32[256]{0:T(256)}, f32[256]{0:T(256)S(1)}, u32[]{:S(2)}) copy-start(f32[256]{0:T(256)S(1)} %fusion.217) | copy-start | bytes 3076
  211.6 180.0 %reduce-scatter.11.cloned.1.call-start = ((), (), s32[]{:S(2)}) async-start(), calls=%async_computation.11 | async-start | bytes 4718592 | tf_op jit(solution)/shard_map/reduce_scatter | solution.py:186
  305.2 162.7 %copy-start.47 = (bf16[2,1024,128]{2,1,0:T(8,128)(2,1)S(1)}, bf16[2,1024,128]{2,1,0:T(8,128)(2,1)}, u32[]{:S(2)}) copy-start(bf16[2,1024,128]{2,1,0:T(8,128)(2,1)} %param.31) | copy-start | bytes 1572868
  305.3 162.7 %all-gather.13.cloned.1.call-start = ((), (), s32[]{:S(2)}) async-start(), calls=%async_computation.12 | async-start | bytes 4718592 | tf_op jit(solution)/shard_map/all_gather | solution.py:166
  306.0 287.6 %copy-start.65 = (f32[1,1024]{1,0:T(1,128)}, f32[1,1024]{1,0:T(1,128)S(1)}, u32[]{:S(2)}) copy-start(f32[1,1024]{1,0:T(1,128)S(1)} %get-tuple-element.441) | copy-start | bytes 12292
  393.2 200.4 %copy-start.2 = (f32[256,1024]{1,0:T(8,128)}, f32[256,1024]{1,0:T(8,128)S(1)}, u32[]{:S(2)}) copy-start(f32[256,1024]{1,0:T(8,128)S(1)} %get-tuple-element.426) | copy-start | bytes 3145732
  393.3 200.4 %copy-start.69 = (f32[256]{0:T(256)}, f32[256]{0:T(256)S(1)}, u32[]{:S(2)}) copy-start(f32[256]{0:T(256)S(1)} %broadcast_multiply_fusion.2) | copy-start | bytes 3076
  393.5 200.1 %copy-start.73 = (f32[256]{0:T(256)}, f32[256]{0:T(256)S(1)}, u32[]{:S(2)}) copy-start(f32[256]{0:T(256)S(1)} %fusion.218) | copy-start | bytes 3076
  394.6 199.0 %reduce-scatter.13.cloned.1.call-start = ((), (), s32[]{:S(2)}) async-start(), calls=%async_computation.13 | async-start | bytes 4718592 | tf_op jit(solution)/shard_map/reduce_scatter | solution.py:175
  507.3 162.5 %all-gather.15.cloned.1.call-start = ((), (), s32[]{:S(2)}) async-start(), calls=%async_computation.14 | async-start | bytes 4718592 | tf_op jit(solution)/shard_map/all_gather | solution.py:183
  596.5 180.0 %reduce-scatter.15.cloned.1.call-start = ((), (), s32[]{:S(2)}) async-start(), calls=%async_computation.15 | async-start | bytes 4718592 | tf_op jit(solution)/shard_map/reduce_scatter | solution.py:186
  690.2 88.1 %copy-start.42 = (bf16[256,1024]{1,0:T(8,128)(2,1)S(1)}, bf16[256,1024]{1,0:T(8,128)(2,1)}, u32[]{:S(2)}) copy-start(bf16[256,1024]{1,0:T(8,128)(2,1)} %param.43) | copy-start | bytes 1572868
  690.2 165.9 %all-gather.17.cloned.1.call-start = ((), (), s32[]{:S(2)}) async-start(), calls=%async_computation.16 | async-start | bytes 4718592 | tf_op jit(solution)/shard_map/all_gather | solution.py:232
  782.7 175.1 %reduce-scatter.17.cloned.1.call-start = ((), (), s32[]{:S(2)}) async-start(), calls=%async_computation.17 | async-start | bytes 4718592 | tf_op jit(solution)/shard_map/reduce_scatter | solution.py:245
  871.5 165.4 %all-gather.19.cloned.1.call-start = ((), (), s32[]{:S(2)}) async-start(), calls=%async_computation.18 | async-start | bytes 4718592 | tf_op jit(solution)/shard_map/all_gather | solution.py:256
  963.5 200.3 %reduce-scatter.19.cloned.1.call-start = ((), (), s32[]{:S(2)}) async-start(), calls=%async_computation.19 | async-start | bytes 4718592 | tf_op jit(solution)/shard_map/reduce_scatter | solution.py:275
  1077.5 88.6 %copy-start.92 = (f32[256]{0:T(256)S(1)}, f32[256]{0:T(256)}, u32[]{:S(2)}) copy-start(f32[256]{0:T(256)} %copy-done.91) | copy-start | bytes 3076
  1077.5 164.4 %copy-start.101 = (f32[1,512]{1,0:T(1,128)S(1)}, f32[1,512]{1,0:T(1,128)}, u32[]{:S(2)}) copy-start(f32[1,512]{1,0:T(1,128)} %copy-done.100) | copy-start | bytes 6148
  1077.5 164.4 %all-gather.21.cloned.1.call-start = ((), (), s32[]{:S(2)}) async-start(), calls=%async_computation.20 | async-start | bytes 4718592 | tf_op jit(solution)/shard_map/all_gather | solution.py:232
  1168.6 175.1 %reduce-scatter.21.cloned.1.call-start = ((), (), s32[]{:S(2)}) async-start(), calls=%async_computation.21 | async-start | bytes 4718592 | tf_op jit(solution)/shard_map/reduce_scatter | solution.py:245
  1257.4 88.7 %copy-start.90 = (f32[256]{0:T(256)S(1)}, f32[256]{0:T(256)}, u32[]{:S(2)}) copy-start(f32[256]{0:T(256)} %copy-done.89) | copy-start | bytes 3076
  1257.4 166.2 %all-gather.23.cloned.1.call-start = ((), (), s32[]{:S(2)}) async-start(), calls=%async_computation.22 | async-start | bytes 4718592 | tf_op jit(solution)/shard_map/all_gather | solution.py:256
  1350.4 236.9 %all-reduce.5.cloned.1.call-start = ((), (), s32[]{:S(2)}) async-start(), calls=%async_computation.24 | async-start | bytes 12582912 | tf_op jit(solution)/shard_map/psum | solution.py:319
  1466.8 212.5 %reduce-scatter.23.cloned.1.call-start = ((), (), s32[]{:S(2)}) async-start(), calls=%async_computation.23 | async-start | bytes 4718592 | tf_op jit(solution)/shard_map/reduce_scatter | solution.py:275
  (107 other events, 2077.1 us)
Sparse Core Ops, SparseCore 0:
  10.1 76.0 all-gather.8
  120.3 86.3 reduce-scatter.8
  211.7 73.1 all-gather.10
  305.4 86.1 reduce-scatter.10
  394.7 73.1 all-gather.12
  507.4 86.1 reduce-scatter.12
  596.6 73.1 all-gather.14
  690.3 86.1 reduce-scatter.14
  782.9 73.1 all-gather.16
  871.6 86.1 reduce-scatter.16
  963.7 73.1 all-gather.18
  1077.6 86.1 reduce-scatter.18
  1168.7 73.1 all-gather.20
  1257.6 86.1 reduce-scatter.20
  1350.5 73.1 all-gather.22
  1467.0 120.3 all-reduce.4
  1591.2 88.0 reduce-scatter.22
where the time goes:
time: 1700 us; the launch traced here: 1690 us
  waiting for transfers between devices  1310 us (77%)
  matrix products  190 us (11%)
  other arithmetic  72.3 us (4%)
  blocking collectives  48.9 us (3%)
  local copies, waits for them, and re-layouts  48.2 us (3%)
    reduce_scatter x2, waiting for transfers between devices, shards(): lax.psum_scatter(row_product_back(grad_inner_low, inner_weight[layer_inde...  173 us
    reduce_scatter x2, waiting for transfers between devices, shards(): lax.psum_scatter(row_product(context, out_weight[layer_index]).astype(jnp...  172 us
    reduce_scatter x2, waiting for transfers between devices, shards(): lax.psum_scatter(row_product(activated, outer_weight[layer_index]).astype...  172 us
    reduce_scatter x2, waiting for transfers between devices, shards(): lax.psum_scatter(input_back_rows((grad_query_low, grad_key_low, grad_valu...  165 us
    all_gather x2, waiting for transfers between devices, shards(): lax.all_gather(hidden_in.astype(jnp.bfloat16), 'tensor', axis=0, tiled=True)  150 us
    all_gather x2, waiting for transfers between devices, shards(): lax.all_gather(normed.astype(jnp.bfloat16), 'tensor', axis=0, tiled=True)  146 us
    all_gather x2, waiting for transfers between devices, shards(): lax.all_gather(grad_mixed.astype(jnp.bfloat16), 'tensor', axis=0, tiled=T...  146 us
    all_gather x2, waiting for transfers between devices, shards(): lax.all_gather(grad_attended.astype(jnp.bfloat16), 'tensor', axis=0, tile...  123 us
  transfers between devices with their start and end apart: 17, of which 17 were waited for; matrix products, arithmetic and copies ran while one was open for 3% of the time, Pallas kernels for 0%

commit v1 on v0

v1 whole, which is shorter than its diff:
```python
from functools import partial

import jax
import jax.numpy as jnp
from jax import lax
from jax.experimental import pallas as pl
from jax.experimental.pallas import tpu as pltpu
from jax.sharding import PartitionSpec as P

HD = 64
WINDOW = 256
EPS = 1e-05
NEGATIVE = -1e30
BF = jnp.bfloat16
F32 = jnp.float32
LANES = 128


def dot_nn(left, right):
    return lax.dot_general(left, right, (((1,), (0,)), ((), ())), preferred_element_type=F32)


def dot_nt(left, right):
    return lax.dot_general(left, right, (((1,), (1,)), ((), ())), preferred_element_type=F32)


def dot_tn(left, right):
    return lax.dot_general(left, right, (((0,), (0,)), ((), ())), preferred_element_type=F32)


def allowed_keys(seg_q, seg_k, halo):
    allowed = seg_q == seg_k
    if halo:
        row = lax.broadcasted_iota(jnp.int32, allowed.shape, 0)
        col = lax.broadcasted_iota(jnp.int32, allowed.shape, 1)
        allowed = jnp.logical_and(allowed, jnp.abs(row + halo - col) <= WINDOW // 2)
    return allowed


def head_lanes(shape, head):
    lane = lax.broadcasted_iota(jnp.int32, shape, 1)
    return (lane // HD) == head


def probabilities(query, key, allowed):
    scores = jnp.where(allowed, dot_nt(query, key) * (HD ** -0.5), NEGATIVE)
    raised = jnp.exp(scores - jnp.max(scores, axis=-1, keepdims=True))
    return raised * (1.0 / jnp.sum(raised, axis=-1, keepdims=True))


def attend_kernel(halo, seg_q_ref, seg_k_ref, q_ref, k_ref, v_ref, c_ref):
    allowed = allowed_keys(seg_q_ref[...], seg_k_ref[...], halo)
    query, key, value = q_ref[...], k_ref[...], v_ref[...]
    total = None
    for head in range(LANES // HD):
        mine = head_lanes(query.shape, head)
        probs = probabilities(jnp.where(mine, query, jnp.zeros_like(query)), key, allowed)
        part = jnp.where(mine, dot_nn(probs.astype(BF), value), 0.0)
        total = part if total is None else total + part
    c_ref[...] = total.astype(BF)


def attend_back_kernel(halo, seg_q_ref, seg_k_ref, q_ref, k_ref, v_ref, g_ref, dq_ref, dk_ref, dv_ref):
    allowed = allowed_keys(seg_q_ref[...], seg_k_ref[...], halo)
    query, key, value, grad = q_ref[...], k_ref[...], v_ref[...], g_ref[...]
    dq = dk = dv = None
    for head in range(LANES // HD):
        mine = head_lanes(query.shape, head)
        own_q = jnp.where(mine, query, jnp.zeros_like(query))
        own_g = jnp.where(mine, grad, jnp.zeros_like(grad))
        probs = probabilities(own_q, key, allowed)
        grad_probs = dot_nt(own_g, value)
        delta = jnp.sum(probs * grad_probs, axis=-1, keepdims=True)
        grad_scores = (probs * (grad_probs - delta)).astype(BF)
        q_part = jnp.where(mine, dot_nn(grad_scores, key), 0.0)
        k_part = dot_tn(grad_scores, own_q)
        v_part = dot_tn(probs.astype(BF), own_g)
        dq = q_part if dq is None else dq + q_part
        dk = k_part if dk is None else dk + k_part
        dv = v_part if dv is None else dv + v_part
    dq_ref[...] = (dq * (HD ** -0.5)).astype(BF)
    dk_ref[...] = (dk * (HD ** -0.5)).astype(BF)
    dv_ref[...] = dv.astype(BF)


def attend(query, key, value, seg_q, seg_k, halo):
    rows, width = query.shape
    keys = key.shape[0]
    whole = lambda shape: pl.BlockSpec(shape, lambda p: (0, 0))
    near = pl.BlockSpec((rows, LANES), lambda p: (0, p))
    far = pl.BlockSpec((keys, LANES), lambda p: (0, p))
    return pl.pallas_call(
        partial(attend_kernel, halo),
        grid=(width // LANES,),
        in_specs=[whole((rows, 1)), whole((1, keys)), near, far, far],
        out_specs=near,
        out_shape=jax.ShapeDtypeStruct((rows, width), BF),
        compiler_params=pltpu.CompilerParams(vmem_limit_bytes=40 * 1024 * 1024),
        cost_estimate=pl.CostEstimate(flops=HINT, bytes_accessed=HINT, transcendentals=0),
        name="attend",
    )(seg_q, seg_k, query, key, value)


def attend_back(query, key, value, grad, seg_q, seg_k, halo):
    rows, width = query.shape
    keys = key.shape[0]
    whole = lambda shape: pl.BlockSpec(shape, lambda p: (0, 0))
    near = pl.BlockSpec((rows, LANES), lambda p: (0, p))
    far = pl.BlockSpec((keys, LANES), lambda p: (0, p))
    return pl.pallas_call(
        partial(attend_back_kernel, halo),
        grid=(width // LANES,),
        in_specs=[whole((rows, 1)), whole((1, keys)), near, far, far, near],
        out_specs=[near, far, far],
        out_shape=[
            jax.ShapeDtypeStruct((rows, width), BF),
            jax.ShapeDtypeStruct((keys, width), BF),
            jax.ShapeDtypeStruct((keys, width), BF),
        ],
        compiler_params=pltpu.CompilerParams(vmem_limit_bytes=48 * 1024 * 1024),
        cost_estimate=pl.CostEstimate(flops=HINT, bytes_accessed=HINT, transcendentals=0),
        name="attend_back",
    )(seg_q, seg_k, query, key, value, grad)


def norm_stats(values):
    center = values - jnp.mean(values, axis=-1, keepdims=True)
    inverse = lax.rsqrt(jnp.mean(center * center, axis=-1, keepdims=True) + EPS)
    return center * inverse, inverse


def norm_back(grad, normal, inverse, gain):
    scaled = grad * gain
    back = inverse * (
        scaled
        - jnp.mean(scaled, axis=-1, keepdims=True)
        - normal * jnp.mean(scaled * normal, axis=-1, keepdims=True)
    )
    return back, jnp.sum(grad * normal, axis=0), jnp.sum(grad, axis=0)


def gelu_and_slope(inner):
    half = 0.5 * (1.0 + lax.erf(inner * (0.5 ** 0.5)))
    bell = jnp.exp(-0.5 * inner * inner) * ((2.0 * jnp.pi) ** -0.5)
    return (inner * half).astype(BF), (half + inner * bell).astype(BF)


def streamed(kernel_step, near, first, second, extra, outs, name):
    count, (rows_of, width) = len(first), first[0].shape
    tile = min(512, rows_of)
    steps = [(k, t * tile) for k in range(count) for t in range(rows_of // tile)]
    near_count, extra_count = len(near), len(extra)

    def kernel(*refs):
        near_refs, refs = refs[:near_count], refs[near_count:]
        extra_refs, refs = refs[:extra_count], refs[extra_count:]
        one_refs, two_refs, refs = refs[:count], refs[count : 2 * count], refs[2 * count :]
        *out_refs, one_held, two_held, sems = refs

        def copies(s):
            k, at = steps[s]
            slot = s % 2
            return [
                pltpu.make_async_copy(one_refs[k].at[pl.ds(at, tile)], one_held.at[slot], sems.at[0, slot]),
                pltpu.make_async_copy(two_refs[k].at[pl.ds(at, tile)], two_held.at[slot], sems.at[1, slot]),
            ]

        for copy in copies(0):
            copy.start()
        for s, (k, at) in enumerate(steps):
            if s + 1 < len(steps):
                for copy in copies(s + 1):
                    copy.start()
            for copy in copies(s):
                copy.wait()
            kernel_step(s, k, at, tile, near_refs, extra_refs, one_held.at[s % 2], two_held.at[s % 2], out_refs)

    whole = pl.BlockSpec(memory_space=pltpu.VMEM)
    anywhere = pl.BlockSpec(memory_space=pl.ANY)
    dtype = first[0].dtype
    return pl.pallas_call(
        kernel,
        in_specs=[whole] * (near_count + extra_count) + [anywhere] * (2 * count),
        out_specs=[whole] * len(outs),
        out_shape=outs,
        scratch_shapes=[
            pltpu.VMEM((2, tile, width), dtype),
            pltpu.VMEM((2, tile, width), dtype),
            pltpu.SemaphoreType.DMA((2, 2)),
        ],
        compiler_params=pltpu.CompilerParams(vmem_limit_bytes=40 * 1024 * 1024),
        cost_estimate=pl.CostEstimate(flops=HINT, bytes_accessed=HINT, transcendentals=0),
        name=name,
    )(*near, *extra, *first, *second)


def feed_forward(rows_low, inner, outer, bias):
    count, (each, width), rows = len(inner), inner[0].shape, rows_low.shape[0]

    def step(s, k, at, tile, near, extra, inner_tile, outer_tile, outs):
        act, slope = gelu_and_slope(
            dot_nt(near[0][...], inner_tile[...]) + extra[0][pl.ds(k, 1), pl.ds(at, tile)]
        )
        outs[1 + k][:, pl.ds(at, tile)] = act
        outs[1 + count + k][:, pl.ds(at, tile)] = slope
        part = dot_nn(act, outer_tile[...])
        outs[0][...] = part if s == 0 else outs[0][...] + part

    shapes = [jax.ShapeDtypeStruct((rows, width), F32)] + [jax.ShapeDtypeStruct((rows, each), BF)] * (2 * count)
    total, *rest = streamed(step, [rows_low], inner, outer, [bias], shapes, "feed_forward")
    return total, rest[:count], rest[count:]


def feed_forward_back(grad_low, inner, outer, slopes):
    count, (each, width), rows = len(inner), inner[0].shape, grad_low.shape[0]

    def step(s, k, at, tile, near, extra, outer_tile, inner_tile, outs):
        grad = (dot_nt(near[0][...], outer_tile[...]) * extra[k][:, pl.ds(at, tile)].astype(F32)).astype(BF)
        outs[2 + k][:, pl.ds(at, tile)] = grad
        outs[1][pl.ds(k, 1), pl.ds(at, tile)] = jnp.sum(grad.astype(F32), axis=0, keepdims=True)
        part = dot_nn(grad, inner_tile[...])
        outs[0][...] = part if s == 0 else outs[0][...] + part

    shapes = [jax.ShapeDtypeStruct((rows, width), F32), jax.ShapeDtypeStruct((count, each), F32)]
    shapes += [jax.ShapeDtypeStruct((rows, each), BF)] * count
    total, sums, *grads = streamed(step, [grad_low], outer, inner, list(slopes), shapes, "feed_forward_back")
    return total, sums, grads


def weight_grad(pairs, add=None):
    columns, width = pairs[0][0].shape[1], pairs[0][1].shape[1]
    tile = min(256, columns)

    def kernel(*refs):
        total = None
        for k in range(len(pairs)):
            part = dot_tn(refs[2 * k][...], refs[2 * k + 1][...])
            total = part if total is None else total + part
        if add is not None:
            total = total + refs[2 * len(pairs)][...].astype(F32)
        refs[-1][...] = total.astype(BF)

    block = pl.BlockSpec((tile, width), lambda t: (t, 0))
    specs, operands = [], []
    for left, right in pairs:
        specs += [
            pl.BlockSpec((left.shape[0], tile), lambda t: (0, t)),
            pl.BlockSpec(right.shape, lambda t: (0, 0)),
        ]
        operands += [left, right]
    if add is not None:
        specs.append(block)
        operands.append(add)
    return pl.pallas_call(
        kernel,
        grid=(columns // tile,),
        in_specs=specs,
        out_specs=block,
        out_shape=jax.ShapeDtypeStruct((columns, width), BF),
        compiler_params=pltpu.CompilerParams(vmem_limit_bytes=32 * 1024 * 1024),
        cost_estimate=pl.CostEstimate(flops=HINT, bytes_accessed=HINT, transcendentals=0),
        name="weight_grad",
    )(*operands)


def gradients_out(turned, plain):
    layers, width = len(turned[0]), turned[0][0].shape[1]
    steps = 4

    def kernel(*refs):
        outs = refs[layers * (len(turned) + len(plain)) :]
        for k, out in enumerate(outs):
            for l in range(layers):
                value = refs[k * layers + l][...].astype(F32)
                out[l] = value.T if k < len(turned) else value

    specs, shapes, out_specs = [], [], []
    for arrays in turned:
        rows = arrays[0].shape[0]
        specs += [pl.BlockSpec((rows, width // steps), lambda t: (0, t))] * layers
        out_specs.append(pl.BlockSpec((layers, width // steps, rows), lambda t: (0, t, 0)))
        shapes.append(jax.ShapeDtypeStruct((layers, width, rows), F32))
    for arrays in plain:
        rows = arrays[0].shape[0]
        specs += [pl.BlockSpec((rows // steps, width), lambda t: (t, 0))] * layers
        out_specs.append(pl.BlockSpec((layers, rows // steps, width), lambda t: (0, t, 0)))
        shapes.append(jax.ShapeDtypeStruct((layers, rows, width), F32))
    return pl.pallas_call(
        kernel,
        grid=(steps,),
        in_specs=specs,
        out_specs=out_specs,
        out_shape=shapes,
        compiler_params=pltpu.CompilerParams(vmem_limit_bytes=40 * 1024 * 1024),
        cost_estimate=pl.CostEstimate(flops=HINT, bytes_accessed=HINT, transcendentals=0),
        name="gradients_out",
    )(*[a for arrays in turned + plain for a in arrays])


class Grid:
    def __init__(self, mesh):
        self.nd, self.nt = mesh.shape["dp"], mesh.shape["tensor"]
        self.nx = self.nd // 2

    def place(self):
        self.dp, self.tensor = lax.axis_index("dp"), lax.axis_index("tensor")
        self.x, self.c = self.dp // 2, self.dp % 2

    def swap(self, array, axis, bit):
        count = self.nd if axis == "dp" else self.nt
        return lax.ppermute(array, axis, [(i, i ^ bit) for i in range(count)])

    def core(self, array):
        return self.swap(array, "dp", 1)

    def bits(self, name):
        low, high = {"x": (2, self.nd), "t": (1, self.nt)}[name]
        found = []
        while low < high:
            found.append(low)
            low *= 2
        return found

    def shift(self, array, by, group):
        pairs = [(i, i + by) for i in range(self.nt) if 0 <= i + by < self.nt and i // group == (i + by) // group]
        return lax.ppermute(array, "tensor", pairs)

    def turned(self, array, name, axis):
        count, at = {"x": (self.nx, self.x), "c": (2, self.c), "t": (self.nt, self.tensor)}[name]
        if count == 2:
            return jnp.where(at == 0, array, lax.rev(array, (axis,)))
        return jnp.take(array, at ^ jnp.arange(count), axis=axis)

    def sum_all(self, array):
        for axis, count in (("dp", self.nd), ("tensor", self.nt)):
            bit = 1
            while bit < count:
                array = array + self.swap(array, axis, bit)
                bit *= 2
        return array


def together(*values):
    return lax.optimization_barrier(values)


def shards(
    grid,
    inputs,
    segments,
    query_weight,
    query_bias,
    key_weight,
    value_weight,
    value_bias,
    out_weight,
    out_bias,
    first_gain,
    first_shift,
    inner_weight,
    inner_bias,
    outer_weight,
    outer_bias,
    second_gain,
    second_shift,
    cotangent,
):
    g = grid
    g.place()
    layers = query_weight.shape[0]
    rows, width = inputs.shape
    heads = query_weight.shape[2]
    cores = 2 if heads // 2 % HD == 0 else 1
    part = heads // cores
    units = inner_weight.shape[2]
    block = units // g.nd
    length = segments.shape[1]
    group = length // rows
    halo = WINDOW // 2
    high_to_low = g.bits("t")[::-1]

    own = segments[g.tensor // group] if segments.shape[0] > 1 else segments[0]
    spot = g.tensor % group
    seg_q = lax.dynamic_slice(own, (spot * rows,), (rows,))[:, None]
    padded = jnp.pad(own, (halo, halo), constant_values=-1)
    seg_near = lax.dynamic_slice(padded, (spot * rows,), (rows + 2 * halo,))[None]
    seg_far = jnp.take(own.reshape(group, rows), spot ^ jnp.arange(group), axis=0).reshape(1, length)

    def far_rows(array, other=None):
        bit = 1
        while bit < group:
            if other is None:
                other = g.swap(array, "tensor", bit)
            array, other = jnp.concatenate([array, other]), None
            bit *= 2
        return array

    def far_sums(array):
        bit = group // 2
        while bit:
            keep, give = jnp.split(array, 2)
            array = keep.astype(F32) + g.swap(give.astype(BF), "tensor", bit).astype(F32)
            bit //= 2
        return array

    def near_rows(array):
        return jnp.concatenate(
            [g.shift(array[rows - halo :], 1, group), array, g.shift(array[:halo], -1, group)]
        )

    def near_sums(array):
        after_rows = g.shift(array[:halo], -1, group).astype(F32)
        before_rows = g.shift(array[rows + halo :], 1, group).astype(F32)
        edge = jnp.zeros((rows - halo, width), F32)
        return (
            array[halo : rows + halo].astype(F32)
            + jnp.concatenate([edge, after_rows])
            + jnp.concatenate([before_rows, edge])
        )

    step_order = [0]
    for bit in high_to_low:
        step_order = step_order + [m | bit for m in step_order]
    blocks = 2 * g.nx

    def by_steps(array):
        for bit in high_to_low:
            array = jnp.concatenate([array, g.swap(array, "tensor", bit)])
        return array

    def back_by_steps(total):
        for bit in high_to_low[::-1]:
            keep, give = jnp.split(total, 2)
            total = (keep.astype(F32) + g.swap(give, "tensor", bit).astype(F32)).astype(BF)
        return total

    def from_steps(array, axis):
        place = jnp.array([step_order.index(m) for m in range(g.nt)])
        return jnp.take(array, place[g.tensor ^ jnp.arange(g.nt)], axis=axis)

    def unit_piece(shard):
        return lax.dynamic_index_in_dim(shard.reshape(g.nd, block, width), g.dp, 0, keepdims=False)

    def over_x(array):
        pieces = [array]
        for bit in g.bits("x"):
            pieces = pieces + [g.swap(a, "dp", bit) for a in pieces]
        return pieces

    def over_core(pieces):
        return pieces + [g.core(a) for a in pieces]

    def head_piece(l):
        pack = jnp.stack([query_weight[l].T, key_weight[l].T, value_weight[l].T, out_weight[l]])
        if cores == 2:
            pack = lax.dynamic_index_in_dim(pack.reshape(4, 2, part, width), g.c, 1, keepdims=False)
        return pack.reshape(1, 4 * part, width)

    def head_first(pack):
        for bit in high_to_low[:-1]:
            pack = jnp.concatenate([pack, g.swap(pack, "tensor", bit)])
        return pack

    def head_last(pack):
        both = [pack, g.swap(pack, "tensor", high_to_low[-1])]
        return [
            jnp.concatenate([a[:, k * part : (k + 1) * part].reshape(-1, width) for a in both]) for k in range(4)
        ]

    def head_rows(kinds):
        return [[a] if cores == 1 else [a, g.core(a)] for a in kinds]

    def bias_rows():
        pack = by_steps(jnp.concatenate([inner_bias, query_bias, value_bias], axis=1)[None])
        unit = pack[..., :units].reshape(g.nt, layers, g.nx, 2, block)
        unit = g.turned(g.turned(unit, "x", 2), "c", 3)
        head = pack[..., units:].reshape(g.nt, layers, 2, cores, part)
        if cores == 2:
            head = g.turned(head, "c", 3)
        unit = jnp.concatenate([unit[:, :1], from_steps(unit[:, 1:], 0)], 1)
        head = jnp.concatenate([head[:, :1], from_steps(head[:, 1:], 0)], 1)
        unit = jnp.transpose(unit, (1, 3, 2, 0, 4)).reshape(layers, blocks, -1)
        return unit, jnp.transpose(head, (1, 2, 3, 0, 4)).reshape(layers, 2, cores, -1)

    moves = [(l, kind) for l in range(layers) for kind in "iu"]
    shard_of = {(l, kind): {"i": inner_weight[l].T, "u": outer_weight[l]}[kind] for l, kind in moves}
    piece_of, gathered, spread, unit_w, head_w = {}, {}, {}, {}, {}
    piece_of[moves[0]] = unit_piece(shard_of[moves[0]])
    stage = 0

    def next_round():
        nonlocal stage
        new = {"piece_of": {}, "gathered": {}, "spread": {}, "unit_w": {}}
        for back, name in enumerate(new):
            if 0 <= stage + 1 - back < len(moves):
                key = moves[stage + 1 - back]
                if back > 1 or key[0] == 0:
                    new[name][key] = (
                        unit_piece(shard_of[key]) if back == 0
                        else by_steps(piece_of[key]) if back == 1
                        else over_x(gathered[key]) if back == 2
                        else over_core(spread[key])
                    )
        stage += 1
        return new

    def end_round(new, carry):
        new, carry = together(new, carry)
        for name, kept in (("piece_of", piece_of), ("gathered", gathered), ("spread", spread), ("unit_w", unit_w)):
            kept.update(new[name])
        return carry

    saved = []
    hidden = inputs.astype(F32)
    for l in range(1, layers):
        pieces = jnp.stack([unit_piece(shard_of[l, "i"]), unit_piece(shard_of[l, "u"])])
        both = lax.all_gather(pieces, "tensor", axis=0)
        for k, kind in enumerate("iu"):
            gathered[l, kind] = both[:, k].reshape(-1, width)
    new = next_round()
    unit_bias, head_bias = bias_rows()
    far = g.swap(inputs, "tensor", 1) if group > 1 else inputs
    first_part = head_first(head_piece(0))
    unit_bias, head_bias, far, first_part = end_round(new, (unit_bias, head_bias, far, first_part))
    new = next_round()
    far_inputs = far_rows(inputs, far)
    kinds = head_last(first_part)
    later = [head_piece(l).reshape(4, part, width) for l in range(1, layers)]
    hidden, far_inputs, kinds, later = end_round(new, (hidden, far_inputs, kinds, later))
    for l in range(layers):
        windowed = l % 2 == 1
        low = hidden.astype(BF)
        new = next_round()
        head_w[l] = head_rows(kinds)
        if l + 1 < layers:
            next_heads = lax.all_gather(later[l], "tensor", axis=1).reshape(4, g.nt * part, width)
        if windowed:
            far, seg_k, reach = near_rows(low), seg_near, halo
        else:
            far = far_inputs if l == 0 else far_rows(low)
            seg_k, reach = seg_far, 0
        q_w, k_w, v_w, o_w = head_w[l]
        query = [(dot_nt(low, w) + head_bias[l, 0, k]).astype(BF) for k, w in enumerate(q_w)]
        key = [dot_nt(far, w).astype(BF) for w in k_w]
        value = [(dot_nt(far, w) + head_bias[l, 1, k]).astype(BF) for k, w in enumerate(v_w)]
        context = [attend(*qkv, seg_q, seg_k, reach) for qkv in zip(query, key, value)]
        attended = hidden + out_bias[l]
        for a, w in zip(context, o_w):
            attended = attended + dot_nn(a, w)
        first_normal, first_inverse = norm_stats(attended)
        normed = first_normal * first_gain[l] + first_shift[l]
        normed_low = normed.astype(BF)
        normed, normed_low = end_round(new, (normed, normed_low))
        new = next_round()
        if l + 1 < layers:
            kinds = [next_heads[k] for k in range(4)]
        outer_now = new["unit_w"].get((l, "u"), unit_w.get((l, "u")))
        total, acts, slopes = feed_forward(normed_low, unit_w[l, "i"], outer_now, unit_bias[l])
        mixed = normed + outer_bias[l] + total
        second_normal, second_inverse = norm_stats(mixed)
        hidden = second_normal * second_gain[l] + second_shift[l]
        if l + 1 < layers:
            hidden, acts = end_round(new, (hidden, acts))
        else:
            end_round(new, ())
        swapped = [g.core(a) for a in [normed_low] + acts[g.nx :]]
        saved.append(
            (low, far, query, key, value, seg_k, reach, context, first_normal, first_inverse,
             normed_low, acts, slopes, second_normal, second_inverse, swapped)
        )
    result = hidden

    def unit_parts(mine, others, right):
        return [weight_grad(list(zip(both, right))) for both in zip(mine, others)]

    def sum_over_x(parts):
        for bit in g.bits("x")[::-1]:
            keep, give = parts[: len(parts) // 2], parts[len(parts) // 2 :]
            parts = [(a.astype(F32) + g.swap(b, "dp", bit).astype(F32)).astype(BF) for a, b in zip(keep, give)]
        return parts[0]

    def head_total(lefts, right):
        received = g.core(weight_grad([(lefts[1], right)])) if cores == 2 else None
        return weight_grad([(lefts[0], right)], received).reshape(g.nt, part, width)

    def head_steps(totals, bits):
        for bit in bits:
            keep, give = jnp.split(totals, 2)
            totals = (keep.astype(F32) + g.swap(give, "tensor", bit).astype(F32)).astype(BF)
        return totals

    def end_units(wide):
        wide = wide[None]
        for bit in g.bits("x"):
            wide = jnp.concatenate([wide, g.swap(wide, "dp", bit)])
        wide = jnp.stack([wide, g.core(wide)], 1)
        return g.turned(g.turned(wide, "x", 0), "c", 1)

    def end_heads(total):
        for bit in g.bits("x"):
            total = (total.astype(F32) + g.swap(total, "dp", bit).astype(F32)).astype(BF)
        if cores == 2:
            return g.turned(jnp.stack([total, g.core(total)]), "c", 0)
        return (total.astype(F32) + g.core(total).astype(F32))[None]

    unit_ends, head_ends, vectors = [[None, None] for _ in range(layers)], [None] * layers, [None] * layers
    grad_hidden = cotangent.astype(F32)
    shares = {}

    for l in reversed(range(layers)):
        (low, far, query, key, value, seg_k, reach, context, first_normal, first_inverse,
         normed_low, acts, slopes, second_normal, second_inverse, swapped) = saved[l]
        q_w, k_w, v_w, o_w = head_w[l]
        inner_w, outer_w = unit_w[l, "i"], unit_w[l, "u"]
        grad_mixed, d_second_gain, d_second_shift = norm_back(
            grad_hidden, second_normal, second_inverse, second_gain[l]
        )
        mixed_low = grad_mixed.astype(BF)
        d_outer_bias = jnp.sum(grad_mixed, axis=0)
        mixed_both = mixed_low, g.core(mixed_low)
        normed_both = normed_low, swapped[0]
        outer_parts = unit_parts(acts[: g.nx], swapped[1:], mixed_both)
        outer_parts, mixed_low, grad_mixed = together(outer_parts, mixed_low, grad_mixed)
        outer_sum = sum_over_x(outer_parts)
        total, d_inner_bias, grad_inner = feed_forward_back(mixed_low, inner_w, outer_w, slopes)
        inner_parts = unit_parts(grad_inner[: g.nx], [g.core(a) for a in grad_inner[g.nx :]], normed_both)
        grad_normed = grad_mixed + total
        grad_attended, d_first_gain, d_first_shift = norm_back(
            grad_normed, first_normal, first_inverse, first_gain[l]
        )
        outer_sum, inner_parts, grad_attended = together(outer_sum, inner_parts, grad_attended)
        inner_sum = sum_over_x(inner_parts)
        if l == 0:
            outer_sum = back_by_steps(outer_sum)
        d_out_bias = jnp.sum(grad_attended, axis=0)
        attended_low = grad_attended.astype(BF)
        grad_context = [dot_nt(attended_low, w).astype(BF) for w in o_w]
        out_total = head_total(context, attended_low)
        if l == 0:
            out_total = back_by_steps(out_total)
        backs = [
            attend_back(query[k], key[k], value[k], grad_context[k], seg_q, seg_k, reach) for k in range(cores)
        ]
        inner_sum, outer_sum, out_total, backs = together(inner_sum, outer_sum, out_total, backs)
        d_query, d_key, d_value = zip(*backs)
        if l == 0:
            v_total = back_by_steps(head_total(d_value, far))
        far_part = sum(
            dot_nn(a, w) for grad, weight in ((d_key, k_w), (d_value, v_w)) for a, w in zip(grad, weight)
        ).astype(BF)
        far_sum = near_sums(far_part) if reach else far_sums(far_part)
        near_sum = grad_attended
        for a, w in zip(d_query, q_w):
            near_sum = near_sum + dot_nn(a, w)
        grad_hidden = near_sum + far_sum
        q_total, k_total = head_total(d_query, low), head_total(d_key, far)
        if l == 0:
            shares[l, "iu"] = jnp.concatenate([back_by_steps(inner_sum), outer_sum])
            kinds = [back_by_steps(q_total), back_by_steps(k_total), v_total, out_total]
            head_ends[l] = jnp.concatenate([a.reshape(-1, width) for a in kinds])
        else:
            pack = jnp.stack([inner_sum.reshape(g.nt, block, width), outer_sum.reshape(g.nt, block, width)], 1)
            shares[l, "iu"] = lax.psum_scatter(
                pack.reshape(-1, width), "tensor", scatter_dimension=0, tiled=True
            )
            pack = jnp.concatenate([q_total, k_total, head_total(d_value, far), out_total], 1)
            head_ends[l] = lax.psum_scatter(
                pack.reshape(-1, width), "tensor", scatter_dimension=0, tiled=True
            )
        unit_order = d_inner_bias.reshape(2, g.nx, g.nt, block)
        unit_order = g.turned(g.turned(unit_order, "c", 0), "x", 1)
        if l == 0:
            unit_order = from_steps(unit_order, 2)
        head_grad = jnp.stack(
            [jnp.stack([jnp.sum(a, axis=0, dtype=F32) for a in grad]) for grad in (d_query, d_value)]
        ).reshape(2, cores, g.nt, part)
        if cores == 2:
            head_grad = g.turned(head_grad, "c", 1)
        if l == 0:
            head_grad = from_steps(head_grad, 2)
        vectors[l] = jnp.concatenate(
            [d_out_bias, d_first_gain, d_first_shift, d_outer_bias, d_second_gain, d_second_shift,
             jnp.transpose(unit_order, (2, 1, 0, 3)).reshape(-1),
             jnp.transpose(head_grad, (0, 2, 1, 3)).reshape(-1)]
        )

    vector = g.sum_all(jnp.stack(vectors))
    shared = [vector[:, k * width : (k + 1) * width] for k in range(6)]

    def own_part(start, count):
        return lax.dynamic_slice(vector, (0, start + g.tensor * count), (layers, count))

    d_inner_bias = own_part(6 * width, units)
    d_query_bias = own_part(6 * width + units * g.nt, heads)
    d_value_bias = own_part(6 * width + (units + heads) * g.nt, heads)

    ends = [
        (end_units(shares[l, "iu"]), end_heads(head_ends[l]))
        for l in range(layers)
    ]

    def shard(l, kind):
        wide, total = ends[l]
        if kind in "iu":
            k = "iu".index(kind)
            array = wide[:, :, k * block : (k + 1) * block].reshape(units, width)
        else:
            k = "qkvo".index(kind)
            array = total[:, k * part : (k + 1) * part].reshape(heads, width)
        return array

    kinds = [[shard(l, kind) for l in range(layers)] for kind in "qkviou"]
    d_query, d_key, d_value, d_inner, d_out, d_outer = gradients_out(kinds[:4], kinds[4:])
    return (
        result,
        grad_hidden,
        d_query,
        d_query_bias,
        d_key,
        d_value,
        d_value_bias,
        d_out,
        shared[0],
        shared[1],
        shared[2],
        d_inner,
        d_inner_bias,
        d_outer,
        shared[3],
        shared[4],
        shared[5],
    )


HINT = 1 << 16


def solution(mesh):
    rows = P(("dp", "tensor"), None)
    columns = P(None, None, "tensor")
    units = P(None, "tensor", None)
    vector = P(None, "tensor")
    in_specs = (
        rows, P("dp", None), columns, vector, columns, columns, vector, units, P(), P(), P(),
        columns, vector, units, P(), P(), P(), rows,
    )
    out_specs = (
        rows, rows, columns, vector, columns, columns, vector, units, P(), P(), P(),
        columns, vector, units, P(), P(), P(),
    )
    return jax.shard_map(
        partial(shards, Grid(mesh)), mesh=mesh, in_specs=in_specs, out_specs=out_specs, check_vma=False
    )
```

time: 1700 us -> 962 us (0.57)
  waiting for transfers between devices: 1310 us -> 480 us
  matrix products: 190 us -> 39.6 us
  Pallas kernels: 0 us -> 150 us
  starting transfers between devices: 2.34 us -> 92.3 us
  blocking collectives: 48.9 us -> 0 us
  local copies, waits for them, and re-layouts: 48.2 us -> 88.6 us
    reduce_scatter x8 -> x2, waiting for transfers between devices: 682 us -> 0.04 us  [shards(): lax.psum_scatter(pack.reshape(-1, width), 'tensor', scatter_dimension=0,...]
    all_gather x8 -> x2, waiting for transfers between devices: 566 us -> 0.01 us  [the longest x1 0.01 us: shards(): both = lax.all_gather(pieces, 'tensor', axis=0)]
    ppermute x0 -> x95, waiting for transfers between devices: none -> 480 us  [the longest x91 473 us: swap(): return lax.ppermute(array, axis, [(i, i ^ bit) for i in range(count)])]
    dot_general x64 -> x32, matrix products: 190 us -> 39.6 us  [the longest x16 20.6 us: dot_nt(): lax.dot_general(left, right, (((1,), (1,)), ((), ())), preferred_element_...]
    pallas_call x0 -> x37, Pallas kernels: none -> 150 us  [the longest x24 46.7 us: weight_grad(): pl.pallas_call(kernel, grid=(columns // tile,), in_specs=specs, out_specs...]
    ppermute x0 -> x95, starting transfers between devices: none -> 92.1 us  [the longest x91 80.5 us: swap(): return lax.ppermute(array, axis, [(i, i ^ bit) for i in range(count)])]
    psum x1 -> x0, waiting for transfers between devices: 61.7 us -> none  [shards(): lax.psum(stacked_sharded[0].astype(jnp.bfloat16), 'dp').astype(jnp.float32)]
    psum x2 -> x0, blocking collectives: 48.9 us -> none  [the longest x1 41.4 us: shards(): lax.psum((stacked_shared[0], stacked_shared[1], stacked_shared[2], stacke...]
  transfers between devices with their start and end apart: 17 -> 99, of which waited for: 17 -> 43; matrix products, arithmetic and copies ran while one was open for 3% -> 17% of each run, Pallas kernels for 0% -> 14%
where the time goes in v1:
time: 962 us; the launch traced here: 952 us
  waiting for transfers between devices  480 us (50%)
  Pallas kernels  150 us (16%)
  starting transfers between devices  92.3 us (10%)
  local copies, waits for them, and re-layouts  88.6 us (9%)
  other arithmetic  83.5 us (9%)
  matrix products  39.6 us (4%)
  between operations  17.8 us (2%)
    ppermute x91, waiting for transfers between devices, swap(): return lax.ppermute(array, axis, [(i, i ^ bit) for i in range(count)])  473 us
    ppermute x91, starting transfers between devices, swap(): return lax.ppermute(array, axis, [(i, i ^ bit) for i in range(count)])  80.5 us
    pallas_call x24, Pallas kernels, weight_grad(): pl.pallas_call(kernel, grid=(columns // tile,), in_specs=specs, out_specs...  46.7 us
    unnamed x421, local copies, waits for them, and re-layouts  43 us
    pallas_call x4, Pallas kernels, streamed(): pl.pallas_call(kernel, in_specs=[whole] * (near_count + extra_count) + [a...  41.8 us
    pallas_call x4, Pallas kernels, attend_back(): pl.pallas_call(partial(attend_back_kernel, halo), grid=(width // LANES,),...  34 us
    pallas_call x4, Pallas kernels, attend(): pl.pallas_call(partial(attend_kernel, halo), grid=(width // LANES,), in_s...  21.8 us
    dot_general x16, matrix products, dot_nt(): lax.dot_general(left, right, (((1,), (1,)), ((), ())), preferred_element_...  20.6 us
  transfers between devices with their start and end apart: 99, of which 43 were waited for; matrix products, arithmetic and copies ran while one was open for 17% of the time, Pallas kernels for 14%

profile of v1, /device:TPU:0, one launch (start us, length us, event | category | flops | bytes accessed | tf_op | source)
XLA Modules:
  0.0 951.8 jit_solution(830803833462033229)
XLA Ops:
  32.3 18.6 %collective-permute-done.5 = f32[1,2,768]{2,1,0:T(2,128)S(1)} collective-permute-done((f32[1,2,768]{2,1,0:T(2,128)S(1)}, f32[1,2,768]{2,1,0:T(2,128)S(1)}, u32[]{:S(2)}, u32[]{:S(2)}) %collective-permute-start.5) | collective-permute-done | bytes 6176 | tf_op jit(solution)/shard_map/ppermute | solution.py:311
  62.3 8.5 collective-permute-done.9
  73.1 29.3 %collective-permute-done.3 = bf16[256,1024]{1,0:T(8,128)(2,1)} collective-permute-done((bf16[256,1024]{1,0:T(8,128)(2,1)}, bf16[256,1024]{1,0:T(8,128)(2,1)}, u32[]{:S(2)}, u32[]{:S(2)}) %collective-permute-start.3) | collective-permute-done | bytes 524320 | tf_op jit(solution)/shard_map/ppermute | solution.py:311
  107.0 31.2 %collective-permute-done.10 = bf16[2,256,1024]{2,1,0:T(8,128)(2,1)} collective-permute-done((bf16[2,256,1024]{2,1,0:T(8,128)(2,1)}, bf16[2,256,1024]{2,1,0:T(8,128)(2,1)}, u32[]{:S(2)}, u32[]{:S(2)}) %collective-permute-start.10) | collective-permute-done | bytes 1048608 | tf_op jit(solution)/shard_map/ppermute | solution.py:311
  147.0 11.6 %collective-permute-done.11 = bf16[128,1024]{1,0:T(8,128)(2,1)S(1)} collective-permute-done((bf16[128,1024]{1,0:T(8,128)(2,1)S(1)}, bf16[128,1024]{1,0:T(8,128)(2,1)S(1)}, u32[]{:S(2)}, u32[]{:S(2)}) %collective-permute-start.11) | collective-permute-done | bytes 262176 | tf_op jit(solution)/shard_map/ppermute | solution.py:311
  167.0 7.5 collective-permute-done.12
  182.2 13.0 %collective-permute-done.15 = bf16[512,1024]{1,0:T(8,128)(2,1)} collective-permute-done((bf16[512,1024]{1,0:T(8,128)(2,1)}, bf16[512,1024]{1,0:T(8,128)(2,1)}, u32[]{:S(2)}, u32[]{:S(2)}) %collective-permute-start.15) | collective-permute-done | bytes 1048608 | tf_op jit(solution)/shard_map/ppermute | solution.py:311
  196.6 19.0 %collective-permute-done.13 = bf16[512,1024]{1,0:T(8,128)(2,1)} collective-permute-done((bf16[512,1024]{1,0:T(8,128)(2,1)}, bf16[512,1024]{1,0:T(8,128)(2,1)}, u32[]{:S(2)}, u32[]{:S(2)}) %collective-permute-start.13) | collective-permute-done | bytes 1048608 | tf_op jit(solution)/shard_map/ppermute | solution.py:311
  252.0 20.7 %collective-permute-done.17.refs_7_.refs_6_ = bf16[1024,1024]{1,0:T(8,128)(2,1)} collective-permute-done((bf16[1024,1024]{1,0:T(8,128)(2,1)}, bf16[1024,1024]{1,0:T(8,128)(2,1)}, u32[]{:S(2)}, u32[]{:S(2)}) %collective-permute-start.17) | collective-permute-done | bytes 2097184 | tf_op jit(solution)/shard_map/ppermute | solution.py:311
  284.3 12.0 %feed_forward.2 = (f32[256,1024]{1,0:T(8,128)S(1)}, bf16[256,1024]{1,0:T(8,128)(2,1)S(1)}, bf16[256,1024]{1,0:T(8,128)(2,1)S(1)}, bf16[256,1024]{1,0:T(8,128)(2,...) custom-call(bf16[256,1024]{1,0:T(8,128)(2,1)} %get-tuple-element.163, ...), custom_call_target="tpu_custom_call" | custom-call | flops 65536 | bytes 65536 | tf_op jit(solution)/shard_map/feed_forward/pallas_call | solution.py:181
  298.2 29.7 %collective-permute-done.1.refs_3_.refs_10_ = bf16[1024,1024]{1,0:T(8,128)(2,1)S(1)} collective-permute-done((bf16[1024,1024]{1,0:T(8,128)(2,1)S(1)}, bf16[1024,1024]{1,0:T(8,128)(2,1)S(1)}, u32[]{:S(2)}, u32[]{:S(2)}) %collective-permute-start.1) | collective-permute-done | bytes 2097184 | tf_op jit(solution)/shard_map/ppermute | solution.py:311
  367.7 21.4 %collective-permute-done.refs_7_.refs_6_ = bf16[1024,1024]{1,0:T(8,128)(2,1)S(1)} collective-permute-done((bf16[1024,1024]{1,0:T(8,128)(2,1)}, bf16[1024,1024]{1,0:T(8,128)(2,1)S(1)}, u32[]{:S(2)}, u32[]{:S(2)}) %collective-permute-start) | collective-permute-done | bytes 2097184 | tf_op jit(solution)/shard_map/ppermute | solution.py:311
  397.7 10.0 %feed_forward.3 = (f32[256,1024]{1,0:T(8,128)S(1)}, bf16[256,1024]{1,0:T(8,128)(2,1)S(1)}, bf16[256,1024]{1,0:T(8,128)(2,1)S(1)}, bf16[256,1024]{1,0:T(8,128)(2,...) custom-call(bf16[256,1024]{1,0:T(8,128)(2,1)S(1)} %get-tuple-element, ...), custom_call_target="tpu_custom_call" | custom-call | flops 65536 | bytes 65536 | tf_op jit(solution)/shard_map/feed_forward/pallas_call | solution.py:181
  420.8 9.3 feed_forward_back.2
  437.7 29.3 %collective-permute-done.39 = bf16[1024,1024]{1,0:T(8,128)(2,1)} collective-permute-done((bf16[1024,1024]{1,0:T(8,128)(2,1)S(1)}, bf16[1024,1024]{1,0:T(8,128)(2,1)}, u32[]{:S(2)}, u32[]{:S(2)}) %collective-permute-start.39) | collective-permute-done | bytes 2097184 | tf_op jit(solution)/shard_map/ppermute | solution.py:311
  476.4 6.8 attend_back.4
  493.9 24.0 %collective-permute-done.43 = bf16[1024,1024]{1,0:T(8,128)(2,1)} collective-permute-done((bf16[1024,1024]{1,0:T(8,128)(2,1)S(1)}, bf16[1024,1024]{1,0:T(8,128)(2,1)}, u32[]{:S(2)}, u32[]{:S(2)}) %collective-permute-start.43) | collective-permute-done | bytes 2097184 | tf_op jit(solution)/shard_map/ppermute | solution.py:311
  587.9 10.5 %feed_forward_back.3 = (f32[256,1024]{1,0:T(8,128)S(1)}, f32[4,1024]{1,0:T(4,128)S(1)}, bf16[256,1024]{1,0:T(8,128)(2,1)S(1)}, bf16[256,1024]{1,0:T(8,128)(2,1)S...) custom-call(bf16[256,1024]{1,0:T(8,128)(2,1)} %convert_element_type.381.refs_1_.refs_0_, ...), custom_call_target="tpu_custom_call" | custom-call | flops 65536 | bytes 65536 | tf_op jit(solution)/shard_map/feed_forward_back/pallas_call | solution.py:181
  640.6 11.7 %collective-permute-start.55 = (bf16[512,1024]{1,0:T(8,128)(2,1)S(1)}, bf16[512,1024]{1,0:T(8,128)(2,1)S(1)}, u32[]{:S(2)}, u32[]{:S(2)}) collective-permute-start(bf16[512,1024]{1,0:T(8,128)(2,1)S(1)} %split.130), channel_id=1, source_target_pairs={{0,1},{1,0},{2,3},{3,2},{4,5},{5,4},{6,7},{7,6},{8,9},{9,8},{10,11... | collective-permute-start | bytes 3145736 | tf_op jit(solution)/shard_map/ppermute | solution.py:311
  655.0 32.3 %collective-permute-done.55 = bf16[512,1024]{1,0:T(8,128)(2,1)S(1)} collective-permute-done((bf16[512,1024]{1,0:T(8,128)(2,1)S(1)}, bf16[512,1024]{1,0:T(8,128)(2,1)S(1)}, u32[]{:S(2)}, u32[]{:S(2)}) %collective-permute-start.55) | collective-permute-done | bytes 1048608 | tf_op jit(solution)/shard_map/ppermute | solution.py:311
  688.4 12.0 %collective-permute-done.59 = bf16[4,64,1024]{2,1,0:T(8,128)(2,1)S(1)} collective-permute-done((bf16[4,64,1024]{2,1,0:T(8,128)(2,1)S(1)}, bf16[4,64,1024]{2,1,0:T(8,128)(2,1)S(1)}, u32[]{:S(2)}, u32[]{:S(2)}) %collective-permute-start.59) | collective-permute-done | bytes 524320 | tf_op jit(solution)/shard_map/ppermute | solution.py:311
  710.5 10.1 %attend_back.6 = (bf16[256,512]{1,0:T(8,128)(2,1)S(1)}, bf16[1024,512]{1,0:T(8,128)(2,1)S(1)}, bf16[1024,512]{1,0:T(8,128)(2,1)S(1)}) custom-call(s32[256,1]{1,0:T(8,128)S(1)} %copy.134.seg_q_ref, s32[1,1024]{1,0:T(1,128)S(1)} %bitcast.292, bf16[256,512]{1,0:T(8,128)(2,1)S(1)} %copy-done.76, bf16[1024,512]{1,0:T(8,128)(2,1)S(1)} %copy-done.36, ...), custom_call_target="tpu_custom_call" | custom-call | flops 65536 | bytes 65536 | tf_op jit(solution)/shard_map/attend_back/pallas_call | solution.py:110
  722.3 10.4 %attend_back.7 = (bf16[256,512]{1,0:T(8,128)(2,1)S(1)}, bf16[1024,512]{1,0:T(8,128)(2,1)S(1)}, bf16[1024,512]{1,0:T(8,128)(2,1)S(1)}) custom-call(s32[256,1]{1,0:T(8,128)S(1)} %copy.134.seg_q_ref, s32[1,1024]{1,0:T(1,128)S(1)} %bitcast.293, bf16[256,512]{1,0:T(8,128)(2,1)S(1)} %copy-done.78, bf16[1024,512]{1,0:T(8,128)(2,1)S(1)} %copy-done.40, ...), custom_call_target="tpu_custom_call" | custom-call | flops 65536 | bytes 65536 | tf_op jit(solution)/shard_map/attend_back/pallas_call | solution.py:110
  734.5 14.8 %collective-permute-done.61 = bf16[1,64,1024]{2,1,0:T(8,128)(2,1)S(1)} collective-permute-done((bf16[1,64,1024]{2,1,0:T(8,128)(2,1)S(1)}, bf16[1,64,1024]{2,1,0:T(8,128)(2,1)S(1)}, u32[]{:S(2)}, u32[]{:S(2)}) %collective-permute-start.61) | collective-permute-done | bytes 131104 | tf_op jit(solution)/shard_map/ppermute | solution.py:311
  771.9 23.0 %collective-permute-done.92 = f32[2,12288]{1,0:T(2,128)S(1)} collective-permute-done((f32[2,12288]{1,0:T(2,128)S(1)}, f32[2,12288]{1,0:T(2,128)S(1)}, u32[]{:S(2)}, u32[]{:S(2)}) %collective-permute-start.92) | collective-permute-done | bytes 98336 | tf_op jit(solution)/shard_map/ppermute | solution.py:311
  825.5 8.9 collective-permute-done.69
  844.5 11.4 %collective-permute-done.74 = bf16[2,64,1024]{2,1,0:T(8,128)(2,1)S(1)} collective-permute-done((bf16[2,64,1024]{2,1,0:T(8,128)(2,1)S(1)}, bf16[2,64,1024]{2,1,0:T(8,128)(2,1)S(1)}, u32[]{:S(2)}, u32[]{:S(2)}) %collective-permute-start.74) | collective-permute-done | bytes 262176 | tf_op jit(solution)/shard_map/ppermute | solution.py:311
  864.8 8.2 collective-permute-done.75
  881.4 10.9 %collective-permute-done.76 = bf16[256,1024]{1,0:T(8,128)(2,1)S(1)} collective-permute-done((bf16[256,1024]{1,0:T(8,128)(2,1)S(1)}, bf16[256,1024]{1,0:T(8,128)(2,1)S(1)}, u32[]{:S(2)}, u32[]{:S(2)}) %collective-permute-start.76) | collective-permute-done | bytes 524320 | tf_op jit(solution)/shard_map/ppermute | solution.py:311
  893.2 8.4 collective-permute-done.86
  908.0 11.0 %collective-permute-done.88 = bf16[1,256,1024]{2,1,0:T(8,128)(2,1)S(1)} collective-permute-done((bf16[1,256,1024]{2,1,0:T(8,128)(2,1)}, bf16[1,256,1024]{2,1,0:T(8,128)(2,1)S(1)}, u32[]{:S(2)}, u32[]{:S(2)}) %collective-permute-start.88) | collective-permute-done | bytes 524320 | tf_op jit(solution)/shard_map/ppermute | solution.py:311
  923.8 11.8 %collective-permute-done.81 = bf16[256,1024]{1,0:T(8,128)(2,1)S(1)} collective-permute-done((bf16[256,1024]{1,0:T(8,128)(2,1)}, bf16[256,1024]{1,0:T(8,128)(2,1)S(1)}, u32[]{:S(2)}, u32[]{:S(2)}) %collective-permute-start.81) | collective-permute-done | bytes 524320 | tf_op jit(solution)/shard_map/ppermute | solution.py:311
  (904 shorter events, 436.6 us)
Async XLA Ops:
  7.2 268.7 %all-gather.5.cloned.1.call-start = ((), (), s32[]{:S(2)}) async-start(), calls=%async_computation.4 | async-start | bytes 4718592 | tf_op jit(solution)/shard_map/all_gather | solution.py:517
  14.4 321.5 %all-gather.7.cloned.1.call-start = ((), (), s32[]{:S(2)}) async-start(), calls=%async_computation.5 | async-start | bytes 4718592 | tf_op jit(solution)/shard_map/all_gather | solution.py:536
  15.0 45.0 %collective-permute-start.2 = (bf16[128,1024]{1,0:T(8,128)(2,1)S(1)}, bf16[128,1024]{1,0:T(8,128)(2,1)S(1)}, u32[]{:S(2)}, u32[]{:S(2)}) collective-permute-start(bf16[128,1024]{1,0:T(8,128)(2,1)S(1)} %dynamic-slice_bitcast_fusion.1), channel_id=1, source_target_pairs={{0,4},{1,5},{2,6},{3,7},{4,0},{5,1},{6,2},{7,3},{8,12},{9,13},{10,... | collective-permute-start | bytes 786440 | tf_op jit(solution)/shard_map/ppermute | solution.py:311
  19.3 124.6 %collective-permute-start.8 = (bf16[256,1024]{1,0:T(8,128)(2,1)S(1)}, bf16[256,1024]{1,0:T(8,128)(2,1)S(1)}, u32[]{:S(2)}, u32[]{:S(2)}) collective-permute-start(bf16[256,1024]{1,0:T(8,128)(2,1)S(1)} %copy-done.127), channel_id=1, source_target_pairs={{0,1},{1,0},{2,3},{3,2},{4,5},{5,4},{6,7},{7,6},{8,9},{9,8},{10,11... | collective-permute-start | bytes 1572872 | tf_op jit(solution)/shard_map/ppermute | solution.py:311
  28.0 42.8 %collective-permute-start.9 = (bf16[1,256,1024]{2,1,0:T(8,128)(2,1)S(1)}, bf16[1,256,1024]{2,1,0:T(8,128)(2,1)S(1)}, u32[]{:S(2)}, u32[]{:S(2)}) collective-permute-start(bf16[1,256,1024]{2,1,0:T(8,128)(2,1)S(1)} %bitcast.304), channel_id=1, source_target_pairs={{0,4},{1,5},{2,6},{3,7},{4,0},{5,1},{6,2},{7,3},{8,12},{9,13},{10,... | collective-permute-start | bytes 1572872 | tf_op jit(solution)/shard_map/ppermute | solution.py:311
  60.9 41.4 %collective-permute-start.3 = (bf16[256,1024]{1,0:T(8,128)(2,1)}, bf16[256,1024]{1,0:T(8,128)(2,1)}, u32[]{:S(2)}, u32[]{:S(2)}) collective-permute-start(bf16[256,1024]{1,0:T(8,128)(2,1)} %pad_maximum_fusion.22), channel_id=1, source_target_pairs={{0,2},{1,3},{2,0},{3,1},{4,6},{5,7},{6,4},{7,5},{8,10},{9,11},{10,... | collective-permute-start | bytes 1572872 | tf_op jit(solution)/shard_map/ppermute | solution.py:311
  71.9 66.3 %collective-permute-start.10 = (bf16[2,256,1024]{2,1,0:T(8,128)(2,1)}, bf16[2,256,1024]{2,1,0:T(8,128)(2,1)}, u32[]{:S(2)}, u32[]{:S(2)}) collective-permute-start(bf16[2,256,1024]{2,1,0:T(8,128)(2,1)} %pad_maximum_fusion.9), channel_id=1, source_target_pairs={{0,2},{1,3},{2,0},{3,1},{4,6},{5,7},{6,4},{7,5},{8,10},{9,11},{10,... | collective-permute-start | bytes 3145736 | tf_op jit(solution)/shard_map/ppermute | solution.py:311
  145.5 72.8 %collective-permute-start.16 = (bf16[4,256,1024]{2,1,0:T(8,128)(2,1)}, bf16[4,256,1024]{2,1,0:T(8,128)(2,1)}, u32[]{:S(2)}, u32[]{:S(2)}) collective-permute-start(bf16[4,256,1024]{2,1,0:T(8,128)(2,1)} %pad_maximum_fusion.3), channel_id=1, source_target_pairs={{0,1},{1,0},{2,3},{3,2},{4,5},{5,4},{6,7},{7,6},{8,9},{9,8},{10,11... | collective-permute-start | bytes 6291464 | tf_op jit(solution)/shard_map/ppermute | solution.py:311
  162.4 60.9 %collective-permute-start.14 = (bf16[1024,1024]{1,0:T(8,128)(2,1)}, bf16[1024,1024]{1,0:T(8,128)(2,1)}, u32[]{:S(2)}, u32[]{:S(2)}) collective-permute-start(bf16[1024,1024]{1,0:T(8,128)(2,1)} %pad_maximum_fusion.2.refs_2_.refs_9_), channel_id=1, source_target_pairs={{0,16},{8,24},{16,0},{24,8},{1,17},{9,25},{17,1},{25,9},{2,18},{10... | collective-permute-start | bytes 6291464 | tf_op jit(solution)/shard_map/ppermute | solution.py:311
  223.3 681.0 %reduce-scatter.5.cloned.1.call-start = ((), (), s32[]{:S(2)}) async-start(), calls=%async_computation.3 | async-start | bytes 4718592 | tf_op jit(solution)/shard_map/reduce_scatter | solution.py:663
  224.3 48.4 %collective-permute-start.17 = (bf16[1024,1024]{1,0:T(8,128)(2,1)}, bf16[1024,1024]{1,0:T(8,128)(2,1)}, u32[]{:S(2)}, u32[]{:S(2)}) collective-permute-start(bf16[1024,1024]{1,0:T(8,128)(2,1)} %pad_maximum_fusion.4.refs_6_.refs_5_), channel_id=1, source_target_pairs={{0,16},{8,24},{16,0},{24,8},{1,17},{9,25},{17,1},{25,9},{2,18},{10... | collective-permute-start | bytes 6291464 | tf_op jit(solution)/shard_map/ppermute | solution.py:311
  225.8 46.9 %collective-permute-start.18 = (bf16[1024,1024]{1,0:T(8,128)(2,1)}, bf16[1024,1024]{1,0:T(8,128)(2,1)S(1)}, u32[]{:S(2)}, u32[]{:S(2)}) collective-permute-start(bf16[1024,1024]{1,0:T(8,128)(2,1)} %pad_maximum_fusion.2.refs_2_.refs_9_), channel_id=1, source_target_pairs={{0,8},{8,0},{16,24},{24,16},{1,9},{9,1},{17,25},{25,17},{2,10},{10... | collective-permute-start | bytes 6291464 | tf_op jit(solution)/shard_map/ppermute | solution.py:311
  280.3 47.6 %collective-permute-start.1 = (bf16[1024,1024]{1,0:T(8,128)(2,1)S(1)}, bf16[1024,1024]{1,0:T(8,128)(2,1)S(1)}, u32[]{:S(2)}, u32[]{:S(2)}) collective-permute-start(bf16[1024,1024]{1,0:T(8,128)(2,1)S(1)} %bitcast.266), channel_id=1, source_target_pairs={{0,16},{8,24},{16,0},{24,8},{1,17},{9,25},{17,1},{25,9},{2,18},{10... | collective-permute-start | bytes 6291464 | tf_op jit(solution)/shard_map/ppermute | solution.py:311
  341.4 47.7 %collective-permute-start = (bf16[1024,1024]{1,0:T(8,128)(2,1)}, bf16[1024,1024]{1,0:T(8,128)(2,1)S(1)}, u32[]{:S(2)}, u32[]{:S(2)}) collective-permute-start(bf16[1024,1024]{1,0:T(8,128)(2,1)} %bitcast.270), channel_id=1, source_target_pairs={{0,16},{8,24},{16,0},{24,8},{1,17},{9,25},{17,1},{25,9},{2,18},{10... | collective-permute-start | bytes 6291464 | tf_op jit(solution)/shard_map/ppermute | solution.py:311
  342.9 46.3 %collective-permute-start.26 = (bf16[1024,1024]{1,0:T(8,128)(2,1)}, bf16[1024,1024]{1,0:T(8,128)(2,1)S(1)}, u32[]{:S(2)}, u32[]{:S(2)}) collective-permute-start(bf16[1024,1024]{1,0:T(8,128)(2,1)} %bitcast.267), channel_id=1, source_target_pairs={{0,8},{8,0},{16,24},{24,16},{1,9},{9,1},{17,25},{25,17},{2,10},{10... | collective-permute-start | bytes 6291464 | tf_op jit(solution)/shard_map/ppermute | solution.py:311
  419.2 47.8 %collective-permute-start.39 = (bf16[1024,1024]{1,0:T(8,128)(2,1)S(1)}, bf16[1024,1024]{1,0:T(8,128)(2,1)}, u32[]{:S(2)}, u32[]{:S(2)}) collective-permute-start(bf16[1024,1024]{1,0:T(8,128)(2,1)S(1)} %weight_grad.25), channel_id=1, source_target_pairs={{0,16},{8,24},{16,0},{24,8},{1,17},{9,25},{17,1},{25,9},{2,18},{10... | collective-permute-start | bytes 6291464 | tf_op jit(solution)/shard_map/ppermute | solution.py:311
  470.9 46.9 %collective-permute-start.43 = (bf16[1024,1024]{1,0:T(8,128)(2,1)S(1)}, bf16[1024,1024]{1,0:T(8,128)(2,1)}, u32[]{:S(2)}, u32[]{:S(2)}) collective-permute-start(bf16[1024,1024]{1,0:T(8,128)(2,1)S(1)} %weight_grad.27), channel_id=1, source_target_pairs={{0,16},{8,24},{16,0},{24,8},{1,17},{9,25},{17,1},{25,9},{2,18},{10... | collective-permute-start | bytes 6291464 | tf_op jit(solution)/shard_map/ppermute | solution.py:311
  522.9 398.1 %reduce-scatter.3.cloned.1.call-start = ((), (), s32[]{:S(2)}) async-start(), calls=%async_computation.2 | async-start | bytes 4718592 | tf_op jit(solution)/shard_map/reduce_scatter | solution.py:667
  522.9 92.8 %collective-permute-start.52 = (bf16[256,1024]{1,0:T(8,128)(2,1)}, bf16[256,1024]{1,0:T(8,128)(2,1)}, u32[]{:S(2)}, u32[]{:S(2)}) collective-permute-start(bf16[256,1024]{1,0:T(8,128)(2,1)} %get-tuple-element.163.refs_0_.refs_1_), channel_id=1, source_target_pairs={{0,8},{8,0},{16,24},{24,16},{1,9},{9,1},{17,25},{25,17},{2,10},{10... | collective-permute-start | bytes 1572872 | tf_op jit(solution)/shard_map/ppermute | solution.py:311
  523.0 47.0 %collective-permute-start.47 = (bf16[256,1024]{1,0:T(8,128)(2,1)}, bf16[256,1024]{1,0:T(8,128)(2,1)}, u32[]{:S(2)}, u32[]{:S(2)}) collective-permute-start(bf16[256,1024]{1,0:T(8,128)(2,1)} %get-tuple-element.225), channel_id=1, source_target_pairs={{0,8},{8,0},{16,24},{24,16},{1,9},{9,1},{17,25},{25,17},{2,10},{10... | collective-permute-start | bytes 1572872 | tf_op jit(solution)/shard_map/ppermute | solution.py:311
  523.5 53.2 %collective-permute-start.49 = (bf16[256,1024]{1,0:T(8,128)(2,1)}, bf16[256,1024]{1,0:T(8,128)(2,1)}, u32[]{:S(2)}, u32[]{:S(2)}) collective-permute-start(bf16[256,1024]{1,0:T(8,128)(2,1)} %get-tuple-element.227), channel_id=1, source_target_pairs={{0,8},{8,0},{16,24},{24,16},{1,9},{9,1},{17,25},{25,17},{2,10},{10... | collective-permute-start | bytes 1572872 | tf_op jit(solution)/shard_map/ppermute | solution.py:311
  557.5 49.2 %collective-permute-start.80 = (bf16[512,1024]{1,0:T(8,128)(2,1)}, bf16[512,1024]{1,0:T(8,128)(2,1)}, u32[]{:S(2)}, u32[]{:S(2)}) collective-permute-start(bf16[512,1024]{1,0:T(8,128)(2,1)} %weight_grad.46), channel_id=1, source_target_pairs={{0,8},{8,0},{16,24},{24,16},{1,9},{9,1},{17,25},{25,17},{2,10},{10... | collective-permute-start | bytes 3145736 | tf_op jit(solution)/shard_map/ppermute | solution.py:311
  570.5 43.3 %collective-permute-start.78 = (bf16[512,1024]{1,0:T(8,128)(2,1)}, bf16[512,1024]{1,0:T(8,128)(2,1)}, u32[]{:S(2)}, u32[]{:S(2)}) collective-permute-start(bf16[512,1024]{1,0:T(8,128)(2,1)} %copy-done.66), channel_id=1, source_target_pairs={{0,8},{8,0},{16,24},{24,16},{1,9},{9,1},{17,25},{25,17},{2,10},{10... | collective-permute-start | bytes 3145736 | tf_op jit(solution)/shard_map/ppermute | solution.py:311
  581.5 48.3 %collective-permute-start.50 = (bf16[1024,1024]{1,0:T(8,128)(2,1)}, bf16[1024,1024]{1,0:T(8,128)(2,1)}, u32[]{:S(2)}, u32[]{:S(2)}) collective-permute-start(bf16[1024,1024]{1,0:T(8,128)(2,1)} %weight_grad.31), channel_id=1, source_target_pairs={{0,16},{8,24},{16,0},{24,8},{1,17},{9,25},{17,1},{25,9},{2,18},{10... | collective-permute-start | bytes 6291464 | tf_op jit(solution)/shard_map/ppermute | solution.py:311
  637.7 112.3 %collective-permute-start.54 = (bf16[1024,1024]{1,0:T(8,128)(2,1)}, bf16[1024,1024]{1,0:T(8,128)(2,1)S(1)}, u32[]{:S(2)}, u32[]{:S(2)}) collective-permute-start(bf16[1024,1024]{1,0:T(8,128)(2,1)} %copy-done.59), channel_id=1, source_target_pairs={{0,16},{8,24},{16,0},{24,8},{1,17},{9,25},{17,1},{25,9},{2,18},{10... | collective-permute-start | bytes 6291464 | tf_op jit(solution)/shard_map/ppermute | solution.py:311
  640.6 46.8 %collective-permute-start.55 = (bf16[512,1024]{1,0:T(8,128)(2,1)S(1)}, bf16[512,1024]{1,0:T(8,128)(2,1)S(1)}, u32[]{:S(2)}, u32[]{:S(2)}) collective-permute-start(bf16[512,1024]{1,0:T(8,128)(2,1)S(1)} %split.130), channel_id=1, source_target_pairs={{0,1},{1,0},{2,3},{3,2},{4,5},{5,4},{6,7},{7,6},{8,9},{9,8},{10,11... | collective-permute-start | bytes 3145736 | tf_op jit(solution)/shard_map/ppermute | solution.py:311
  655.0 45.4 %collective-permute-start.59 = (bf16[4,64,1024]{2,1,0:T(8,128)(2,1)S(1)}, bf16[4,64,1024]{2,1,0:T(8,128)(2,1)S(1)}, u32[]{:S(2)}, u32[]{:S(2)}) collective-permute-start(bf16[4,64,1024]{2,1,0:T(8,128)(2,1)S(1)} %bitcast.343), channel_id=1, source_target_pairs={{0,1},{1,0},{2,3},{3,2},{4,5},{5,4},{6,7},{7,6},{8,9},{9,8},{10,11... | collective-permute-start | bytes 1572872 | tf_op jit(solution)/shard_map/ppermute | solution.py:311
  764.9 41.7 %collective-permute-start.72 = (bf16[512,1024]{1,0:T(8,128)(2,1)S(1)}, bf16[512,1024]{1,0:T(8,128)(2,1)S(1)}, u32[]{:S(2)}, u32[]{:S(2)}) collective-permute-start(bf16[512,1024]{1,0:T(8,128)(2,1)S(1)} %weight_grad.40), channel_id=1, source_target_pairs={{0,8},{8,0},{16,24},{24,16},{1,9},{9,1},{17,25},{25,17},{2,10},{10... | collective-permute-start | bytes 3145736 | tf_op jit(solution)/shard_map/ppermute | solution.py:311
  766.9 41.9 %collective-permute-start.68 = (bf16[512,1024]{1,0:T(8,128)(2,1)S(1)}, bf16[512,1024]{1,0:T(8,128)(2,1)S(1)}, u32[]{:S(2)}, u32[]{:S(2)}) collective-permute-start(bf16[512,1024]{1,0:T(8,128)(2,1)S(1)} %weight_grad.38), channel_id=1, source_target_pairs={{0,8},{8,0},{16,24},{24,16},{1,9},{9,1},{17,25},{25,17},{2,10},{10... | collective-permute-start | bytes 3145736 | tf_op jit(solution)/shard_map/ppermute | solution.py:311
  767.2 44.9 %collective-permute-start.64 = (bf16[512,1024]{1,0:T(8,128)(2,1)S(1)}, bf16[512,1024]{1,0:T(8,128)(2,1)S(1)}, u32[]{:S(2)}, u32[]{:S(2)}) collective-permute-start(bf16[512,1024]{1,0:T(8,128)(2,1)S(1)} %weight_grad.36), channel_id=1, source_target_pairs={{0,8},{8,0},{16,24},{24,16},{1,9},{9,1},{17,25},{25,17},{2,10},{10... | collective-permute-start | bytes 3145736 | tf_op jit(solution)/shard_map/ppermute | solution.py:311
  767.6 46.4 %collective-permute-start.83 = (bf16[512,1024]{1,0:T(8,128)(2,1)S(1)}, bf16[512,1024]{1,0:T(8,128)(2,1)S(1)}, u32[]{:S(2)}, u32[]{:S(2)}) collective-permute-start(bf16[512,1024]{1,0:T(8,128)(2,1)S(1)} %split.168), channel_id=1, source_target_pairs={{0,1},{1,0},{2,3},{3,2},{4,5},{5,4},{6,7},{7,6},{8,9},{9,8},{10,11... | collective-permute-start | bytes 3145736 | tf_op jit(solution)/shard_map/ppermute | solution.py:311
  805.9 73.7 %collective-permute-start.62 = (bf16[512,1024]{1,0:T(8,128)(2,1)S(1)}, bf16[512,1024]{1,0:T(8,128)(2,1)S(1)}, u32[]{:S(2)}, u32[]{:S(2)}) collective-permute-start(bf16[512,1024]{1,0:T(8,128)(2,1)S(1)} %split.184), channel_id=1, source_target_pairs={{0,2},{1,3},{2,0},{3,1},{4,6},{5,7},{6,4},{7,5},{8,10},{9,11},{10,... | collective-permute-start | bytes 3145736 | tf_op jit(solution)/shard_map/ppermute | solution.py:311
  (266 other events, 2925.6 us)
Sparse Core Ops, SparseCore 0:
  14.5 114.6 all-gather.4
  223.4 73.5 all-gather.6
  523.0 93.7 reduce-scatter.4
  637.8 115.3 reduce-scatter.2

commit v2 on v1

--- a/solution.py
+++ b/solution.py
@@ -96,7 +96,7 @@
         out_specs=near,
         out_shape=jax.ShapeDtypeStruct((rows, width), BF),
         compiler_params=pltpu.CompilerParams(vmem_limit_bytes=40 * 1024 * 1024),
-        cost_estimate=pl.CostEstimate(flops=HINT, bytes_accessed=HINT, transcendentals=0),
+        cost_estimate=hint(6.5 * keys / 1024),
         name="attend",
     )(seg_q, seg_k, query, key, value)
 
@@ -118,7 +118,7 @@
             jax.ShapeDtypeStruct((keys, width), BF),
         ],
         compiler_params=pltpu.CompilerParams(vmem_limit_bytes=48 * 1024 * 1024),
-        cost_estimate=pl.CostEstimate(flops=HINT, bytes_accessed=HINT, transcendentals=0),
+        cost_estimate=hint(10.0 * keys / 1024),
         name="attend_back",
     )(seg_q, seg_k, query, key, value, grad)
 
@@ -143,6 +143,10 @@
     half = 0.5 * (1.0 + lax.erf(inner * (0.5 ** 0.5)))
     bell = jnp.exp(-0.5 * inner * inner) * ((2.0 * jnp.pi) ** -0.5)
     return (inner * half).astype(BF), (half + inner * bell).astype(BF)
+
+
+def hint(us):
+    return pl.CostEstimate(flops=0, bytes_accessed=int(us * 1.3e6), transcendentals=0)
 
 
 def streamed(kernel_step, near, first, second, extra, outs, name):
@@ -189,7 +193,7 @@
             pltpu.SemaphoreType.DMA((2, 2)),
         ],
         compiler_params=pltpu.CompilerParams(vmem_limit_bytes=40 * 1024 * 1024),
-        cost_estimate=pl.CostEstimate(flops=HINT, bytes_accessed=HINT, transcendentals=0),
+        cost_estimate=hint(10.0),
         name=name,
     )(*near, *extra, *first, *second)
 
@@ -258,7 +262,7 @@
         out_specs=block,
         out_shape=jax.ShapeDtypeStruct((columns, width), BF),
         compiler_params=pltpu.CompilerParams(vmem_limit_bytes=32 * 1024 * 1024),
-        cost_estimate=pl.CostEstimate(flops=HINT, bytes_accessed=HINT, transcendentals=0),
+        cost_estimate=hint(2.0 * sum(a.shape[0] for a, _ in pairs) * columns / (512 * 1024)),
         name="weight_grad",
     )(*operands)
 
@@ -292,7 +296,7 @@
         out_specs=out_specs,
         out_shape=shapes,
         compiler_params=pltpu.CompilerParams(vmem_limit_bytes=40 * 1024 * 1024),
-        cost_estimate=pl.CostEstimate(flops=HINT, bytes_accessed=HINT, transcendentals=0),
+        cost_estimate=hint(5.0),
         name="gradients_out",
     )(*[a for arrays in turned + plain for a in arrays])
 
@@ -330,14 +334,6 @@
         if count == 2:
             return jnp.where(at == 0, array, lax.rev(array, (axis,)))
         return jnp.take(array, at ^ jnp.arange(count), axis=axis)
-
-    def sum_all(self, array):
-        for axis, count in (("dp", self.nd), ("tensor", self.nt)):
-            bit = 1
-            while bit < count:
-                array = array + self.swap(array, axis, bit)
-                bit *= 2
-        return array
 
 
 def together(*values):
@@ -428,12 +424,6 @@
             array = jnp.concatenate([array, g.swap(array, "tensor", bit)])
         return array
 
-    def back_by_steps(total):
-        for bit in high_to_low[::-1]:
-            keep, give = jnp.split(total, 2)
-            total = (keep.astype(F32) + g.swap(give, "tensor", bit).astype(F32)).astype(BF)
-        return total
-
     def from_steps(array, axis):
         place = jnp.array([step_order.index(m) for m in range(g.nt)])
         return jnp.take(array, place[g.tensor ^ jnp.arange(g.nt)], axis=axis)
@@ -512,20 +502,22 @@
 
     saved = []
     hidden = inputs.astype(F32)
-    for l in range(1, layers):
-        pieces = jnp.stack([unit_piece(shard_of[l, "i"]), unit_piece(shard_of[l, "u"])])
-        both = lax.all_gather(pieces, "tensor", axis=0)
-        for k, kind in enumerate("iu"):
-            gathered[l, kind] = both[:, k].reshape(-1, width)
     new = next_round()
     unit_bias, head_bias = bias_rows()
     far = g.swap(inputs, "tensor", 1) if group > 1 else inputs
     first_part = head_first(head_piece(0))
-    unit_bias, head_bias, far, first_part = end_round(new, (unit_bias, head_bias, far, first_part))
+    later = [
+        (jnp.stack([unit_piece(shard_of[l, "i"]), unit_piece(shard_of[l, "u"])]), head_piece(l).reshape(4, part, width))
+        for l in range(1, layers)
+    ]
+    unit_bias, head_bias, far, first_part, later = end_round(new, (unit_bias, head_bias, far, first_part, later))
+    for l in range(1, layers):
+        both = lax.all_gather(later[l - 1][0], "tensor", axis=0)
+        for k, kind in enumerate("iu"):
+            gathered[l, kind] = both[:, k].reshape(-1, width)
     new = next_round()
     far_inputs = far_rows(inputs, far)
     kinds = head_last(first_part)
-    later = [head_piece(l).reshape(4, part, width) for l in range(1, layers)]
     hidden, far_inputs, kinds, later = end_round(new, (hidden, far_inputs, kinds, later))
     for l in range(layers):
         windowed = l % 2 == 1
@@ -533,7 +525,7 @@
         new = next_round()
         head_w[l] = head_rows(kinds)
         if l + 1 < layers:
-            next_heads = lax.all_gather(later[l], "tensor", axis=1).reshape(4, g.nt * part, width)
+            next_heads = lax.all_gather(later[l][1], "tensor", axis=1).reshape(4, g.nt * part, width)
         if windowed:
             far, seg_k, reach = near_rows(low), seg_near, halo
         else:
@@ -583,30 +575,28 @@
         received = g.core(weight_grad([(lefts[1], right)])) if cores == 2 else None
         return weight_grad([(lefts[0], right)], received).reshape(g.nt, part, width)
 
-    def head_steps(totals, bits):
-        for bit in bits:
-            keep, give = jnp.split(totals, 2)
-            totals = (keep.astype(F32) + g.swap(give, "tensor", bit).astype(F32)).astype(BF)
-        return totals
-
-    def end_units(wide):
+    def one_step(total, bit):
+        keep, give = jnp.split(total, 2)
+        return (keep.astype(F32) + g.swap(give, "tensor", bit).astype(F32)).astype(BF)
+
+    def end_over_x(wide, total):
         wide = wide[None]
         for bit in g.bits("x"):
             wide = jnp.concatenate([wide, g.swap(wide, "dp", bit)])
+            total = (total.astype(F32) + g.swap(total, "dp", bit).astype(F32)).astype(BF)
+        return wide, total
+
+    def end_over_core(wide, total):
         wide = jnp.stack([wide, g.core(wide)], 1)
-        return g.turned(g.turned(wide, "x", 0), "c", 1)
-
-    def end_heads(total):
-        for bit in g.bits("x"):
-            total = (total.astype(F32) + g.swap(total, "dp", bit).astype(F32)).astype(BF)
+        wide = g.turned(g.turned(wide, "x", 0), "c", 1)
         if cores == 2:
-            return g.turned(jnp.stack([total, g.core(total)]), "c", 0)
-        return (total.astype(F32) + g.core(total).astype(F32))[None]
-
-    unit_ends, head_ends, vectors = [[None, None] for _ in range(layers)], [None] * layers, [None] * layers
+            return wide, g.turned(jnp.stack([total, g.core(total)]), "c", 0)
+        return wide, (total.astype(F32) + g.core(total).astype(F32))[None]
+
+    ends, vectors, later_units = [None] * layers, [None] * layers, [None] * layers
     grad_hidden = cotangent.astype(F32)
-    shares = {}
-
+    units_before = None
+    first_bits = high_to_low[::-1]
     for l in reversed(range(layers)):
         (low, far, query, key, value, seg_k, reach, context, first_normal, first_inverse,
          normed_low, acts, slopes, second_normal, second_inverse, swapped) = saved[l]
@@ -620,53 +610,44 @@
         mixed_both = mixed_low, g.core(mixed_low)
         normed_both = normed_low, swapped[0]
         outer_parts = unit_parts(acts[: g.nx], swapped[1:], mixed_both)
-        outer_parts, mixed_low, grad_mixed = together(outer_parts, mixed_low, grad_mixed)
-        outer_sum = sum_over_x(outer_parts)
+        outer_parts, mixed_low, grad_mixed, units_before = together(
+            outer_parts, mixed_low, grad_mixed, units_before
+        )
+        if units_before is not None:
+            pack = jnp.stack(units_before, 1)
+            later_units[l + 1] = lax.psum_scatter(
+                pack.reshape(-1, width), "tensor", scatter_dimension=0, tiled=True
+            )
+        outer_sum = sum_over_x(outer_parts).reshape(g.nt, block, width)
         total, d_inner_bias, grad_inner = feed_forward_back(mixed_low, inner_w, outer_w, slopes)
         inner_parts = unit_parts(grad_inner[: g.nx], [g.core(a) for a in grad_inner[g.nx :]], normed_both)
         grad_normed = grad_mixed + total
         grad_attended, d_first_gain, d_first_shift = norm_back(
             grad_normed, first_normal, first_inverse, first_gain[l]
         )
-        outer_sum, inner_parts, grad_attended = together(outer_sum, inner_parts, grad_attended)
-        inner_sum = sum_over_x(inner_parts)
-        if l == 0:
-            outer_sum = back_by_steps(outer_sum)
+        inner_parts, grad_attended = together(inner_parts, grad_attended)
+        inner_sum = sum_over_x(inner_parts).reshape(g.nt, block, width)
         d_out_bias = jnp.sum(grad_attended, axis=0)
         attended_low = grad_attended.astype(BF)
         grad_context = [dot_nt(attended_low, w).astype(BF) for w in o_w]
         out_total = head_total(context, attended_low)
-        if l == 0:
-            out_total = back_by_steps(out_total)
-        backs = [
-            attend_back(query[k], key[k], value[k], grad_context[k], seg_q, seg_k, reach) for k in range(cores)
-        ]
-        inner_sum, outer_sum, out_total, backs = together(inner_sum, outer_sum, out_total, backs)
+        backs = []
+        for k in range(cores):
+            backs.append(attend_back(query[k], key[k], value[k], grad_context[k], seg_q, seg_k, reach))
+            if k == 0:
+                backs, outer_sum, grad_context, out_total = together(backs, outer_sum, grad_context, out_total)
+            elif l == 0:
+                outer_sum, out_total = one_step(outer_sum, first_bits[0]), one_step(out_total, first_bits[0])
+        backs, outer_sum, out_total = together(backs, outer_sum, out_total)
         d_query, d_key, d_value = zip(*backs)
-        if l == 0:
-            v_total = back_by_steps(head_total(d_value, far))
         far_part = sum(
             dot_nn(a, w) for grad, weight in ((d_key, k_w), (d_value, v_w)) for a, w in zip(grad, weight)
         ).astype(BF)
-        far_sum = near_sums(far_part) if reach else far_sums(far_part)
         near_sum = grad_attended
         for a, w in zip(d_query, q_w):
             near_sum = near_sum + dot_nn(a, w)
-        grad_hidden = near_sum + far_sum
-        q_total, k_total = head_total(d_query, low), head_total(d_key, far)
-        if l == 0:
-            shares[l, "iu"] = jnp.concatenate([back_by_steps(inner_sum), outer_sum])
-            kinds = [back_by_steps(q_total), back_by_steps(k_total), v_total, out_total]
-            head_ends[l] = jnp.concatenate([a.reshape(-1, width) for a in kinds])
-        else:
-            pack = jnp.stack([inner_sum.reshape(g.nt, block, width), outer_sum.reshape(g.nt, block, width)], 1)
-            shares[l, "iu"] = lax.psum_scatter(
-                pack.reshape(-1, width), "tensor", scatter_dimension=0, tiled=True
-            )
-            pack = jnp.concatenate([q_total, k_total, head_total(d_value, far), out_total], 1)
-            head_ends[l] = lax.psum_scatter(
-                pack.reshape(-1, width), "tensor", scatter_dimension=0, tiled=True
-            )
+        v_total = head_total(d_value, far)
+        totals = [head_total(d_query, low), head_total(d_key, far), v_total]
         unit_order = d_inner_bias.reshape(2, g.nx, g.nt, block)
         unit_order = g.turned(g.turned(unit_order, "c", 0), "x", 1)
         if l == 0:
@@ -683,8 +664,59 @@
              jnp.transpose(unit_order, (2, 1, 0, 3)).reshape(-1),
              jnp.transpose(head_grad, (0, 2, 1, 3)).reshape(-1)]
         )
-
-    vector = g.sum_all(jnp.stack(vectors))
+        if l:
+            far_sum = near_sums(far_part) if reach else far_sums(far_part)
+            grad_hidden = near_sum + far_sum
+            pack = jnp.concatenate([*totals, out_total], 1)
+            ends[l] = lax.psum_scatter(pack.reshape(-1, width), "tensor", scatter_dimension=0, tiled=True)
+            units_before = inner_sum, outer_sum
+    steps_done = cores - 1
+    vector = jnp.stack(vectors)
+    hops = [(axis, 1 << k) for axis, count in (("dp", g.nd), ("tensor", g.nt)) for k in range(count.bit_length() - 1)]
+    far_bits = [1 << k for k in range(group.bit_length() - 1)][::-1]
+
+    def next_hop(vector):
+        return vector + g.swap(vector, *hops.pop(0)) if hops else vector
+
+    for bit in first_bits[steps_done : steps_done + 1]:
+        outer_sum, out_total = one_step(outer_sum, bit), one_step(out_total, bit)
+    inner_sum, totals[2] = one_step(inner_sum, first_bits[0]), one_step(totals[2], first_bits[0])
+    totals, outer_sum, out_total, inner_sum, vector, far_part = together(
+        totals, outer_sum, out_total, inner_sum, vector, far_part
+    )
+    for number, bit in enumerate(first_bits):
+        totals[:2] = [one_step(a, bit) for a in totals[:2]]
+        if number + 1 < len(first_bits):
+            inner_sum = one_step(inner_sum, first_bits[number + 1])
+            totals[2] = one_step(totals[2], first_bits[number + 1])
+        if number + steps_done + 1 < len(first_bits):
+            more = first_bits[number + steps_done + 1]
+            outer_sum, out_total = one_step(outer_sum, more), one_step(out_total, more)
+        vector = next_hop(vector)
+        if far_bits:
+            keep, give = jnp.split(far_part, 2)
+            far_part = keep.astype(F32) + g.swap(give.astype(BF), "tensor", far_bits.pop(0)).astype(F32)
+        if number == 1:
+            for l in range(1, layers):
+                ends[l] = end_over_x(later_units[l], ends[l])
+        if number == 2:
+            for l in range(1, layers):
+                ends[l] = end_over_core(*ends[l])
+        totals, outer_sum, out_total, inner_sum, vector, far_part, ends = together(
+            totals, outer_sum, out_total, inner_sum, vector, far_part, ends
+        )
+    while far_bits:
+        keep, give = jnp.split(far_part, 2)
+        far_part = keep.astype(F32) + g.swap(give.astype(BF), "tensor", far_bits.pop(0)).astype(F32)
+    grad_hidden = near_sum + far_part
+    wide = jnp.concatenate([a.reshape(-1, width) for a in (inner_sum, outer_sum)])
+    total = jnp.concatenate([a.reshape(-1, width) for a in (*totals, out_total)])
+    vector = next_hop(vector)
+    wide, total, vector = together(*end_over_x(wide, total), vector)
+    ends[0] = end_over_core(wide, total)
+    while hops:
+        vector = next_hop(vector)
+
     shared = [vector[:, k * width : (k + 1) * width] for k in range(6)]
 
     def own_part(start, count):
@@ -693,11 +725,6 @@
     d_inner_bias = own_part(6 * width, units)
     d_query_bias = own_part(6 * width + units * g.nt, heads)
     d_value_bias = own_part(6 * width + (units + heads) * g.nt, heads)
-
-    ends = [
-        (end_units(shares[l, "iu"]), end_heads(head_ends[l]))
-        for l in range(layers)
-    ]
 
     def shard(l, kind):
         wide, total = ends[l]
@@ -732,9 +759,6 @@
     )
 
 
-HINT = 1 << 16
-
-
 def solution(mesh):
     rows = P(("dp", "tensor"), None)
     columns = P(None, None, "tensor")

time: 962 us -> 860 us (0.89)
  waiting for transfers between devices: 480 us -> 395 us
    ppermute x91, waiting for transfers between devices: 473 us -> 386 us  [swap(): return lax.ppermute(array, axis, [(i, i ^ bit) for i in range(count)])]
    unnamed x421 -> x407, local copies, waits for them, and re-layouts: 43 us -> 35.7 us
  transfers between devices with their start and end apart: 99 -> 99, of which waited for: 43 -> 41; matrix products, arithmetic and copies ran while one was open for 17% -> 19% of each run, Pallas kernels for 14% -> 14%
where the time goes in v2:
time: 860 us; the launch traced here: 851 us
  waiting for transfers between devices  395 us (46%)
  Pallas kernels  144 us (17%)
  starting transfers between devices  88.7 us (10%)
  local copies, waits for them, and re-layouts  86.9 us (10%)
  other arithmetic  81.4 us (9%)
  matrix products  36.3 us (4%)
  between operations  17.6 us (2%)
    ppermute x91, waiting for transfers between devices, swap(): return lax.ppermute(array, axis, [(i, i ^ bit) for i in range(count)])  386 us
    ppermute x91, starting transfers between devices, swap(): return lax.ppermute(array, axis, [(i, i ^ bit) for i in range(count)])  77.2 us
    pallas_call x24, Pallas kernels, weight_grad(): pl.pallas_call(kernel, grid=(columns // tile,), in_specs=specs, out_specs...  43.5 us
    pallas_call x4, Pallas kernels, streamed(): pl.pallas_call(kernel, in_specs=[whole] * (near_count + extra_count) + [a...  39.5 us
    unnamed x407, local copies, waits for them, and re-layouts  35.7 us
    pallas_call x4, Pallas kernels, attend_back(): pl.pallas_call(partial(attend_back_kernel, halo), grid=(width // LANES,),...  34 us
    pallas_call x4, Pallas kernels, attend(): pl.pallas_call(partial(attend_kernel, halo), grid=(width // LANES,), in_s...  21.7 us
    dot_general x16, matrix products, dot_nn(): lax.dot_general(left, right, (((1,), (0,)), ((), ())), preferred_element_...  20.7 us
  transfers between devices with their start and end apart: 99, of which 41 were waited for; matrix products, arithmetic and copies ran while one was open for 19% of the time, Pallas kernels for 14%

profile of v2, /device:TPU:0, one launch (start us, length us, event | category | flops | bytes accessed | tf_op | source)
XLA Modules:
  0.0 850.6 jit_solution(15452239500367768380)
XLA Ops:
  37.2 8.3 collective-permute-done.3
  59.8 10.1 %collective-permute-done.1 = bf16[256,1024]{1,0:T(8,128)(2,1)S(1)} collective-permute-done((bf16[256,1024]{1,0:T(8,128)(2,1)S(1)}, bf16[256,1024]{1,0:T(8,128)(2,1)S(1)}, u32[]{:S(2)}, u32[]{:S(2)}) %collective-permute-start.1) | collective-permute-done | bytes 524320 | tf_op jit(solution)/shard_map/ppermute | solution.py:315
  73.4 16.9 %collective-permute-done.8 = bf16[2,256,1024]{2,1,0:T(8,128)(2,1)} collective-permute-done((bf16[2,256,1024]{2,1,0:T(8,128)(2,1)}, bf16[2,256,1024]{2,1,0:T(8,128)(2,1)}, u32[]{:S(2)}, u32[]{:S(2)}) %collective-permute-start.8) | collective-permute-done | bytes 1048608 | tf_op jit(solution)/shard_map/ppermute | solution.py:315
  99.9 8.8 %collective-permute-done.11 = bf16[128,1024]{1,0:T(8,128)(2,1)S(1)} collective-permute-done((bf16[128,1024]{1,0:T(8,128)(2,1)S(1)}, bf16[128,1024]{1,0:T(8,128)(2,1)S(1)}, u32[]{:S(2)}, u32[]{:S(2)}) %collective-permute-start.11) | collective-permute-done | bytes 262176 | tf_op jit(solution)/shard_map/ppermute | solution.py:315
  119.2 17.8 %collective-permute-done.12 = bf16[256,1024]{1,0:T(8,128)(2,1)S(1)} collective-permute-done((bf16[256,1024]{1,0:T(8,128)(2,1)S(1)}, bf16[256,1024]{1,0:T(8,128)(2,1)S(1)}, u32[]{:S(2)}, u32[]{:S(2)}) %collective-permute-start.12) | collective-permute-done | bytes 524320 | tf_op jit(solution)/shard_map/ppermute | solution.py:315
  140.7 38.2 %collective-permute-done.15 = bf16[512,1024]{1,0:T(8,128)(2,1)S(1)} collective-permute-done((bf16[512,1024]{1,0:T(8,128)(2,1)S(1)}, bf16[512,1024]{1,0:T(8,128)(2,1)S(1)}, u32[]{:S(2)}, u32[]{:S(2)}) %collective-permute-start.15) | collective-permute-done | bytes 1048608 | tf_op jit(solution)/shard_map/ppermute | solution.py:315
  180.2 14.4 %collective-permute-done.13 = bf16[512,1024]{1,0:T(8,128)(2,1)S(1)} collective-permute-done((bf16[512,1024]{1,0:T(8,128)(2,1)S(1)}, bf16[512,1024]{1,0:T(8,128)(2,1)S(1)}, u32[]{:S(2)}, u32[]{:S(2)}) %collective-permute-start.13) | collective-permute-done | bytes 1048608 | tf_op jit(solution)/shard_map/ppermute | solution.py:315
  207.1 6.5 attend.4.refs_0_
  219.9 6.3 attend.5.refs_0_
  228.8 33.5 %collective-permute-done.17.refs_7_.refs_6_ = bf16[1024,1024]{1,0:T(8,128)(2,1)} collective-permute-done((bf16[1024,1024]{1,0:T(8,128)(2,1)}, bf16[1024,1024]{1,0:T(8,128)(2,1)}, u32[]{:S(2)}, u32[]{:S(2)}) %collective-permute-start.17) | collective-permute-done | bytes 2097184 | tf_op jit(solution)/shard_map/ppermute | solution.py:315
  272.5 10.4 %feed_forward.2 = (f32[256,1024]{1,0:T(8,128)S(1)}, bf16[256,1024]{1,0:T(8,128)(2,1)S(1)}, bf16[256,1024]{1,0:T(8,128)(2,1)S(1)}, bf16[256,1024]{1,0:T(8,128)(2,...) custom-call(bf16[256,1024]{1,0:T(8,128)(2,1)S(1)} %get-tuple-element, ...), custom_call_target="tpu_custom_call" | custom-call | bytes 13000000 | tf_op jit(solution)/shard_map/feed_forward/pallas_call | solution.py:185
  286.5 31.9 %collective-permute-done.10.refs_3_.refs_10_ = bf16[1024,1024]{1,0:T(8,128)(2,1)S(1)} collective-permute-done((bf16[1024,1024]{1,0:T(8,128)(2,1)S(1)}, bf16[1024,1024]{1,0:T(8,128)(2,1)S(1)}, u32[]{:S(2)}, u32[]{:S(2)}) %collective-permute-start.10) | collective-permute-done | bytes 2097184 | tf_op jit(solution)/shard_map/ppermute | solution.py:315
  329.8 9.6 %collective-permute-done.28 = bf16[128,1024]{1,0:T(8,128)(2,1)S(1)} collective-permute-done((bf16[128,1024]{1,0:T(8,128)(2,1)S(1)}, bf16[128,1024]{1,0:T(8,128)(2,1)S(1)}, u32[]{:S(2)}, u32[]{:S(2)}) %collective-permute-start.28) | collective-permute-done | bytes 262176 | tf_op jit(solution)/shard_map/ppermute | solution.py:330
  371.3 10.0 %feed_forward.3 = (f32[256,1024]{1,0:T(8,128)S(1)}, bf16[256,1024]{1,0:T(8,128)(2,1)S(1)}, bf16[256,1024]{1,0:T(8,128)(2,1)S(1)}, bf16[256,1024]{1,0:T(8,128)(2,...) custom-call(bf16[256,1024]{1,0:T(8,128)(2,1)S(1)} %get-tuple-element, ...), custom_call_target="tpu_custom_call" | custom-call | bytes 13000000 | tf_op jit(solution)/shard_map/feed_forward/pallas_call | solution.py:185
  395.0 9.4 %feed_forward_back.2 = (f32[256,1024]{1,0:T(8,128)S(1)}, f32[4,1024]{1,0:T(4,128)S(1)}, bf16[256,1024]{1,0:T(8,128)(2,1)S(1)}, bf16[256,1024]{1,0:T(8,128)(2,1)S...) custom-call(bf16[256,1024]{1,0:T(8,128)(2,1)S(1)} %convert_element_type.363.refs_1_.refs_0_, ...), custom_call_target="tpu_custom_call" | custom-call | bytes 13000000 | tf_op jit(solution)/shard_map/feed_forward_back/pallas_call | solution.py:185
  422.7 7.0 attend_back.4
  431.0 22.4 %collective-permute-done.42 = bf16[1024,1024]{1,0:T(8,128)(2,1)} collective-permute-done((bf16[1024,1024]{1,0:T(8,128)(2,1)S(1)}, bf16[1024,1024]{1,0:T(8,128)(2,1)}, u32[]{:S(2)}, u32[]{:S(2)}) %collective-permute-start.42) | collective-permute-done | bytes 2097184 | tf_op jit(solution)/shard_map/ppermute | solution.py:315
  457.4 6.8 attend_back.5
  519.0 7.6 collective-permute-done.49
  541.4 9.8 %feed_forward_back.3 = (f32[256,1024]{1,0:T(8,128)S(1)}, f32[4,1024]{1,0:T(4,128)S(1)}, bf16[256,1024]{1,0:T(8,128)(2,1)S(1)}, bf16[256,1024]{1,0:T(8,128)(2,1)S...) custom-call(bf16[256,1024]{1,0:T(8,128)(2,1)S(1)} %convert_element_type.372.refs_1_.refs_0_, ...), custom_call_target="tpu_custom_call" | custom-call | bytes 13000000 | tf_op jit(solution)/shard_map/feed_forward_back/pallas_call | solution.py:185
  577.8 10.1 %attend_back.6 = (bf16[256,512]{1,0:T(8,128)(2,1)S(1)}, bf16[1024,512]{1,0:T(8,128)(2,1)S(1)}, bf16[1024,512]{1,0:T(8,128)(2,1)S(1)}) custom-call(s32[256,1]{1,0:T(8,128)S(1)} %copy.125.seg_q_ref, s32[1,1024]{1,0:T(1,128)S(1)} %bitcast.291, bf16[256,512]{1,0:T(8,128)(2,1)S(1)} %copy-done.63, bf16[1024,512]{1,0:T(8,128)(2,1)S(1)} %copy-done.34, ...), custom_call_target="tpu_custom_call" | custom-call | bytes 13000000 | tf_op jit(solution)/shard_map/attend_back/pallas_call | solution.py:110
  591.4 11.6 %collective-permute-done.53 = bf16[1024,1024]{1,0:T(8,128)(2,1)} collective-permute-done((bf16[1024,1024]{1,0:T(8,128)(2,1)}, bf16[1024,1024]{1,0:T(8,128)(2,1)}, u32[]{:S(2)}, u32[]{:S(2)}) %collective-permute-start.53) | collective-permute-done | bytes 2097184 | tf_op jit(solution)/shard_map/ppermute | solution.py:315
  607.9 10.1 %attend_back.7 = (bf16[256,512]{1,0:T(8,128)(2,1)S(1)}, bf16[1024,512]{1,0:T(8,128)(2,1)S(1)}, bf16[1024,512]{1,0:T(8,128)(2,1)S(1)}) custom-call(s32[256,1]{1,0:T(8,128)S(1)} %copy.125.seg_q_ref, s32[1,1024]{1,0:T(1,128)S(1)} %bitcast.292, bf16[256,512]{1,0:T(8,128)(2,1)S(1)} %copy-done.61, bf16[1024,512]{1,0:T(8,128)(2,1)S(1)} %copy-done.30, ...), custom_call_target="tpu_custom_call" | custom-call | bytes 13000000 | tf_op jit(solution)/shard_map/attend_back/pallas_call | solution.py:110
  618.1 28.9 %collective-permute-done.63 = bf16[1024,1024]{1,0:T(8,128)(2,1)} collective-permute-done((bf16[1024,1024]{1,0:T(8,128)(2,1)}, bf16[1024,1024]{1,0:T(8,128)(2,1)}, u32[]{:S(2)}, u32[]{:S(2)}) %collective-permute-start.63) | collective-permute-done | bytes 2097184 | tf_op jit(solution)/shard_map/ppermute | solution.py:315
  674.7 5.4 collective-permute-done.62
  682.4 8.3 collective-permute-done.61
  703.8 8.2 collective-permute-done.69
  718.0 31.4 %collective-permute-done.67 = bf16[2,64,1024]{2,1,0:T(8,128)(2,1)S(1)} collective-permute-done((bf16[2,64,1024]{2,1,0:T(8,128)(2,1)S(1)}, bf16[2,64,1024]{2,1,0:T(8,128)(2,1)S(1)}, u32[]{:S(2)}, u32[]{:S(2)}) %collective-permute-start.67) | collective-permute-done | bytes 262176 | tf_op jit(solution)/shard_map/ppermute | solution.py:315
  790.0 8.8 %collective-permute-done.85 = bf16[1,64,1024]{2,1,0:T(8,128)(2,1)S(1)} collective-permute-done((bf16[1,64,1024]{2,1,0:T(8,128)(2,1)S(1)}, bf16[1,64,1024]{2,1,0:T(8,128)(2,1)S(1)}, u32[]{:S(2)}, u32[]{:S(2)}) %collective-permute-start.85) | collective-permute-done | bytes 131104 | tf_op jit(solution)/shard_map/ppermute | solution.py:315
  807.1 10.3 %collective-permute-done.90 = bf16[256,1024]{1,0:T(8,128)(2,1)S(1)} collective-permute-done((bf16[256,1024]{1,0:T(8,128)(2,1)S(1)}, bf16[256,1024]{1,0:T(8,128)(2,1)S(1)}, u32[]{:S(2)}, u32[]{:S(2)}) %collective-permute-start.90) | collective-permute-done | bytes 524320 | tf_op jit(solution)/shard_map/ppermute | solution.py:315
  817.6 9.4 %collective-permute-done.89 = bf16[1,256,1024]{2,1,0:T(8,128)(2,1)S(1)} collective-permute-done((bf16[1,256,1024]{2,1,0:T(8,128)(2,1)S(1)}, bf16[1,256,1024]{2,1,0:T(8,128)(2,1)S(1)}, u32[]{:S(2)}, u32[]{:S(2)}) %collective-permute-start.89) | collective-permute-done | bytes 524320 | tf_op jit(solution)/shard_map/ppermute | solution.py:315
  838.4 5.5 gradients_out.1
  (888 shorter events, 399.4 us)
Async XLA Ops:
  7.2 258.3 %all-gather.5.cloned.1.call-start = ((), (), s32[]{:S(2)}) async-start(), calls=%async_computation.4 | async-start | bytes 4718592 | tf_op jit(solution)/shard_map/all_gather | solution.py:515
  11.5 43.5 %collective-permute-start.7 = (bf16[1,256,1024]{2,1,0:T(8,128)(2,1)S(1)}, bf16[1,256,1024]{2,1,0:T(8,128)(2,1)}, u32[]{:S(2)}, u32[]{:S(2)}) collective-permute-start(bf16[1,256,1024]{2,1,0:T(8,128)(2,1)S(1)} %bitcast.305), channel_id=1, source_target_pairs={{0,4},{1,5},{2,6},{3,7},{4,0},{5,1},{6,2},{7,3},{8,12},{9,13},{10,... | collective-permute-start | bytes 1572872 | tf_op jit(solution)/shard_map/ppermute | solution.py:315
  15.6 29.9 %collective-permute-start.3 = (f32[1,2,768]{2,1,0:T(2,128)S(1)}, f32[1,2,768]{2,1,0:T(2,128)S(1)}, u32[]{:S(2)}, u32[]{:S(2)}) collective-permute-start(f32[1,2,768]{2,1,0:T(2,128)S(1)} %maximum_bitcast_fusion.3), channel_id=1, source_target_pairs={{0,4},{1,5},{2,6},{3,7},{4,0},{5,1},{6,2},{7,3},{8,12},{9,13},{10,... | collective-permute-start | bytes 18440 | tf_op jit(solution)/shard_map/ppermute | solution.py:315
  21.7 33.2 %collective-permute-start = (bf16[128,1024]{1,0:T(8,128)(2,1)S(1)}, bf16[128,1024]{1,0:T(8,128)(2,1)S(1)}, u32[]{:S(2)}, u32[]{:S(2)}) collective-permute-start(bf16[128,1024]{1,0:T(8,128)(2,1)S(1)} %dynamic-slice_bitcast_fusion.1), channel_id=1, source_target_pairs={{0,4},{1,5},{2,6},{3,7},{4,0},{5,1},{6,2},{7,3},{8,12},{9,13},{10,... | collective-permute-start | bytes 786440 | tf_op jit(solution)/shard_map/ppermute | solution.py:315
  24.6 71.2 %collective-permute-start.6 = (bf16[256,1024]{1,0:T(8,128)(2,1)S(1)}, bf16[256,1024]{1,0:T(8,128)(2,1)}, u32[]{:S(2)}, u32[]{:S(2)}) collective-permute-start(bf16[256,1024]{1,0:T(8,128)(2,1)S(1)} %copy-done.113), channel_id=1, source_target_pairs={{0,1},{1,0},{2,3},{3,2},{4,5},{5,4},{6,7},{7,6},{8,9},{9,8},{10,11... | collective-permute-start | bytes 1572872 | tf_op jit(solution)/shard_map/ppermute | solution.py:315
  57.2 33.1 %collective-permute-start.8 = (bf16[2,256,1024]{2,1,0:T(8,128)(2,1)}, bf16[2,256,1024]{2,1,0:T(8,128)(2,1)}, u32[]{:S(2)}, u32[]{:S(2)}) collective-permute-start(bf16[2,256,1024]{2,1,0:T(8,128)(2,1)} %pad_maximum_fusion.9), channel_id=1, source_target_pairs={{0,2},{1,3},{2,0},{3,1},{4,6},{5,7},{6,4},{7,5},{8,10},{9,11},{10,... | collective-permute-start | bytes 3145736 | tf_op jit(solution)/shard_map/ppermute | solution.py:315
  95.9 223.9 %all-gather.7.cloned.1.call-start = ((), (), s32[]{:S(2)}) async-start(), calls=%async_computation.5 | async-start | bytes 4718592 | tf_op jit(solution)/shard_map/all_gather | solution.py:528
  98.4 97.8 %collective-permute-start.16 = (bf16[4,256,1024]{2,1,0:T(8,128)(2,1)}, bf16[4,256,1024]{2,1,0:T(8,128)(2,1)}, u32[]{:S(2)}, u32[]{:S(2)}) collective-permute-start(bf16[4,256,1024]{2,1,0:T(8,128)(2,1)} %pad_maximum_fusion.3), channel_id=1, source_target_pairs={{0,1},{1,0},{2,3},{3,2},{4,5},{5,4},{6,7},{7,6},{8,9},{9,8},{10,11... | collective-permute-start | bytes 6291464 | tf_op jit(solution)/shard_map/ppermute | solution.py:315
  118.2 60.8 %collective-permute-start.15 = (bf16[512,1024]{1,0:T(8,128)(2,1)S(1)}, bf16[512,1024]{1,0:T(8,128)(2,1)S(1)}, u32[]{:S(2)}, u32[]{:S(2)}) collective-permute-start(bf16[512,1024]{1,0:T(8,128)(2,1)S(1)} %pad_maximum_fusion.11), channel_id=1, source_target_pairs={{0,2},{1,3},{2,0},{3,1},{4,6},{5,7},{6,4},{7,5},{8,10},{9,11},{10,... | collective-permute-start | bytes 3145736 | tf_op jit(solution)/shard_map/ppermute | solution.py:315
  118.2 82.9 %collective-permute-start.14 = (bf16[1024,1024]{1,0:T(8,128)(2,1)}, bf16[1024,1024]{1,0:T(8,128)(2,1)}, u32[]{:S(2)}, u32[]{:S(2)}) collective-permute-start(bf16[1024,1024]{1,0:T(8,128)(2,1)} %pad_maximum_fusion.2.refs_2_.refs_9_), channel_id=1, source_target_pairs={{0,16},{8,24},{16,0},{24,8},{1,17},{9,25},{17,1},{25,9},{2,18},{10... | collective-permute-start | bytes 6291464 | tf_op jit(solution)/shard_map/ppermute | solution.py:315
  137.1 57.6 %collective-permute-start.13 = (bf16[512,1024]{1,0:T(8,128)(2,1)S(1)}, bf16[512,1024]{1,0:T(8,128)(2,1)S(1)}, u32[]{:S(2)}, u32[]{:S(2)}) collective-permute-start(bf16[512,1024]{1,0:T(8,128)(2,1)S(1)} %pad_maximum_fusion.10), channel_id=1, source_target_pairs={{0,1},{1,0},{2,3},{3,2},{4,5},{5,4},{6,7},{7,6},{8,9},{9,8},{10,11... | collective-permute-start | bytes 3145736 | tf_op jit(solution)/shard_map/ppermute | solution.py:315
  201.2 550.9 %reduce-scatter.3.cloned.1.call-start = ((), (), s32[]{:S(2)}) async-start(), calls=%async_computation.2 | async-start | bytes 4718592 | tf_op jit(solution)/shard_map/reduce_scatter | solution.py:671
  214.1 48.2 %collective-permute-start.17 = (bf16[1024,1024]{1,0:T(8,128)(2,1)}, bf16[1024,1024]{1,0:T(8,128)(2,1)}, u32[]{:S(2)}, u32[]{:S(2)}) collective-permute-start(bf16[1024,1024]{1,0:T(8,128)(2,1)} %pad_maximum_fusion.4.refs_6_.refs_5_), channel_id=1, source_target_pairs={{0,16},{8,24},{16,0},{24,8},{1,17},{9,25},{17,1},{25,9},{2,18},{10... | collective-permute-start | bytes 6291464 | tf_op jit(solution)/shard_map/ppermute | solution.py:315
  215.6 46.7 %collective-permute-start.18 = (bf16[1024,1024]{1,0:T(8,128)(2,1)}, bf16[1024,1024]{1,0:T(8,128)(2,1)S(1)}, u32[]{:S(2)}, u32[]{:S(2)}) collective-permute-start(bf16[1024,1024]{1,0:T(8,128)(2,1)} %pad_maximum_fusion.2.refs_2_.refs_9_), channel_id=1, source_target_pairs={{0,8},{8,0},{16,24},{24,16},{1,9},{9,1},{17,25},{25,17},{2,10},{10... | collective-permute-start | bytes 6291464 | tf_op jit(solution)/shard_map/ppermute | solution.py:315
  215.7 48.0 %collective-permute-start.19 = (bf16[1024,1024]{1,0:T(8,128)(2,1)}, bf16[1024,1024]{1,0:T(8,128)(2,1)S(1)}, u32[]{:S(2)}, u32[]{:S(2)}) collective-permute-start(bf16[1024,1024]{1,0:T(8,128)(2,1)} %collective-permute-done.14.refs_3_.refs_10_), channel_id=1, source_target_pairs={{0,8},{8,0},{16,24},{24,16},{1,9},{9,1},{17,25},{25,17},{2,10},{10... | collective-permute-start | bytes 6291464 | tf_op jit(solution)/shard_map/ppermute | solution.py:315
  269.9 48.6 %collective-permute-start.10 = (bf16[1024,1024]{1,0:T(8,128)(2,1)S(1)}, bf16[1024,1024]{1,0:T(8,128)(2,1)S(1)}, u32[]{:S(2)}, u32[]{:S(2)}) collective-permute-start(bf16[1024,1024]{1,0:T(8,128)(2,1)S(1)} %bitcast.263), channel_id=1, source_target_pairs={{0,16},{8,24},{16,0},{24,8},{1,17},{9,25},{17,1},{25,9},{2,18},{10... | collective-permute-start | bytes 6291464 | tf_op jit(solution)/shard_map/ppermute | solution.py:315
  285.0 77.5 %collective-permute-start.9 = (bf16[1024,1024]{1,0:T(8,128)(2,1)}, bf16[1024,1024]{1,0:T(8,128)(2,1)}, u32[]{:S(2)}, u32[]{:S(2)}) collective-permute-start(bf16[1024,1024]{1,0:T(8,128)(2,1)} %bitcast.43.refs_6_.refs_5_), channel_id=1, source_target_pairs={{0,16},{8,24},{16,0},{24,8},{1,17},{9,25},{17,1},{25,9},{2,18},{10... | collective-permute-start | bytes 6291464 | tf_op jit(solution)/shard_map/ppermute | solution.py:315
  405.6 47.8 %collective-permute-start.42 = (bf16[1024,1024]{1,0:T(8,128)(2,1)S(1)}, bf16[1024,1024]{1,0:T(8,128)(2,1)}, u32[]{:S(2)}, u32[]{:S(2)}) collective-permute-start(bf16[1024,1024]{1,0:T(8,128)(2,1)S(1)} %weight_grad.25), channel_id=1, source_target_pairs={{0,16},{8,24},{16,0},{24,8},{1,17},{9,25},{17,1},{25,9},{2,18},{10... | collective-permute-start | bytes 6291464 | tf_op jit(solution)/shard_map/ppermute | solution.py:315
  473.8 285.6 %reduce-scatter.5.cloned.1.call-start = ((), (), s32[]{:S(2)}) async-start(), calls=%async_computation.3 | async-start | bytes 4718592 | tf_op jit(solution)/shard_map/reduce_scatter | solution.py:618
  473.9 88.0 %collective-permute-start.51 = (bf16[256,1024]{1,0:T(8,128)(2,1)S(1)}, bf16[256,1024]{1,0:T(8,128)(2,1)}, u32[]{:S(2)}, u32[]{:S(2)}) collective-permute-start(bf16[256,1024]{1,0:T(8,128)(2,1)S(1)} %get-tuple-element.217.refs_0_.refs_1_), channel_id=1, source_target_pairs={{0,8},{8,0},{16,24},{24,16},{1,9},{9,1},{17,25},{25,17},{2,10},{10... | collective-permute-start | bytes 1572872 | tf_op jit(solution)/shard_map/ppermute | solution.py:315
  474.1 57.1 %collective-permute-start.48 = (bf16[256,1024]{1,0:T(8,128)(2,1)}, bf16[256,1024]{1,0:T(8,128)(2,1)}, u32[]{:S(2)}, u32[]{:S(2)}) collective-permute-start(bf16[256,1024]{1,0:T(8,128)(2,1)} %copy-done.91), channel_id=1, source_target_pairs={{0,8},{8,0},{16,24},{24,16},{1,9},{9,1},{17,25},{25,17},{2,10},{10... | collective-permute-start | bytes 1572872 | tf_op jit(solution)/shard_map/ppermute | solution.py:315
  478.6 48.1 %collective-permute-start.49 = (bf16[1024,1024]{1,0:T(8,128)(2,1)}, bf16[1024,1024]{1,0:T(8,128)(2,1)}, u32[]{:S(2)}, u32[]{:S(2)}) collective-permute-start(bf16[1024,1024]{1,0:T(8,128)(2,1)} %copy-done.49), channel_id=1, source_target_pairs={{0,16},{8,24},{16,0},{24,8},{1,17},{9,25},{17,1},{25,9},{2,18},{10... | collective-permute-start | bytes 6291464 | tf_op jit(solution)/shard_map/ppermute | solution.py:315
  554.2 48.8 %collective-permute-start.53 = (bf16[1024,1024]{1,0:T(8,128)(2,1)}, bf16[1024,1024]{1,0:T(8,128)(2,1)}, u32[]{:S(2)}, u32[]{:S(2)}) collective-permute-start(bf16[1024,1024]{1,0:T(8,128)(2,1)} %weight_grad.31), channel_id=1, source_target_pairs={{0,16},{8,24},{16,0},{24,8},{1,17},{9,25},{17,1},{25,9},{2,18},{10... | collective-permute-start | bytes 6291464 | tf_op jit(solution)/shard_map/ppermute | solution.py:315
  571.1 75.9 %collective-permute-start.63 = (bf16[1024,1024]{1,0:T(8,128)(2,1)}, bf16[1024,1024]{1,0:T(8,128)(2,1)}, u32[]{:S(2)}, u32[]{:S(2)}) collective-permute-start(bf16[1024,1024]{1,0:T(8,128)(2,1)} %weight_grad.33), channel_id=1, source_target_pairs={{0,16},{8,24},{16,0},{24,8},{1,17},{9,25},{17,1},{25,9},{2,18},{10... | collective-permute-start | bytes 6291464 | tf_op jit(solution)/shard_map/ppermute | solution.py:315
  605.7 48.1 %collective-permute-start.55 = (bf16[4,128,1024]{2,1,0:T(8,128)(2,1)S(1)}, bf16[4,128,1024]{2,1,0:T(8,128)(2,1)S(1)}, u32[]{:S(2)}, u32[]{:S(2)}) collective-permute-start(bf16[4,128,1024]{2,1,0:T(8,128)(2,1)S(1)} %split.126), channel_id=1, source_target_pairs={{0,1},{1,0},{2,3},{3,2},{4,5},{5,4},{6,7},{7,6},{8,9},{9,8},{10,11... | collective-permute-start | bytes 3145736 | tf_op jit(solution)/shard_map/ppermute | solution.py:315
  607.5 45.3 %collective-permute-start.56 = (bf16[4,64,1024]{2,1,0:T(8,128)(2,1)S(1)}, bf16[4,64,1024]{2,1,0:T(8,128)(2,1)S(1)}, u32[]{:S(2)}, u32[]{:S(2)}) collective-permute-start(bf16[4,64,1024]{2,1,0:T(8,128)(2,1)S(1)} %split.128), channel_id=1, source_target_pairs={{0,1},{1,0},{2,3},{3,2},{4,5},{5,4},{6,7},{7,6},{8,9},{9,8},{10,11... | collective-permute-start | bytes 1572872 | tf_op jit(solution)/shard_map/ppermute | solution.py:315
  651.2 39.8 %collective-permute-start.64 = (bf16[4,128,1024]{2,1,0:T(8,128)(2,1)}, bf16[4,128,1024]{2,1,0:T(8,128)(2,1)}, u32[]{:S(2)}, u32[]{:S(2)}) collective-permute-start(bf16[4,128,1024]{2,1,0:T(8,128)(2,1)} %bitcast.93), channel_id=1, source_target_pairs={{0,1},{1,0},{2,3},{3,2},{4,5},{5,4},{6,7},{7,6},{8,9},{9,8},{10,11... | collective-permute-start | bytes 3145736 | tf_op jit(solution)/shard_map/ppermute | solution.py:315
  699.6 52.1 %collective-permute-start.72 = (bf16[512,1024]{1,0:T(8,128)(2,1)S(1)}, bf16[512,1024]{1,0:T(8,128)(2,1)S(1)}, u32[]{:S(2)}, u32[]{:S(2)}) collective-permute-start(bf16[512,1024]{1,0:T(8,128)(2,1)S(1)} %split.152), channel_id=1, source_target_pairs={{0,2},{1,3},{2,0},{3,1},{4,6},{5,7},{6,4},{7,5},{8,10},{9,11},{10,... | collective-permute-start | bytes 3145736 | tf_op jit(solution)/shard_map/ppermute | solution.py:315
  700.8 48.6 %collective-permute-start.70 = (bf16[2,128,1024]{2,1,0:T(8,128)(2,1)S(1)}, bf16[2,128,1024]{2,1,0:T(8,128)(2,1)S(1)}, u32[]{:S(2)}, u32[]{:S(2)}) collective-permute-start(bf16[2,128,1024]{2,1,0:T(8,128)(2,1)S(1)} %split.150), channel_id=1, source_target_pairs={{0,2},{1,3},{2,0},{3,1},{4,6},{5,7},{6,4},{7,5},{8,10},{9,11},{10,... | collective-permute-start | bytes 1572872 | tf_op jit(solution)/shard_map/ppermute | solution.py:315
  701.9 47.5 %collective-permute-start.67 = (bf16[2,64,1024]{2,1,0:T(8,128)(2,1)S(1)}, bf16[2,64,1024]{2,1,0:T(8,128)(2,1)S(1)}, u32[]{:S(2)}, u32[]{:S(2)}) collective-permute-start(bf16[2,64,1024]{2,1,0:T(8,128)(2,1)S(1)} %split.144), channel_id=1, source_target_pairs={{0,2},{1,3},{2,0},{3,1},{4,6},{5,7},{6,4},{7,5},{8,10},{9,11},{10,... | collective-permute-start | bytes 786440 | tf_op jit(solution)/shard_map/ppermute | solution.py:315
  712.0 38.5 %collective-permute-start.66 = (bf16[4,64,1024]{2,1,0:T(8,128)(2,1)S(1)}, bf16[4,64,1024]{2,1,0:T(8,128)(2,1)S(1)}, u32[]{:S(2)}, u32[]{:S(2)}) collective-permute-start(bf16[4,64,1024]{2,1,0:T(8,128)(2,1)S(1)} %split.142), channel_id=1, source_target_pairs={{0,1},{1,0},{2,3},{3,2},{4,5},{5,4},{6,7},{7,6},{8,9},{9,8},{10,11... | collective-permute-start | bytes 1572872 | tf_op jit(solution)/shard_map/ppermute | solution.py:315
  716.7 34.8 %collective-permute-start.65 = (bf16[4,64,1024]{2,1,0:T(8,128)(2,1)S(1)}, bf16[4,64,1024]{2,1,0:T(8,128)(2,1)S(1)}, u32[]{:S(2)}, u32[]{:S(2)}) collective-permute-start(bf16[4,64,1024]{2,1,0:T(8,128)(2,1)S(1)} %split.140), channel_id=1, source_target_pairs={{0,1},{1,0},{2,3},{3,2},{4,5},{5,4},{6,7},{7,6},{8,9},{9,8},{10,11... | collective-permute-start | bytes 1572872 | tf_op jit(solution)/shard_map/ppermute | solution.py:315
  (259 other events, 2485.1 us)
Sparse Core Ops, SparseCore 0:
  96.0 107.7 all-gather.4
  206.6 71.5 all-gather.6
  474.0 92.7 reduce-scatter.2
  574.5 109.8 reduce-scatter.4

commit v3 on v2

--- a/solution.py
+++ b/solution.py
@@ -579,21 +579,32 @@
         keep, give = jnp.split(total, 2)
         return (keep.astype(F32) + g.swap(give, "tensor", bit).astype(F32)).astype(BF)
 
-    def end_over_x(wide, total):
+    def end_over_x(wide, plain, total):
         wide = wide[None]
         for bit in g.bits("x"):
             wide = jnp.concatenate([wide, g.swap(wide, "dp", bit)])
+            if plain is not None:
+                plain = (plain.astype(F32) + g.swap(plain, "dp", bit).astype(F32)).astype(BF)
             total = (total.astype(F32) + g.swap(total, "dp", bit).astype(F32)).astype(BF)
-        return wide, total
-
-    def end_over_core(wide, total):
+        return wide, plain, total
+
+    def end_over_core(wide, plain, total):
         wide = jnp.stack([wide, g.core(wide)], 1)
         wide = g.turned(g.turned(wide, "x", 0), "c", 1)
+        if plain is not None:
+            plain = jnp.stack([plain, g.core(plain)]).reshape(2, g.nx, block, width)
+            plain = g.turned(plain, "c", 0).swapaxes(0, 1)
         if cores == 2:
-            return wide, g.turned(jnp.stack([total, g.core(total)]), "c", 0)
-        return wide, (total.astype(F32) + g.core(total).astype(F32))[None]
-
-    ends, vectors, later_units = [None] * layers, [None] * layers, [None] * layers
+            return wide, plain, g.turned(jnp.stack([total, g.core(total)]), "c", 0)
+        return wide, plain, (total.astype(F32) + g.core(total).astype(F32))[None]
+
+    ends, vectors = [None] * layers, [None] * layers
+    later_sums, later_outer = [None] * layers, [None] * layers
+
+    def over_tensor(arrays):
+        pack = jnp.concatenate(arrays, 1).reshape(-1, width)
+        return lax.psum_scatter(pack, "tensor", scatter_dimension=0, tiled=True)
+
     grad_hidden = cotangent.astype(F32)
     units_before = None
     first_bits = high_to_low[::-1]
@@ -614,11 +625,12 @@
             outer_parts, mixed_low, grad_mixed, units_before
         )
         if units_before is not None:
-            pack = jnp.stack(units_before, 1)
-            later_units[l + 1] = lax.psum_scatter(
-                pack.reshape(-1, width), "tensor", scatter_dimension=0, tiled=True
-            )
-        outer_sum = sum_over_x(outer_parts).reshape(g.nt, block, width)
+            later_sums[l + 1] = over_tensor(units_before)
+        if l:
+            later_outer[l] = over_tensor([a.reshape(g.nt, block, width) for a in outer_parts])
+            outer_sum = None
+        else:
+            outer_sum = sum_over_x(outer_parts).reshape(g.nt, block, width)
         total, d_inner_bias, grad_inner = feed_forward_back(mixed_low, inner_w, outer_w, slopes)
         inner_parts = unit_parts(grad_inner[: g.nx], [g.core(a) for a in grad_inner[g.nx :]], normed_both)
         grad_normed = grad_mixed + total
@@ -667,9 +679,7 @@
         if l:
             far_sum = near_sums(far_part) if reach else far_sums(far_part)
             grad_hidden = near_sum + far_sum
-            pack = jnp.concatenate([*totals, out_total], 1)
-            ends[l] = lax.psum_scatter(pack.reshape(-1, width), "tensor", scatter_dimension=0, tiled=True)
-            units_before = inner_sum, outer_sum
+            units_before = [inner_sum, *totals, out_total]
     steps_done = cores - 1
     vector = jnp.stack(vectors)
     hops = [(axis, 1 << k) for axis, count in (("dp", g.nd), ("tensor", g.nt)) for k in range(count.bit_length() - 1)]
@@ -698,7 +708,8 @@
             far_part = keep.astype(F32) + g.swap(give.astype(BF), "tensor", far_bits.pop(0)).astype(F32)
         if number == 1:
             for l in range(1, layers):
-                ends[l] = end_over_x(later_units[l], ends[l])
+                plain = g.turned(later_outer[l].reshape(-1, block, width), "x", 0).reshape(-1, width)
+                ends[l] = end_over_x(later_sums[l][:block], plain, later_sums[l][block:])
         if number == 2:
             for l in range(1, layers):
                 ends[l] = end_over_core(*ends[l])
@@ -712,8 +723,9 @@
     wide = jnp.concatenate([a.reshape(-1, width) for a in (inner_sum, outer_sum)])
     total = jnp.concatenate([a.reshape(-1, width) for a in (*totals, out_total)])
     vector = next_hop(vector)
-    wide, total, vector = together(*end_over_x(wide, total), vector)
-    ends[0] = end_over_core(wide, total)
+    wide, _, total = end_over_x(wide, None, total)
+    wide, total, vector = together(wide, total, vector)
+    ends[0] = end_over_core(wide, None, total)
     while hops:
         vector = next_hop(vector)
 
@@ -727,8 +739,10 @@
     d_value_bias = own_part(6 * width + (units + heads) * g.nt, heads)
 
     def shard(l, kind):
-        wide, total = ends[l]
-        if kind in "iu":
+        wide, plain, total = ends[l]
+        if kind == "u" and plain is not None:
+            array = plain.reshape(units, width)
+        elif kind in "iu":
             k = "iu".index(kind)
             array = wide[:, :, k * block : (k + 1) * block].reshape(units, width)
         else:

time: 860 us -> 844 us (0.981)
  waiting for transfers between devices: 395 us -> 352 us
  local copies, waits for them, and re-layouts: 86.9 us -> 105 us
  Pallas kernels: 144 us -> 159 us
    ppermute x91 -> x92, waiting for transfers between devices: 386 us -> 329 us  [swap(): return lax.ppermute(array, axis, [(i, i ^ bit) for i in range(count)])]
    ppermute x4, waiting for transfers between devices: 9.58 us -> 23.2 us  [shift(): return lax.ppermute(array, 'tensor', pairs)]
    unnamed x407 -> x449, local copies, waits for them, and re-layouts: 35.7 us -> 47.4 us
    pallas_call x24, Pallas kernels: 43.5 us -> 54.9 us  [weight_grad(): pl.pallas_call(kernel, grid=(columns // tile,), in_specs=specs, out_specs...]
    ppermute x91 -> x92, starting transfers between devices: 77.2 us -> 71.9 us  [swap(): return lax.ppermute(array, axis, [(i, i ^ bit) for i in range(count)])]
  transfers between devices with their start and end apart: 99 -> 100, of which waited for: 41 -> 39; matrix products, arithmetic and copies ran while one was open for 19% -> 21% of each run, Pallas kernels for 14% -> 17%
where the time goes in v3:
time: 844 us; the launch traced here: 833 us
  waiting for transfers between devices  352 us (42%)
  Pallas kernels  159 us (19%)
  local copies, waits for them, and re-layouts  105 us (12%)
  other arithmetic  86.2 us (10%)
  starting transfers between devices  81.8 us (10%)
  matrix products  31.4 us (4%)
  between operations  17.8 us (2%)
    ppermute x92, waiting for transfers between devices, swap(): return lax.ppermute(array, axis, [(i, i ^ bit) for i in range(count)])  329 us
    ppermute x92, starting transfers between devices, swap(): return lax.ppermute(array, axis, [(i, i ^ bit) for i in range(count)])  71.9 us
    pallas_call x24, Pallas kernels, weight_grad(): pl.pallas_call(kernel, grid=(columns // tile,), in_specs=specs, out_specs...  54.9 us
    unnamed x449, local copies, waits for them, and re-layouts  47.4 us
    pallas_call x4, Pallas kernels, streamed(): pl.pallas_call(kernel, in_specs=[whole] * (near_count + extra_count) + [a...  43.1 us
    pallas_call x4, Pallas kernels, attend_back(): pl.pallas_call(partial(attend_back_kernel, halo), grid=(width // LANES,),...  33.8 us
    ppermute x4, waiting for transfers between devices, shift(): return lax.ppermute(array, 'tensor', pairs)  23.2 us
    pallas_call x4, Pallas kernels, attend(): pl.pallas_call(partial(attend_kernel, halo), grid=(width // LANES,), in_s...  21.7 us
  transfers between devices with their start and end apart: 100, of which 39 were waited for; matrix products, arithmetic and copies ran while one was open for 21% of the time, Pallas kernels for 17%

profile of v3, /device:TPU:0, one launch (start us, length us, event | category | flops | bytes accessed | tf_op | source)
XLA Modules:
  0.0 833.4 jit_solution(1359538128231330669)
XLA Ops:
  43.2 10.7 %collective-permute-done.4 = f32[2,2,768]{2,1,0:T(2,128)S(1)} collective-permute-done((f32[2,2,768]{2,1,0:T(2,128)S(1)}, f32[2,2,768]{2,1,0:T(2,128)S(1)}, u32[]{:S(2)}, u32[]{:S(2)}) %collective-permute-start.4) | collective-permute-done | bytes 12320 | tf_op jit(solution)/shard_map/ppermute | solution.py:315
  63.2 10.1 %collective-permute-done.1 = bf16[256,1024]{1,0:T(8,128)(2,1)S(1)} collective-permute-done((bf16[256,1024]{1,0:T(8,128)(2,1)S(1)}, bf16[256,1024]{1,0:T(8,128)(2,1)S(1)}, u32[]{:S(2)}, u32[]{:S(2)}) %collective-permute-start.1) | collective-permute-done | bytes 524320 | tf_op jit(solution)/shard_map/ppermute | solution.py:315
  75.7 12.0 %collective-permute-done.8 = bf16[2,256,1024]{2,1,0:T(8,128)(2,1)} collective-permute-done((bf16[2,256,1024]{2,1,0:T(8,128)(2,1)}, bf16[2,256,1024]{2,1,0:T(8,128)(2,1)}, u32[]{:S(2)}, u32[]{:S(2)}) %collective-permute-start.8) | collective-permute-done | bytes 1048608 | tf_op jit(solution)/shard_map/ppermute | solution.py:315
  95.6 7.5 collective-permute-done.11
  110.8 22.4 %collective-permute-done.12 = bf16[256,1024]{1,0:T(8,128)(2,1)S(1)} collective-permute-done((bf16[256,1024]{1,0:T(8,128)(2,1)S(1)}, bf16[256,1024]{1,0:T(8,128)(2,1)S(1)}, u32[]{:S(2)}, u32[]{:S(2)}) %collective-permute-start.12) | collective-permute-done | bytes 524320 | tf_op jit(solution)/shard_map/ppermute | solution.py:315
  137.7 29.4 %collective-permute-done.15 = bf16[512,1024]{1,0:T(8,128)(2,1)S(1)} collective-permute-done((bf16[512,1024]{1,0:T(8,128)(2,1)S(1)}, bf16[512,1024]{1,0:T(8,128)(2,1)S(1)}, u32[]{:S(2)}, u32[]{:S(2)}) %collective-permute-start.15) | collective-permute-done | bytes 1048608 | tf_op jit(solution)/shard_map/ppermute | solution.py:315
  168.4 16.6 %collective-permute-done.13 = bf16[512,1024]{1,0:T(8,128)(2,1)S(1)} collective-permute-done((bf16[512,1024]{1,0:T(8,128)(2,1)S(1)}, bf16[512,1024]{1,0:T(8,128)(2,1)S(1)}, u32[]{:S(2)}, u32[]{:S(2)}) %collective-permute-start.13) | collective-permute-done | bytes 1048608 | tf_op jit(solution)/shard_map/ppermute | solution.py:315
  200.1 6.5 attend.4.refs_0_
  211.2 6.3 attend.5.refs_0_
  231.0 11.5 %feed_forward.2 = (f32[256,1024]{1,0:T(8,128)S(1)}, bf16[256,1024]{1,0:T(8,128)(2,1)S(1)}, bf16[256,1024]{1,0:T(8,128)(2,1)S(1)}, bf16[256,1024]{1,0:T(8,128)(2,...) custom-call(bf16[256,1024]{1,0:T(8,128)(2,1)} %get-tuple-element.219, ...), custom_call_target="tpu_custom_call" | custom-call | bytes 13000000 | tf_op jit(solution)/shard_map/feed_forward/pallas_call | solution.py:185
  246.1 30.2 %collective-permute-done.10.refs_3_.refs_10_ = bf16[1024,1024]{1,0:T(8,128)(2,1)S(1)} collective-permute-done((bf16[1024,1024]{1,0:T(8,128)(2,1)S(1)}, bf16[1024,1024]{1,0:T(8,128)(2,1)S(1)}, u32[]{:S(2)}, u32[]{:S(2)}) %collective-permute-start.10) | collective-permute-done | bytes 2097184 | tf_op jit(solution)/shard_map/ppermute | solution.py:315
  313.2 7.3 collective-permute-done.9.refs_7_.refs_6_
  329.2 11.0 %feed_forward.3 = (f32[256,1024]{1,0:T(8,128)S(1)}, bf16[256,1024]{1,0:T(8,128)(2,1)S(1)}, bf16[256,1024]{1,0:T(8,128)(2,1)S(1)}, bf16[256,1024]{1,0:T(8,128)(2,...) custom-call(bf16[256,1024]{1,0:T(8,128)(2,1)} %get-tuple-element.235, ...), custom_call_target="tpu_custom_call" | custom-call | bytes 13000000 | tf_op jit(solution)/shard_map/feed_forward/pallas_call | solution.py:185
  354.8 9.9 %feed_forward_back.2 = (f32[256,1024]{1,0:T(8,128)S(1)}, f32[4,1024]{1,0:T(4,128)S(1)}, bf16[256,1024]{1,0:T(8,128)(2,1)S(1)}, bf16[256,1024]{1,0:T(8,128)(2,1)S...) custom-call(bf16[256,1024]{1,0:T(8,128)(2,1)S(1)} %convert_element_type.363.refs_1_.refs_0_, ...), custom_call_target="tpu_custom_call" | custom-call | bytes 13000000 | tf_op jit(solution)/shard_map/feed_forward_back/pallas_call | solution.py:185
  391.8 6.8 attend_back.4
  405.8 6.8 attend_back.5
  421.0 14.1 %collective-permute-done.44 = bf16[128,1024]{1,0:T(8,128)(2,1)S(1)} collective-permute-done((bf16[128,1024]{1,0:T(8,128)(2,1)S(1)}, bf16[128,1024]{1,0:T(8,128)(2,1)S(1)}, u32[]{:S(2)}, u32[]{:S(2)}) %collective-permute-start.44) | collective-permute-done | bytes 262176 | tf_op jit(solution)/shard_map/ppermute | solution.py:330
  477.1 10.7 %feed_forward_back.3 = (f32[256,1024]{1,0:T(8,128)S(1)}, f32[4,1024]{1,0:T(4,128)S(1)}, bf16[256,1024]{1,0:T(8,128)(2,1)S(1)}, bf16[256,1024]{1,0:T(8,128)(2,1)S...) custom-call(bf16[256,1024]{1,0:T(8,128)(2,1)} %convert_element_type.369.refs_1_.refs_0_, ...), custom_call_target="tpu_custom_call" | custom-call | bytes 13000000 | tf_op jit(solution)/shard_map/feed_forward_back/pallas_call | solution.py:185
  514.5 10.1 %attend_back.6 = (bf16[256,512]{1,0:T(8,128)(2,1)S(1)}, bf16[1024,512]{1,0:T(8,128)(2,1)S(1)}, bf16[1024,512]{1,0:T(8,128)(2,1)S(1)}) custom-call(s32[256,1]{1,0:T(8,128)S(1)} %copy.122.seg_q_ref, s32[1,1024]{1,0:T(1,128)S(1)} %bitcast.298, bf16[256,512]{1,0:T(8,128)(2,1)S(1)} %copy-done.81, bf16[1024,512]{1,0:T(8,128)(2,1)S(1)} %copy-done.40, ...), custom_call_target="tpu_custom_call" | custom-call | bytes 13000000 | tf_op jit(solution)/shard_map/attend_back/pallas_call | solution.py:110
  531.8 6.9 collective-permute-done.55
  545.5 10.1 %attend_back.7 = (bf16[256,512]{1,0:T(8,128)(2,1)S(1)}, bf16[1024,512]{1,0:T(8,128)(2,1)S(1)}, bf16[1024,512]{1,0:T(8,128)(2,1)S(1)}) custom-call(s32[256,1]{1,0:T(8,128)S(1)} %copy.122.seg_q_ref, s32[1,1024]{1,0:T(1,128)S(1)} %bitcast.299, bf16[256,512]{1,0:T(8,128)(2,1)S(1)} %copy-done.79, bf16[1024,512]{1,0:T(8,128)(2,1)S(1)} %copy-done.36, ...), custom_call_target="tpu_custom_call" | custom-call | bytes 13000000 | tf_op jit(solution)/shard_map/attend_back/pallas_call | solution.py:110
  556.8 25.9 %collective-permute-done.65 = bf16[1024,1024]{1,0:T(8,128)(2,1)} collective-permute-done((bf16[1024,1024]{1,0:T(8,128)(2,1)S(1)}, bf16[1024,1024]{1,0:T(8,128)(2,1)}, u32[]{:S(2)}, u32[]{:S(2)}) %collective-permute-start.65) | collective-permute-done | bytes 2097184 | tf_op jit(solution)/shard_map/ppermute | solution.py:315
  602.0 8.6 %collective-permute-start.63 = (bf16[2,128,1024]{2,1,0:T(8,128)(2,1)}, bf16[2,128,1024]{2,1,0:T(8,128)(2,1)}, u32[]{:S(2)}, u32[]{:S(2)}) collective-permute-start(bf16[2,128,1024]{2,1,0:T(8,128)(2,1)} %split.133), channel_id=1, source_target_pairs={{0,2},{1,3},{2,0},{3,1},{4,6},{5,7},{6,4},{7,5},{8,10},{9,11},{10,... | collective-permute-start | bytes 1572872 | tf_op jit(solution)/shard_map/ppermute | solution.py:315
  623.9 30.0 %collective-permute-done.64 = bf16[2,64,1024]{2,1,0:T(8,128)(2,1)} collective-permute-done((bf16[2,64,1024]{2,1,0:T(8,128)(2,1)}, bf16[2,64,1024]{2,1,0:T(8,128)(2,1)}, u32[]{:S(2)}, u32[]{:S(2)}) %collective-permute-start.64) | collective-permute-done | bytes 262176 | tf_op jit(solution)/shard_map/ppermute | solution.py:315
  665.3 6.7 collective-permute-done.62
  681.1 7.1 collective-permute-done.69
  693.3 7.5 collective-permute-done.68
  703.1 21.3 %collective-permute-done.74 = bf16[512,1024]{1,0:T(8,128)(2,1)S(1)} collective-permute-done((bf16[512,1024]{1,0:T(8,128)(2,1)S(1)}, bf16[512,1024]{1,0:T(8,128)(2,1)S(1)}, u32[]{:S(2)}, u32[]{:S(2)}) %collective-permute-start.74) | collective-permute-done | bytes 1048608 | tf_op jit(solution)/shard_map/ppermute | solution.py:315
  756.5 13.1 %collective-permute-done.81 = bf16[1,128,1024]{2,1,0:T(8,128)(2,1)S(1)} collective-permute-done((bf16[1,128,1024]{2,1,0:T(8,128)(2,1)S(1)}, bf16[1,128,1024]{2,1,0:T(8,128)(2,1)S(1)}, u32[]{:S(2)}, u32[]{:S(2)}) %collective-permute-start.81) | collective-permute-done | bytes 262176 | tf_op jit(solution)/shard_map/ppermute | solution.py:315
  792.2 7.5 collective-permute-done.90
  799.8 8.9 %collective-permute-done.91 = bf16[256,1024]{1,0:T(8,128)(2,1)S(1)} collective-permute-done((bf16[256,1024]{1,0:T(8,128)(2,1)S(1)}, bf16[256,1024]{1,0:T(8,128)(2,1)S(1)}, u32[]{:S(2)}, u32[]{:S(2)}) %collective-permute-start.91) | collective-permute-done | bytes 524320 | tf_op jit(solution)/shard_map/ppermute | solution.py:315
  809.7 7.3 collective-permute-done.95
  (936 shorter events, 414.8 us)
Async XLA Ops:
  7.2 216.2 %all-gather.5.cloned.1.call-start = ((), (), s32[]{:S(2)}) async-start(), calls=%async_computation.4 | async-start | bytes 4718592 | tf_op jit(solution)/shard_map/all_gather | solution.py:515
  13.2 45.1 %collective-permute-start = (bf16[128,1024]{1,0:T(8,128)(2,1)S(1)}, bf16[128,1024]{1,0:T(8,128)(2,1)S(1)}, u32[]{:S(2)}, u32[]{:S(2)}) collective-permute-start(bf16[128,1024]{1,0:T(8,128)(2,1)S(1)} %dynamic-slice_bitcast_fusion.1), channel_id=1, source_target_pairs={{0,4},{1,5},{2,6},{3,7},{4,0},{5,1},{6,2},{7,3},{8,12},{9,13},{10,... | collective-permute-start | bytes 786440 | tf_op jit(solution)/shard_map/ppermute | solution.py:315
  17.4 75.9 %collective-permute-start.6 = (bf16[256,1024]{1,0:T(8,128)(2,1)S(1)}, bf16[256,1024]{1,0:T(8,128)(2,1)}, u32[]{:S(2)}, u32[]{:S(2)}) collective-permute-start(bf16[256,1024]{1,0:T(8,128)(2,1)S(1)} %copy-done.125), channel_id=1, source_target_pairs={{0,1},{1,0},{2,3},{3,2},{4,5},{5,4},{6,7},{7,6},{8,9},{9,8},{10,11... | collective-permute-start | bytes 1572872 | tf_op jit(solution)/shard_map/ppermute | solution.py:315
  28.7 29.7 %collective-permute-start.7 = (bf16[1,256,1024]{2,1,0:T(8,128)(2,1)S(1)}, bf16[1,256,1024]{2,1,0:T(8,128)(2,1)}, u32[]{:S(2)}, u32[]{:S(2)}) collective-permute-start(bf16[1,256,1024]{2,1,0:T(8,128)(2,1)S(1)} %bitcast.311), channel_id=1, source_target_pairs={{0,4},{1,5},{2,6},{3,7},{4,0},{5,1},{6,2},{7,3},{8,12},{9,13},{10,... | collective-permute-start | bytes 1572872 | tf_op jit(solution)/shard_map/ppermute | solution.py:315
  60.6 27.1 %collective-permute-start.8 = (bf16[2,256,1024]{2,1,0:T(8,128)(2,1)}, bf16[2,256,1024]{2,1,0:T(8,128)(2,1)}, u32[]{:S(2)}, u32[]{:S(2)}) collective-permute-start(bf16[2,256,1024]{2,1,0:T(8,128)(2,1)} %pad_maximum_fusion.7), channel_id=1, source_target_pairs={{0,2},{1,3},{2,0},{3,1},{4,6},{5,7},{6,4},{7,5},{8,10},{9,11},{10,... | collective-permute-start | bytes 3145736 | tf_op jit(solution)/shard_map/ppermute | solution.py:315
  93.3 184.4 %all-gather.7.cloned.1.call-start = ((), (), s32[]{:S(2)}) async-start(), calls=%async_computation.5 | async-start | bytes 4718592 | tf_op jit(solution)/shard_map/all_gather | solution.py:528
  95.1 91.4 %collective-permute-start.16 = (bf16[4,256,1024]{2,1,0:T(8,128)(2,1)}, bf16[4,256,1024]{2,1,0:T(8,128)(2,1)}, u32[]{:S(2)}, u32[]{:S(2)}) collective-permute-start(bf16[4,256,1024]{2,1,0:T(8,128)(2,1)} %pad_maximum_fusion.2), channel_id=1, source_target_pairs={{0,1},{1,0},{2,3},{3,2},{4,5},{5,4},{6,7},{7,6},{8,9},{9,8},{10,11... | collective-permute-start | bytes 6291464 | tf_op jit(solution)/shard_map/ppermute | solution.py:315
  103.1 30.1 %collective-permute-start.12 = (bf16[256,1024]{1,0:T(8,128)(2,1)S(1)}, bf16[256,1024]{1,0:T(8,128)(2,1)S(1)}, u32[]{:S(2)}, u32[]{:S(2)}) collective-permute-start(bf16[256,1024]{1,0:T(8,128)(2,1)S(1)} %pad_maximum_fusion.22), channel_id=1, source_target_pairs={{0,2},{1,3},{2,0},{3,1},{4,6},{5,7},{6,4},{7,5},{8,10},{9,11},{10,... | collective-permute-start | bytes 1572872 | tf_op jit(solution)/shard_map/ppermute | solution.py:315
  107.6 83.9 %collective-permute-start.14 = (bf16[1024,1024]{1,0:T(8,128)(2,1)}, bf16[1024,1024]{1,0:T(8,128)(2,1)}, u32[]{:S(2)}, u32[]{:S(2)}) collective-permute-start(bf16[1024,1024]{1,0:T(8,128)(2,1)} %pad_maximum_fusion.1.refs_2_.refs_9_), channel_id=1, source_target_pairs={{0,16},{8,24},{16,0},{24,8},{1,17},{9,25},{17,1},{25,9},{2,18},{10... | collective-permute-start | bytes 6291464 | tf_op jit(solution)/shard_map/ppermute | solution.py:315
  110.3 56.9 %collective-permute-start.15 = (bf16[512,1024]{1,0:T(8,128)(2,1)S(1)}, bf16[512,1024]{1,0:T(8,128)(2,1)S(1)}, u32[]{:S(2)}, u32[]{:S(2)}) collective-permute-start(bf16[512,1024]{1,0:T(8,128)(2,1)S(1)} %pad_maximum_fusion.9), channel_id=1, source_target_pairs={{0,2},{1,3},{2,0},{3,1},{4,6},{5,7},{6,4},{7,5},{8,10},{9,11},{10,... | collective-permute-start | bytes 3145736 | tf_op jit(solution)/shard_map/ppermute | solution.py:315
  133.3 51.7 %collective-permute-start.13 = (bf16[512,1024]{1,0:T(8,128)(2,1)S(1)}, bf16[512,1024]{1,0:T(8,128)(2,1)S(1)}, u32[]{:S(2)}, u32[]{:S(2)}) collective-permute-start(bf16[512,1024]{1,0:T(8,128)(2,1)S(1)} %pad_maximum_fusion.8), channel_id=1, source_target_pairs={{0,1},{1,0},{2,3},{3,2},{4,5},{5,4},{6,7},{7,6},{8,9},{9,8},{10,11... | collective-permute-start | bytes 3145736 | tf_op jit(solution)/shard_map/ppermute | solution.py:315
  191.5 538.2 %reduce-scatter.5.cloned.1.call-start = ((), (), s32[]{:S(2)}) async-start(), calls=%async_computation.3 | async-start | bytes 4718592 | tf_op jit(solution)/shard_map/reduce_scatter | solution.py:606
  193.0 27.2 %collective-permute-start.17 = (bf16[1024,1024]{1,0:T(8,128)(2,1)}, bf16[1024,1024]{1,0:T(8,128)(2,1)}, u32[]{:S(2)}, u32[]{:S(2)}) collective-permute-start(bf16[1024,1024]{1,0:T(8,128)(2,1)} %pad_maximum_fusion.3.refs_6_.refs_5_), channel_id=1, source_target_pairs={{0,16},{8,24},{16,0},{24,8},{1,17},{9,25},{17,1},{25,9},{2,18},{10... | collective-permute-start | bytes 6291464 | tf_op jit(solution)/shard_map/ppermute | solution.py:315
  227.7 48.6 %collective-permute-start.10 = (bf16[1024,1024]{1,0:T(8,128)(2,1)S(1)}, bf16[1024,1024]{1,0:T(8,128)(2,1)S(1)}, u32[]{:S(2)}, u32[]{:S(2)}) collective-permute-start(bf16[1024,1024]{1,0:T(8,128)(2,1)S(1)} %bitcast.268), channel_id=1, source_target_pairs={{0,16},{8,24},{16,0},{24,8},{1,17},{9,25},{17,1},{25,9},{2,18},{10... | collective-permute-start | bytes 6291464 | tf_op jit(solution)/shard_map/ppermute | solution.py:315
  244.6 75.9 %collective-permute-start.9 = (bf16[1024,1024]{1,0:T(8,128)(2,1)}, bf16[1024,1024]{1,0:T(8,128)(2,1)}, u32[]{:S(2)}, u32[]{:S(2)}) collective-permute-start(bf16[1024,1024]{1,0:T(8,128)(2,1)} %bitcast.43.refs_6_.refs_5_), channel_id=1, source_target_pairs={{0,16},{8,24},{16,0},{24,8},{1,17},{9,25},{17,1},{25,9},{2,18},{10... | collective-permute-start | bytes 6291464 | tf_op jit(solution)/shard_map/ppermute | solution.py:315
  291.4 29.0 %collective-permute-start.26 = (bf16[1024,1024]{1,0:T(8,128)(2,1)S(1)}, bf16[1024,1024]{1,0:T(8,128)(2,1)S(1)}, u32[]{:S(2)}, u32[]{:S(2)}) collective-permute-start(bf16[1024,1024]{1,0:T(8,128)(2,1)S(1)} %bitcast.270), channel_id=1, source_target_pairs={{0,8},{8,0},{16,24},{24,16},{1,9},{9,1},{17,25},{25,17},{2,10},{10... | collective-permute-start | bytes 6291464 | tf_op jit(solution)/shard_map/ppermute | solution.py:315
  345.2 103.4 %collective-permute-start.45 = (bf16[256,1024]{1,0:T(8,128)(2,1)}, bf16[256,1024]{1,0:T(8,128)(2,1)}, u32[]{:S(2)}, u32[]{:S(2)}) collective-permute-start(bf16[256,1024]{1,0:T(8,128)(2,1)} %get-tuple-element.281), channel_id=1, source_target_pairs={{0,8},{8,0},{16,24},{24,16},{1,9},{9,1},{17,25},{25,17},{2,10},{10... | collective-permute-start | bytes 1572872 | tf_op jit(solution)/shard_map/ppermute | solution.py:315
  345.7 34.2 %collective-permute-start.40 = (bf16[256,1024]{1,0:T(8,128)(2,1)}, bf16[256,1024]{1,0:T(8,128)(2,1)}, u32[]{:S(2)}, u32[]{:S(2)}) collective-permute-start(bf16[256,1024]{1,0:T(8,128)(2,1)} %get-tuple-element.235.refs_0_.refs_1_), channel_id=1, source_target_pairs={{0,8},{8,0},{16,24},{24,16},{1,9},{9,1},{17,25},{25,17},{2,10},{10... | collective-permute-start | bytes 1572872 | tf_op jit(solution)/shard_map/ppermute | solution.py:315
  376.5 373.7 %reduce-scatter.3.cloned.1.call-start = ((), (), s32[]{:S(2)}) async-start(), calls=%async_computation.2 | async-start | bytes 7077888 | tf_op jit(solution)/shard_map/reduce_scatter | solution.py:606
  398.6 65.3 %collective-permute-start.48 = (bf16[1024,1024]{1,0:T(8,128)(2,1)}, bf16[1024,1024]{1,0:T(8,128)(2,1)}, u32[]{:S(2)}, u32[]{:S(2)}) collective-permute-start(bf16[1024,1024]{1,0:T(8,128)(2,1)} %weight_grad.27), channel_id=1, source_target_pairs={{0,16},{8,24},{16,0},{24,8},{1,17},{9,25},{17,1},{25,9},{2,18},{10... | collective-permute-start | bytes 6291464 | tf_op jit(solution)/shard_map/ppermute | solution.py:315
  448.7 25.2 %collective-permute-start.51 = (bf16[512,1024]{1,0:T(8,128)(2,1)}, bf16[512,1024]{1,0:T(8,128)(2,1)}, u32[]{:S(2)}, u32[]{:S(2)}) collective-permute-start(bf16[512,1024]{1,0:T(8,128)(2,1)} %copy-done.69), channel_id=1, source_target_pairs={{0,8},{8,0},{16,24},{24,16},{1,9},{9,1},{17,25},{25,17},{2,10},{10... | collective-permute-start | bytes 3145736 | tf_op jit(solution)/shard_map/ppermute | solution.py:315
  458.5 45.7 %collective-permute-start.53 = (bf16[256,1024]{1,0:T(8,128)(2,1)}, bf16[256,1024]{1,0:T(8,128)(2,1)}, u32[]{:S(2)}, u32[]{:S(2)}) collective-permute-start(bf16[256,1024]{1,0:T(8,128)(2,1)} %get-tuple-element.219.refs_0_.refs_1_), channel_id=1, source_target_pairs={{0,8},{8,0},{16,24},{24,16},{1,9},{9,1},{17,25},{25,17},{2,10},{10... | collective-permute-start | bytes 1572872 | tf_op jit(solution)/shard_map/ppermute | solution.py:315
  489.9 48.8 %collective-permute-start.55 = (bf16[1024,1024]{1,0:T(8,128)(2,1)}, bf16[1024,1024]{1,0:T(8,128)(2,1)}, u32[]{:S(2)}, u32[]{:S(2)}) collective-permute-start(bf16[1024,1024]{1,0:T(8,128)(2,1)} %weight_grad.31), channel_id=1, source_target_pairs={{0,16},{8,24},{16,0},{24,8},{1,17},{9,25},{17,1},{25,9},{2,18},{10... | collective-permute-start | bytes 6291464 | tf_op jit(solution)/shard_map/ppermute | solution.py:315
  512.2 70.5 %collective-permute-start.65 = (bf16[1024,1024]{1,0:T(8,128)(2,1)S(1)}, bf16[1024,1024]{1,0:T(8,128)(2,1)}, u32[]{:S(2)}, u32[]{:S(2)}) collective-permute-start(bf16[1024,1024]{1,0:T(8,128)(2,1)S(1)} %weight_grad.39), channel_id=1, source_target_pairs={{0,16},{8,24},{16,0},{24,8},{1,17},{9,25},{17,1},{25,9},{2,18},{10... | collective-permute-start | bytes 6291464 | tf_op jit(solution)/shard_map/ppermute | solution.py:315
  542.5 52.0 %collective-permute-start.57 = (bf16[4,128,1024]{2,1,0:T(8,128)(2,1)}, bf16[4,128,1024]{2,1,0:T(8,128)(2,1)S(1)}, u32[]{:S(2)}, u32[]{:S(2)}) collective-permute-start(bf16[4,128,1024]{2,1,0:T(8,128)(2,1)} %split.126), channel_id=1, source_target_pairs={{0,1},{1,0},{2,3},{3,2},{4,5},{5,4},{6,7},{7,6},{8,9},{9,8},{10,11... | collective-permute-start | bytes 3145736 | tf_op jit(solution)/shard_map/ppermute | solution.py:315
  555.7 38.5 %collective-permute-start.58 = (bf16[4,64,1024]{2,1,0:T(8,128)(2,1)S(1)}, bf16[4,64,1024]{2,1,0:T(8,128)(2,1)S(1)}, u32[]{:S(2)}, u32[]{:S(2)}) collective-permute-start(bf16[4,64,1024]{2,1,0:T(8,128)(2,1)S(1)} %split.128), channel_id=1, source_target_pairs={{0,1},{1,0},{2,3},{3,2},{4,5},{5,4},{6,7},{7,6},{8,9},{9,8},{10,11... | collective-permute-start | bytes 1572872 | tf_op jit(solution)/shard_map/ppermute | solution.py:315
  586.8 73.2 %collective-permute-start.66 = (bf16[4,128,1024]{2,1,0:T(8,128)(2,1)}, bf16[4,128,1024]{2,1,0:T(8,128)(2,1)}, u32[]{:S(2)}, u32[]{:S(2)}) collective-permute-start(bf16[4,128,1024]{2,1,0:T(8,128)(2,1)} %bitcast.95), channel_id=1, source_target_pairs={{0,1},{1,0},{2,3},{3,2},{4,5},{5,4},{6,7},{7,6},{8,9},{9,8},{10,11... | collective-permute-start | bytes 3145736 | tf_op jit(solution)/shard_map/ppermute | solution.py:315
  596.5 65.2 %collective-permute-start.59 = (bf16[512,1024]{1,0:T(8,128)(2,1)}, bf16[512,1024]{1,0:T(8,128)(2,1)}, u32[]{:S(2)}, u32[]{:S(2)}) collective-permute-start(bf16[512,1024]{1,0:T(8,128)(2,1)} %weight_grad.42), channel_id=1, source_target_pairs={{0,8},{8,0},{16,24},{24,16},{1,9},{9,1},{17,25},{25,17},{2,10},{10... | collective-permute-start | bytes 3145736 | tf_op jit(solution)/shard_map/ppermute | solution.py:315
  600.6 54.3 %collective-permute-start.61 = (bf16[512,1024]{1,0:T(8,128)(2,1)}, bf16[512,1024]{1,0:T(8,128)(2,1)}, u32[]{:S(2)}, u32[]{:S(2)}) collective-permute-start(bf16[512,1024]{1,0:T(8,128)(2,1)} %weight_grad.46), channel_id=1, source_target_pairs={{0,8},{8,0},{16,24},{24,16},{1,9},{9,1},{17,25},{25,17},{2,10},{10... | collective-permute-start | bytes 3145736 | tf_op jit(solution)/shard_map/ppermute | solution.py:315
  602.0 55.7 %collective-permute-start.63 = (bf16[2,128,1024]{2,1,0:T(8,128)(2,1)}, bf16[2,128,1024]{2,1,0:T(8,128)(2,1)}, u32[]{:S(2)}, u32[]{:S(2)}) collective-permute-start(bf16[2,128,1024]{2,1,0:T(8,128)(2,1)} %split.133), channel_id=1, source_target_pairs={{0,2},{1,3},{2,0},{3,1},{4,6},{5,7},{6,4},{7,5},{8,10},{9,11},{10,... | collective-permute-start | bytes 1572872 | tf_op jit(solution)/shard_map/ppermute | solution.py:315
  611.4 42.5 %collective-permute-start.64 = (bf16[2,64,1024]{2,1,0:T(8,128)(2,1)}, bf16[2,64,1024]{2,1,0:T(8,128)(2,1)}, u32[]{:S(2)}, u32[]{:S(2)}) collective-permute-start(bf16[2,64,1024]{2,1,0:T(8,128)(2,1)} %split.135), channel_id=1, source_target_pairs={{0,2},{1,3},{2,0},{3,1},{4,6},{5,7},{6,4},{7,5},{8,10},{9,11},{10,... | collective-permute-start | bytes 786440 | tf_op jit(solution)/shard_map/ppermute | solution.py:315
  688.1 36.3 %collective-permute-start.74 = (bf16[512,1024]{1,0:T(8,128)(2,1)S(1)}, bf16[512,1024]{1,0:T(8,128)(2,1)S(1)}, u32[]{:S(2)}, u32[]{:S(2)}) collective-permute-start(bf16[512,1024]{1,0:T(8,128)(2,1)S(1)} %split.152), channel_id=1, source_target_pairs={{0,2},{1,3},{2,0},{3,1},{4,6},{5,7},{6,4},{7,5},{8,10},{9,11},{10,... | collective-permute-start | bytes 3145736 | tf_op jit(solution)/shard_map/ppermute | solution.py:315
  (279 other events, 2561.6 us)
Sparse Core Ops, SparseCore 0:
  93.5 105.0 all-gather.4
  201.4 72.6 all-gather.6
  376.6 93.0 reduce-scatter.4
  501.6 151.3 reduce-scatter.2

commit v4 on v3

--- a/solution.py
+++ b/solution.py
@@ -691,6 +691,7 @@
     for bit in first_bits[steps_done : steps_done + 1]:
         outer_sum, out_total = one_step(outer_sum, bit), one_step(out_total, bit)
     inner_sum, totals[2] = one_step(inner_sum, first_bits[0]), one_step(totals[2], first_bits[0])
+    vector = next_hop(vector)
     totals, outer_sum, out_total, inner_sum, vector, far_part = together(
         totals, outer_sum, out_total, inner_sum, vector, far_part
     )

time: 844 us -> 828 us (0.981)
  waiting for transfers between devices: 352 us -> 335 us
    ppermute x92, waiting for transfers between devices: 329 us -> 310 us  [swap(): return lax.ppermute(array, axis, [(i, i ^ bit) for i in range(count)])]
    unnamed x449 -> x455, local copies, waits for them, and re-layouts: 47.4 us -> 49.5 us
  transfers between devices with their start and end apart: 100 -> 100, of which waited for: 39 -> 38; matrix products, arithmetic and copies ran while one was open for 21% -> 21% of each run, Pallas kernels for 17% -> 18%
where the time goes in v4:
time: 828 us; the launch traced here: 818 us
  waiting for transfers between devices  335 us (40%)
  Pallas kernels  160 us (19%)
  local copies, waits for them, and re-layouts  106 us (13%)
  starting transfers between devices  84.8 us (10%)
  other arithmetic  84.6 us (10%)
  matrix products  30.2 us (4%)
  between operations  17.8 us (2%)
    ppermute x92, waiting for transfers between devices, swap(): return lax.ppermute(array, axis, [(i, i ^ bit) for i in range(count)])  310 us
    ppermute x92, starting transfers between devices, swap(): return lax.ppermute(array, axis, [(i, i ^ bit) for i in range(count)])  74.7 us
    pallas_call x24, Pallas kernels, weight_grad(): pl.pallas_call(kernel, grid=(columns // tile,), in_specs=specs, out_specs...  55.6 us
    unnamed x455, local copies, waits for them, and re-layouts  49.5 us
    pallas_call x4, Pallas kernels, streamed(): pl.pallas_call(kernel, in_specs=[whole] * (near_count + extra_count) + [a...  43.1 us
    pallas_call x4, Pallas kernels, attend_back(): pl.pallas_call(partial(attend_back_kernel, halo), grid=(width // LANES,),...  33.8 us
    ppermute x4, waiting for transfers between devices, shift(): return lax.ppermute(array, 'tensor', pairs)  24.4 us
    pallas_call x4, Pallas kernels, attend(): pl.pallas_call(partial(attend_kernel, halo), grid=(width // LANES,), in_s...  21.7 us
  transfers between devices with their start and end apart: 100, of which 38 were waited for; matrix products, arithmetic and copies ran while one was open for 21% of the time, Pallas kernels for 18%

profile of v4, /device:TPU:0, one launch (start us, length us, event | category | flops | bytes accessed | tf_op | source)
XLA Modules:
  0.0 817.8 jit_solution(15350190045762756006)
XLA Ops:
  43.2 10.7 %collective-permute-done.4 = f32[2,2,768]{2,1,0:T(2,128)S(1)} collective-permute-done((f32[2,2,768]{2,1,0:T(2,128)S(1)}, f32[2,2,768]{2,1,0:T(2,128)S(1)}, u32[]{:S(2)}, u32[]{:S(2)}) %collective-permute-start.4) | collective-permute-done | bytes 12320 | tf_op jit(solution)/shard_map/ppermute | solution.py:315
  63.2 10.1 %collective-permute-done.1 = bf16[256,1024]{1,0:T(8,128)(2,1)S(1)} collective-permute-done((bf16[256,1024]{1,0:T(8,128)(2,1)S(1)}, bf16[256,1024]{1,0:T(8,128)(2,1)S(1)}, u32[]{:S(2)}, u32[]{:S(2)}) %collective-permute-start.1) | collective-permute-done | bytes 524320 | tf_op jit(solution)/shard_map/ppermute | solution.py:315
  75.7 12.0 %collective-permute-done.8 = bf16[2,256,1024]{2,1,0:T(8,128)(2,1)} collective-permute-done((bf16[2,256,1024]{2,1,0:T(8,128)(2,1)}, bf16[2,256,1024]{2,1,0:T(8,128)(2,1)}, u32[]{:S(2)}, u32[]{:S(2)}) %collective-permute-start.8) | collective-permute-done | bytes 1048608 | tf_op jit(solution)/shard_map/ppermute | solution.py:315
  95.6 7.5 collective-permute-done.11
  110.8 22.4 %collective-permute-done.12 = bf16[256,1024]{1,0:T(8,128)(2,1)S(1)} collective-permute-done((bf16[256,1024]{1,0:T(8,128)(2,1)S(1)}, bf16[256,1024]{1,0:T(8,128)(2,1)S(1)}, u32[]{:S(2)}, u32[]{:S(2)}) %collective-permute-start.12) | collective-permute-done | bytes 524320 | tf_op jit(solution)/shard_map/ppermute | solution.py:315
  137.7 29.4 %collective-permute-done.15 = bf16[512,1024]{1,0:T(8,128)(2,1)S(1)} collective-permute-done((bf16[512,1024]{1,0:T(8,128)(2,1)S(1)}, bf16[512,1024]{1,0:T(8,128)(2,1)S(1)}, u32[]{:S(2)}, u32[]{:S(2)}) %collective-permute-start.15) | collective-permute-done | bytes 1048608 | tf_op jit(solution)/shard_map/ppermute | solution.py:315
  168.4 16.6 %collective-permute-done.13 = bf16[512,1024]{1,0:T(8,128)(2,1)S(1)} collective-permute-done((bf16[512,1024]{1,0:T(8,128)(2,1)S(1)}, bf16[512,1024]{1,0:T(8,128)(2,1)S(1)}, u32[]{:S(2)}, u32[]{:S(2)}) %collective-permute-start.13) | collective-permute-done | bytes 1048608 | tf_op jit(solution)/shard_map/ppermute | solution.py:315
  200.0 6.5 attend.4.refs_0_
  211.1 6.3 attend.5.refs_0_
  230.9 11.5 %feed_forward.2 = (f32[256,1024]{1,0:T(8,128)S(1)}, bf16[256,1024]{1,0:T(8,128)(2,1)S(1)}, bf16[256,1024]{1,0:T(8,128)(2,1)S(1)}, bf16[256,1024]{1,0:T(8,128)(2,...) custom-call(bf16[256,1024]{1,0:T(8,128)(2,1)} %get-tuple-element.219, ...), custom_call_target="tpu_custom_call" | custom-call | bytes 13000000 | tf_op jit(solution)/shard_map/feed_forward/pallas_call | solution.py:185
  246.1 30.2 %collective-permute-done.10.refs_3_.refs_10_ = bf16[1024,1024]{1,0:T(8,128)(2,1)S(1)} collective-permute-done((bf16[1024,1024]{1,0:T(8,128)(2,1)S(1)}, bf16[1024,1024]{1,0:T(8,128)(2,1)S(1)}, u32[]{:S(2)}, u32[]{:S(2)}) %collective-permute-start.10) | collective-permute-done | bytes 2097184 | tf_op jit(solution)/shard_map/ppermute | solution.py:315
  313.2 7.3 collective-permute-done.9.refs_7_.refs_6_
  329.3 11.0 %feed_forward.3 = (f32[256,1024]{1,0:T(8,128)S(1)}, bf16[256,1024]{1,0:T(8,128)(2,1)S(1)}, bf16[256,1024]{1,0:T(8,128)(2,1)S(1)}, bf16[256,1024]{1,0:T(8,128)(2,...) custom-call(bf16[256,1024]{1,0:T(8,128)(2,1)} %get-tuple-element.235, ...), custom_call_target="tpu_custom_call" | custom-call | bytes 13000000 | tf_op jit(solution)/shard_map/feed_forward/pallas_call | solution.py:185
  354.8 9.9 %feed_forward_back.2 = (f32[256,1024]{1,0:T(8,128)S(1)}, f32[4,1024]{1,0:T(4,128)S(1)}, bf16[256,1024]{1,0:T(8,128)(2,1)S(1)}, bf16[256,1024]{1,0:T(8,128)(2,1)S...) custom-call(bf16[256,1024]{1,0:T(8,128)(2,1)S(1)} %convert_element_type.363.refs_1_.refs_0_, ...), custom_call_target="tpu_custom_call" | custom-call | bytes 13000000 | tf_op jit(solution)/shard_map/feed_forward_back/pallas_call | solution.py:185
  390.9 6.8 attend_back.4
  404.9 6.8 attend_back.5
  420.3 15.2 %collective-permute-done.44 = bf16[128,1024]{1,0:T(8,128)(2,1)S(1)} collective-permute-done((bf16[128,1024]{1,0:T(8,128)(2,1)S(1)}, bf16[128,1024]{1,0:T(8,128)(2,1)S(1)}, u32[]{:S(2)}, u32[]{:S(2)}) %collective-permute-start.44) | collective-permute-done | bytes 262176 | tf_op jit(solution)/shard_map/ppermute | solution.py:330
  477.5 10.7 %feed_forward_back.3 = (f32[256,1024]{1,0:T(8,128)S(1)}, f32[4,1024]{1,0:T(4,128)S(1)}, bf16[256,1024]{1,0:T(8,128)(2,1)S(1)}, bf16[256,1024]{1,0:T(8,128)(2,1)S...) custom-call(bf16[256,1024]{1,0:T(8,128)(2,1)} %convert_element_type.369.refs_1_.refs_0_, ...), custom_call_target="tpu_custom_call" | custom-call | bytes 13000000 | tf_op jit(solution)/shard_map/feed_forward_back/pallas_call | solution.py:185
  515.2 10.1 %attend_back.6 = (bf16[256,512]{1,0:T(8,128)(2,1)S(1)}, bf16[1024,512]{1,0:T(8,128)(2,1)S(1)}, bf16[1024,512]{1,0:T(8,128)(2,1)S(1)}) custom-call(s32[256,1]{1,0:T(8,128)S(1)} %copy.122.seg_q_ref, s32[1,1024]{1,0:T(1,128)S(1)} %bitcast.298, bf16[256,512]{1,0:T(8,128)(2,1)S(1)} %copy-done.83, bf16[1024,512]{1,0:T(8,128)(2,1)S(1)} %copy-done.42, ...), custom_call_target="tpu_custom_call" | custom-call | bytes 13000000 | tf_op jit(solution)/shard_map/attend_back/pallas_call | solution.py:110
  532.1 7.0 collective-permute-done.55
  545.0 10.1 %attend_back.7 = (bf16[256,512]{1,0:T(8,128)(2,1)S(1)}, bf16[1024,512]{1,0:T(8,128)(2,1)S(1)}, bf16[1024,512]{1,0:T(8,128)(2,1)S(1)}) custom-call(s32[256,1]{1,0:T(8,128)S(1)} %copy.122.seg_q_ref, s32[1,1024]{1,0:T(1,128)S(1)} %bitcast.299, bf16[256,512]{1,0:T(8,128)(2,1)S(1)} %copy-done.81, bf16[1024,512]{1,0:T(8,128)(2,1)S(1)} %copy-done.38, ...), custom_call_target="tpu_custom_call" | custom-call | bytes 13000000 | tf_op jit(solution)/shard_map/attend_back/pallas_call | solution.py:110
  556.1 27.1 %collective-permute-done.65 = bf16[1024,1024]{1,0:T(8,128)(2,1)} collective-permute-done((bf16[1024,1024]{1,0:T(8,128)(2,1)}, bf16[1024,1024]{1,0:T(8,128)(2,1)}, u32[]{:S(2)}, u32[]{:S(2)}) %collective-permute-start.65) | collective-permute-done | bytes 2097184 | tf_op jit(solution)/shard_map/ppermute | solution.py:315
  589.8 8.1 collective-permute-done.58
  606.5 6.2 collective-permute-start.63
  627.1 21.6 %collective-permute-done.64 = bf16[2,64,1024]{2,1,0:T(8,128)(2,1)S(1)} collective-permute-done((bf16[2,64,1024]{2,1,0:T(8,128)(2,1)S(1)}, bf16[2,64,1024]{2,1,0:T(8,128)(2,1)S(1)}, u32[]{:S(2)}, u32[]{:S(2)}) %collective-permute-start.64) | collective-permute-done | bytes 262176 | tf_op jit(solution)/shard_map/ppermute | solution.py:315
  659.3 6.6 collective-permute-done.62
  675.9 8.3 %collective-permute-done.70 = bf16[2,64,1024]{2,1,0:T(8,128)(2,1)S(1)} collective-permute-done((bf16[2,64,1024]{2,1,0:T(8,128)(2,1)S(1)}, bf16[2,64,1024]{2,1,0:T(8,128)(2,1)S(1)}, u32[]{:S(2)}, u32[]{:S(2)}) %collective-permute-start.70) | collective-permute-done | bytes 262176 | tf_op jit(solution)/shard_map/ppermute | solution.py:315
  686.9 6.7 collective-permute-done.69
  697.7 19.8 %collective-permute-done.75 = bf16[512,1024]{1,0:T(8,128)(2,1)S(1)} collective-permute-done((bf16[512,1024]{1,0:T(8,128)(2,1)S(1)}, bf16[512,1024]{1,0:T(8,128)(2,1)S(1)}, u32[]{:S(2)}, u32[]{:S(2)}) %collective-permute-start.75) | collective-permute-done | bytes 1048608 | tf_op jit(solution)/shard_map/ppermute | solution.py:315
  749.4 10.4 %collective-permute-done.82 = bf16[1,128,1024]{2,1,0:T(8,128)(2,1)S(1)} collective-permute-done((bf16[1,128,1024]{2,1,0:T(8,128)(2,1)S(1)}, bf16[1,128,1024]{2,1,0:T(8,128)(2,1)S(1)}, u32[]{:S(2)}, u32[]{:S(2)}) %collective-permute-start.82) | collective-permute-done | bytes 262176 | tf_op jit(solution)/shard_map/ppermute | solution.py:315
  783.9 6.1 collective-permute-done.91
  790.1 10.0 %collective-permute-done.92 = bf16[256,1024]{1,0:T(8,128)(2,1)S(1)} collective-permute-done((bf16[256,1024]{1,0:T(8,128)(2,1)S(1)}, bf16[256,1024]{1,0:T(8,128)(2,1)S(1)}, u32[]{:S(2)}, u32[]{:S(2)}) %collective-permute-start.92) | collective-permute-done | bytes 524320 | tf_op jit(solution)/shard_map/ppermute | solution.py:315
  (942 shorter events, 411.0 us)
Async XLA Ops:
  7.2 216.2 %all-gather.5.cloned.1.call-start = ((), (), s32[]{:S(2)}) async-start(), calls=%async_computation.4 | async-start | bytes 4718592 | tf_op jit(solution)/shard_map/all_gather | solution.py:515
  13.2 45.1 %collective-permute-start = (bf16[128,1024]{1,0:T(8,128)(2,1)S(1)}, bf16[128,1024]{1,0:T(8,128)(2,1)S(1)}, u32[]{:S(2)}, u32[]{:S(2)}) collective-permute-start(bf16[128,1024]{1,0:T(8,128)(2,1)S(1)} %dynamic-slice_bitcast_fusion.1), channel_id=1, source_target_pairs={{0,4},{1,5},{2,6},{3,7},{4,0},{5,1},{6,2},{7,3},{8,12},{9,13},{10,... | collective-permute-start | bytes 786440 | tf_op jit(solution)/shard_map/ppermute | solution.py:315
  17.4 75.9 %collective-permute-start.6 = (bf16[256,1024]{1,0:T(8,128)(2,1)S(1)}, bf16[256,1024]{1,0:T(8,128)(2,1)}, u32[]{:S(2)}, u32[]{:S(2)}) collective-permute-start(bf16[256,1024]{1,0:T(8,128)(2,1)S(1)} %copy-done.124), channel_id=1, source_target_pairs={{0,1},{1,0},{2,3},{3,2},{4,5},{5,4},{6,7},{7,6},{8,9},{9,8},{10,11... | collective-permute-start | bytes 1572872 | tf_op jit(solution)/shard_map/ppermute | solution.py:315
  28.7 29.7 %collective-permute-start.7 = (bf16[1,256,1024]{2,1,0:T(8,128)(2,1)S(1)}, bf16[1,256,1024]{2,1,0:T(8,128)(2,1)}, u32[]{:S(2)}, u32[]{:S(2)}) collective-permute-start(bf16[1,256,1024]{2,1,0:T(8,128)(2,1)S(1)} %bitcast.311), channel_id=1, source_target_pairs={{0,4},{1,5},{2,6},{3,7},{4,0},{5,1},{6,2},{7,3},{8,12},{9,13},{10,... | collective-permute-start | bytes 1572872 | tf_op jit(solution)/shard_map/ppermute | solution.py:315
  60.6 27.1 %collective-permute-start.8 = (bf16[2,256,1024]{2,1,0:T(8,128)(2,1)}, bf16[2,256,1024]{2,1,0:T(8,128)(2,1)}, u32[]{:S(2)}, u32[]{:S(2)}) collective-permute-start(bf16[2,256,1024]{2,1,0:T(8,128)(2,1)} %pad_maximum_fusion.7), channel_id=1, source_target_pairs={{0,2},{1,3},{2,0},{3,1},{4,6},{5,7},{6,4},{7,5},{8,10},{9,11},{10,... | collective-permute-start | bytes 3145736 | tf_op jit(solution)/shard_map/ppermute | solution.py:315
  93.3 184.4 %all-gather.7.cloned.1.call-start = ((), (), s32[]{:S(2)}) async-start(), calls=%async_computation.5 | async-start | bytes 4718592 | tf_op jit(solution)/shard_map/all_gather | solution.py:528
  95.1 91.4 %collective-permute-start.16 = (bf16[4,256,1024]{2,1,0:T(8,128)(2,1)}, bf16[4,256,1024]{2,1,0:T(8,128)(2,1)}, u32[]{:S(2)}, u32[]{:S(2)}) collective-permute-start(bf16[4,256,1024]{2,1,0:T(8,128)(2,1)} %pad_maximum_fusion.2), channel_id=1, source_target_pairs={{0,1},{1,0},{2,3},{3,2},{4,5},{5,4},{6,7},{7,6},{8,9},{9,8},{10,11... | collective-permute-start | bytes 6291464 | tf_op jit(solution)/shard_map/ppermute | solution.py:315
  103.1 30.1 %collective-permute-start.12 = (bf16[256,1024]{1,0:T(8,128)(2,1)S(1)}, bf16[256,1024]{1,0:T(8,128)(2,1)S(1)}, u32[]{:S(2)}, u32[]{:S(2)}) collective-permute-start(bf16[256,1024]{1,0:T(8,128)(2,1)S(1)} %pad_maximum_fusion.22), channel_id=1, source_target_pairs={{0,2},{1,3},{2,0},{3,1},{4,6},{5,7},{6,4},{7,5},{8,10},{9,11},{10,... | collective-permute-start | bytes 1572872 | tf_op jit(solution)/shard_map/ppermute | solution.py:315
  107.6 83.8 %collective-permute-start.14 = (bf16[1024,1024]{1,0:T(8,128)(2,1)}, bf16[1024,1024]{1,0:T(8,128)(2,1)}, u32[]{:S(2)}, u32[]{:S(2)}) collective-permute-start(bf16[1024,1024]{1,0:T(8,128)(2,1)} %pad_maximum_fusion.1.refs_2_.refs_9_), channel_id=1, source_target_pairs={{0,16},{8,24},{16,0},{24,8},{1,17},{9,25},{17,1},{25,9},{2,18},{10... | collective-permute-start | bytes 6291464 | tf_op jit(solution)/shard_map/ppermute | solution.py:315
  110.3 56.9 %collective-permute-start.15 = (bf16[512,1024]{1,0:T(8,128)(2,1)S(1)}, bf16[512,1024]{1,0:T(8,128)(2,1)S(1)}, u32[]{:S(2)}, u32[]{:S(2)}) collective-permute-start(bf16[512,1024]{1,0:T(8,128)(2,1)S(1)} %pad_maximum_fusion.9), channel_id=1, source_target_pairs={{0,2},{1,3},{2,0},{3,1},{4,6},{5,7},{6,4},{7,5},{8,10},{9,11},{10,... | collective-permute-start | bytes 3145736 | tf_op jit(solution)/shard_map/ppermute | solution.py:315
  133.3 51.7 %collective-permute-start.13 = (bf16[512,1024]{1,0:T(8,128)(2,1)S(1)}, bf16[512,1024]{1,0:T(8,128)(2,1)S(1)}, u32[]{:S(2)}, u32[]{:S(2)}) collective-permute-start(bf16[512,1024]{1,0:T(8,128)(2,1)S(1)} %pad_maximum_fusion.8), channel_id=1, source_target_pairs={{0,1},{1,0},{2,3},{3,2},{4,5},{5,4},{6,7},{7,6},{8,9},{9,8},{10,11... | collective-permute-start | bytes 3145736 | tf_op jit(solution)/shard_map/ppermute | solution.py:315
  191.5 531.2 %reduce-scatter.5.cloned.1.call-start = ((), (), s32[]{:S(2)}) async-start(), calls=%async_computation.3 | async-start | bytes 4718592 | tf_op jit(solution)/shard_map/reduce_scatter | solution.py:606
  193.0 27.3 %collective-permute-start.17 = (bf16[1024,1024]{1,0:T(8,128)(2,1)}, bf16[1024,1024]{1,0:T(8,128)(2,1)}, u32[]{:S(2)}, u32[]{:S(2)}) collective-permute-start(bf16[1024,1024]{1,0:T(8,128)(2,1)} %pad_maximum_fusion.3.refs_6_.refs_5_), channel_id=1, source_target_pairs={{0,16},{8,24},{16,0},{24,8},{1,17},{9,25},{17,1},{25,9},{2,18},{10... | collective-permute-start | bytes 6291464 | tf_op jit(solution)/shard_map/ppermute | solution.py:315
  227.8 48.5 %collective-permute-start.10 = (bf16[1024,1024]{1,0:T(8,128)(2,1)S(1)}, bf16[1024,1024]{1,0:T(8,128)(2,1)S(1)}, u32[]{:S(2)}, u32[]{:S(2)}) collective-permute-start(bf16[1024,1024]{1,0:T(8,128)(2,1)S(1)} %bitcast.268), channel_id=1, source_target_pairs={{0,16},{8,24},{16,0},{24,8},{1,17},{9,25},{17,1},{25,9},{2,18},{10... | collective-permute-start | bytes 6291464 | tf_op jit(solution)/shard_map/ppermute | solution.py:315
  244.5 76.0 %collective-permute-start.9 = (bf16[1024,1024]{1,0:T(8,128)(2,1)}, bf16[1024,1024]{1,0:T(8,128)(2,1)}, u32[]{:S(2)}, u32[]{:S(2)}) collective-permute-start(bf16[1024,1024]{1,0:T(8,128)(2,1)} %bitcast.43.refs_6_.refs_5_), channel_id=1, source_target_pairs={{0,16},{8,24},{16,0},{24,8},{1,17},{9,25},{17,1},{25,9},{2,18},{10... | collective-permute-start | bytes 6291464 | tf_op jit(solution)/shard_map/ppermute | solution.py:315
  291.4 29.0 %collective-permute-start.26 = (bf16[1024,1024]{1,0:T(8,128)(2,1)S(1)}, bf16[1024,1024]{1,0:T(8,128)(2,1)S(1)}, u32[]{:S(2)}, u32[]{:S(2)}) collective-permute-start(bf16[1024,1024]{1,0:T(8,128)(2,1)S(1)} %bitcast.270), channel_id=1, source_target_pairs={{0,8},{8,0},{16,24},{24,16},{1,9},{9,1},{17,25},{25,17},{2,10},{10... | collective-permute-start | bytes 6291464 | tf_op jit(solution)/shard_map/ppermute | solution.py:315
  345.3 103.8 %collective-permute-start.45 = (bf16[256,1024]{1,0:T(8,128)(2,1)}, bf16[256,1024]{1,0:T(8,128)(2,1)}, u32[]{:S(2)}, u32[]{:S(2)}) collective-permute-start(bf16[256,1024]{1,0:T(8,128)(2,1)} %get-tuple-element.281), channel_id=1, source_target_pairs={{0,8},{8,0},{16,24},{24,16},{1,9},{9,1},{17,25},{25,17},{2,10},{10... | collective-permute-start | bytes 1572872 | tf_op jit(solution)/shard_map/ppermute | solution.py:315
  345.7 33.3 %collective-permute-start.40 = (bf16[256,1024]{1,0:T(8,128)(2,1)}, bf16[256,1024]{1,0:T(8,128)(2,1)}, u32[]{:S(2)}, u32[]{:S(2)}) collective-permute-start(bf16[256,1024]{1,0:T(8,128)(2,1)} %get-tuple-element.235.refs_0_.refs_1_), channel_id=1, source_target_pairs={{0,8},{8,0},{16,24},{24,16},{1,9},{9,1},{17,25},{25,17},{2,10},{10... | collective-permute-start | bytes 1572872 | tf_op jit(solution)/shard_map/ppermute | solution.py:315
  376.4 366.6 %reduce-scatter.3.cloned.1.call-start = ((), (), s32[]{:S(2)}) async-start(), calls=%async_computation.2 | async-start | bytes 7077888 | tf_op jit(solution)/shard_map/reduce_scatter | solution.py:606
  397.7 66.7 %collective-permute-start.48 = (bf16[1024,1024]{1,0:T(8,128)(2,1)}, bf16[1024,1024]{1,0:T(8,128)(2,1)}, u32[]{:S(2)}, u32[]{:S(2)}) collective-permute-start(bf16[1024,1024]{1,0:T(8,128)(2,1)} %weight_grad.27), channel_id=1, source_target_pairs={{0,16},{8,24},{16,0},{24,8},{1,17},{9,25},{17,1},{25,9},{2,18},{10... | collective-permute-start | bytes 6291464 | tf_op jit(solution)/shard_map/ppermute | solution.py:315
  446.4 24.8 %collective-permute-start.50 = (bf16[512,1024]{1,0:T(8,128)(2,1)}, bf16[512,1024]{1,0:T(8,128)(2,1)}, u32[]{:S(2)}, u32[]{:S(2)}) collective-permute-start(bf16[512,1024]{1,0:T(8,128)(2,1)} %weight_grad.34), channel_id=1, source_target_pairs={{0,8},{8,0},{16,24},{24,16},{1,9},{9,1},{17,25},{25,17},{2,10},{10... | collective-permute-start | bytes 3145736 | tf_op jit(solution)/shard_map/ppermute | solution.py:315
  449.1 25.2 %collective-permute-start.51 = (bf16[512,1024]{1,0:T(8,128)(2,1)}, bf16[512,1024]{1,0:T(8,128)(2,1)}, u32[]{:S(2)}, u32[]{:S(2)}) collective-permute-start(bf16[512,1024]{1,0:T(8,128)(2,1)} %copy-done.71), channel_id=1, source_target_pairs={{0,8},{8,0},{16,24},{24,16},{1,9},{9,1},{17,25},{25,17},{2,10},{10... | collective-permute-start | bytes 3145736 | tf_op jit(solution)/shard_map/ppermute | solution.py:315
  459.0 39.7 %collective-permute-start.53 = (bf16[256,1024]{1,0:T(8,128)(2,1)}, bf16[256,1024]{1,0:T(8,128)(2,1)}, u32[]{:S(2)}, u32[]{:S(2)}) collective-permute-start(bf16[256,1024]{1,0:T(8,128)(2,1)} %get-tuple-element.219.refs_0_.refs_1_), channel_id=1, source_target_pairs={{0,8},{8,0},{16,24},{24,16},{1,9},{9,1},{17,25},{25,17},{2,10},{10... | collective-permute-start | bytes 1572872 | tf_op jit(solution)/shard_map/ppermute | solution.py:315
  490.3 48.8 %collective-permute-start.55 = (bf16[1024,1024]{1,0:T(8,128)(2,1)}, bf16[1024,1024]{1,0:T(8,128)(2,1)}, u32[]{:S(2)}, u32[]{:S(2)}) collective-permute-start(bf16[1024,1024]{1,0:T(8,128)(2,1)} %weight_grad.31), channel_id=1, source_target_pairs={{0,16},{8,24},{16,0},{24,8},{1,17},{9,25},{17,1},{25,9},{2,18},{10... | collective-permute-start | bytes 6291464 | tf_op jit(solution)/shard_map/ppermute | solution.py:315
  509.3 73.9 %collective-permute-start.65 = (bf16[1024,1024]{1,0:T(8,128)(2,1)}, bf16[1024,1024]{1,0:T(8,128)(2,1)}, u32[]{:S(2)}, u32[]{:S(2)}) collective-permute-start(bf16[1024,1024]{1,0:T(8,128)(2,1)} %weight_grad.39), channel_id=1, source_target_pairs={{0,16},{8,24},{16,0},{24,8},{1,17},{9,25},{17,1},{25,9},{2,18},{10... | collective-permute-start | bytes 6291464 | tf_op jit(solution)/shard_map/ppermute | solution.py:315
  541.9 57.1 %collective-permute-start.57 = (bf16[4,128,1024]{2,1,0:T(8,128)(2,1)S(1)}, bf16[4,128,1024]{2,1,0:T(8,128)(2,1)S(1)}, u32[]{:S(2)}, u32[]{:S(2)}) collective-permute-start(bf16[4,128,1024]{2,1,0:T(8,128)(2,1)S(1)} %split.126), channel_id=1, source_target_pairs={{0,1},{1,0},{2,3},{3,2},{4,5},{5,4},{6,7},{7,6},{8,9},{9,8},{10,11... | collective-permute-start | bytes 3145736 | tf_op jit(solution)/shard_map/ppermute | solution.py:315
  555.2 42.7 %collective-permute-start.58 = (bf16[4,64,1024]{2,1,0:T(8,128)(2,1)S(1)}, bf16[4,64,1024]{2,1,0:T(8,128)(2,1)S(1)}, u32[]{:S(2)}, u32[]{:S(2)}) collective-permute-start(bf16[4,64,1024]{2,1,0:T(8,128)(2,1)S(1)} %split.128), channel_id=1, source_target_pairs={{0,1},{1,0},{2,3},{3,2},{4,5},{5,4},{6,7},{7,6},{8,9},{9,8},{10,11... | collective-permute-start | bytes 1572872 | tf_op jit(solution)/shard_map/ppermute | solution.py:315
  587.3 66.7 %collective-permute-start.66 = (bf16[4,128,1024]{2,1,0:T(8,128)(2,1)}, bf16[4,128,1024]{2,1,0:T(8,128)(2,1)}, u32[]{:S(2)}, u32[]{:S(2)}) collective-permute-start(bf16[4,128,1024]{2,1,0:T(8,128)(2,1)} %bitcast.95), channel_id=1, source_target_pairs={{0,1},{1,0},{2,3},{3,2},{4,5},{5,4},{6,7},{7,6},{8,9},{9,8},{10,11... | collective-permute-start | bytes 3145736 | tf_op jit(solution)/shard_map/ppermute | solution.py:315
  600.9 54.8 %collective-permute-start.59 = (bf16[512,1024]{1,0:T(8,128)(2,1)}, bf16[512,1024]{1,0:T(8,128)(2,1)}, u32[]{:S(2)}, u32[]{:S(2)}) collective-permute-start(bf16[512,1024]{1,0:T(8,128)(2,1)} %weight_grad.42), channel_id=1, source_target_pairs={{0,8},{8,0},{16,24},{24,16},{1,9},{9,1},{17,25},{25,17},{2,10},{10... | collective-permute-start | bytes 3145736 | tf_op jit(solution)/shard_map/ppermute | solution.py:315
  605.1 43.8 %collective-permute-start.61 = (bf16[512,1024]{1,0:T(8,128)(2,1)}, bf16[512,1024]{1,0:T(8,128)(2,1)}, u32[]{:S(2)}, u32[]{:S(2)}) collective-permute-start(bf16[512,1024]{1,0:T(8,128)(2,1)} %weight_grad.46), channel_id=1, source_target_pairs={{0,8},{8,0},{16,24},{24,16},{1,9},{9,1},{17,25},{25,17},{2,10},{10... | collective-permute-start | bytes 3145736 | tf_op jit(solution)/shard_map/ppermute | solution.py:315
  606.5 45.2 %collective-permute-start.63 = (bf16[2,128,1024]{2,1,0:T(8,128)(2,1)}, bf16[2,128,1024]{2,1,0:T(8,128)(2,1)}, u32[]{:S(2)}, u32[]{:S(2)}) collective-permute-start(bf16[2,128,1024]{2,1,0:T(8,128)(2,1)} %split.133), channel_id=1, source_target_pairs={{0,2},{1,3},{2,0},{3,1},{4,6},{5,7},{6,4},{7,5},{8,10},{9,11},{10,... | collective-permute-start | bytes 1572872 | tf_op jit(solution)/shard_map/ppermute | solution.py:315
  684.2 33.2 %collective-permute-start.75 = (bf16[512,1024]{1,0:T(8,128)(2,1)S(1)}, bf16[512,1024]{1,0:T(8,128)(2,1)S(1)}, u32[]{:S(2)}, u32[]{:S(2)}) collective-permute-start(bf16[512,1024]{1,0:T(8,128)(2,1)S(1)} %split.152), channel_id=1, source_target_pairs={{0,2},{1,3},{2,0},{3,1},{4,6},{5,7},{6,4},{7,5},{8,10},{9,11},{10,... | collective-permute-start | bytes 3145736 | tf_op jit(solution)/shard_map/ppermute | solution.py:315
  (282 other events, 2530.8 us)
Sparse Core Ops, SparseCore 0:
  93.5 105.0 all-gather.4
  201.4 72.6 all-gather.6
  376.5 93.3 reduce-scatter.4
  512.8 144.2 reduce-scatter.2
